TPU v7x, 256 devices: a whole 4x4x8 slice. The times are simulated.
256 devices in a mesh: expert: 16 (over x_lo, y, core), hidden: 16 (over z, x_hi).
Axes of the slice: x: 4 (x_hi: 2, x_lo: 2; x = x_hi * 2 + x_lo), y: 4, z: 8, core: 2. Of those that a mesh axis runs over, the one named last changes fastest.
Arguments:
- tokens: bfloat16 [4096, 7168], P('expert', 'hidden'), may hold values from -6 to 6
- route_ids: int32 [4096, 2], P('expert'), may hold values from 0 to 15, all different within a row; in each aligned block of 256 rows (0 to 255, 256 to 511, ...) at most 40 rows name the same one
- route_weight: float32 [4096, 2], P('expert'), may hold values from 0.2 to 2
- w_gate: bfloat16 [16, 7168, 2048], P('expert', None, 'hidden'), may hold values from -0.0625 to 0.0625
- w_up: bfloat16 [16, 7168, 2048], P('expert', None, 'hidden'), may hold values from -0.0625 to 0.0625
- w_down: bfloat16 [16, 2048, 7168], P('expert', 'hidden'), may hold values from -0.125 to 0.125
Outputs:
- mixed: bfloat16 [4096, 7168], P('expert', 'hidden')
Inputs may be any that keep to these rules, and one draw needn't show every extreme that they name: `route_ids`: each row names 2 different experts. In the aligned blocks of 256 rows, no expert is named by more than 40 rows of one block, a bound that some block reaches.
All inputs are finite; a program needn't handle non-finite values.
Results may differ from a plain program's by a relative error of at most 0.0057.
Values may be sent and summed in bfloat16 or wider, within the bound.
No kernel may reach another device: no remote copies, remote signals or barrier semaphores. Data moves between devices by JAX's collectives and lax.ppermute only.
A program may use at most 128 MiB of HBM per device.

v0:
```python
import jax
import jax.numpy as jnp
from jax import lax
from jax.sharding import PartitionSpec as P

TOP = 2


def on_device(tokens, route_ids, route_weight, w_gate, w_up, w_down):
    experts = lax.axis_size("expert")
    rows_dev = tokens.shape[0]
    capacity = (rows_dev * TOP * 5 + 4 * experts - 1) // (4 * experts)
    slot_count = experts * capacity
    matches = route_ids[:, :, None] == jnp.arange(experts, dtype=jnp.int32)[None, None, :]
    chosen = jnp.sum(matches.astype(jnp.int32), axis=1)
    ranking = jnp.cumsum(chosen, axis=0) - chosen
    slot_ids = jnp.arange(capacity, dtype=jnp.int32)
    placed = (chosen.T[:, None, :] == 1) & (ranking.T[:, None, :] == slot_ids[None, :, None])
    every_row = lax.all_gather(tokens, "expert", axis=0, tiled=True)
    every_route = lax.all_gather(route_ids, "expert", axis=0, tiled=True)
    own_expert = lax.axis_index("expert")
    flagged = jnp.sum((every_route == own_expert).astype(jnp.int32), axis=1).reshape(
        experts, rows_dev
    )
    ordering = jnp.cumsum(flagged, axis=1) - flagged
    picks = (flagged[:, None, :] == 1) & (ordering[:, None, :] == slot_ids[None, :, None])
    arrived = jnp.einsum(
        "sct,std->scd",
        picks.astype(jnp.bfloat16),
        every_row.reshape(experts, rows_dev, -1),
        preferred_element_type=jnp.float32,
    ).astype(jnp.bfloat16)
    flat_rows = arrived.reshape(slot_count, -1)
    gate_w = w_gate[0]
    up_w = w_up[0]
    down_w = w_down[0]
    fragment = lax.all_gather(flat_rows, "hidden", axis=1, tiled=True)
    gate_sum = jnp.dot(fragment, gate_w, preferred_element_type=jnp.float32)
    up_sum = jnp.dot(fragment, up_w, preferred_element_type=jnp.float32)
    hidden = (jax.nn.silu(gate_sum) * up_sum).astype(jnp.bfloat16)
    partials = jnp.dot(hidden, down_w, preferred_element_type=jnp.float32)
    produced = lax.psum_scatter(partials, "hidden", scatter_dimension=1, tiled=True)
    produced = produced.astype(jnp.bfloat16).reshape(experts, capacity, -1)
    returned = lax.all_to_all(produced, "expert", split_axis=0, concat_axis=0, tiled=True)
    per_expert = jnp.sum(jnp.where(matches, route_weight[:, :, None], jnp.float32(0.0)), axis=1)
    combine_table = placed.astype(jnp.float32) * per_expert.T[:, None, :]
    mixed = jnp.einsum(
        "ect,ecd->td", combine_table, returned.astype(jnp.float32), precision=lax.Precision.HIGHEST
    )
    return mixed.astype(jnp.bfloat16)


def solution(mesh):
    in_specs = (
        P("expert", "hidden"),
        P("expert", None),
        P("expert", None),
        P("expert", None, "hidden"),
        P("expert", None, "hidden"),
        P("expert", "hidden", None),
    )
    out_specs = P("expert", "hidden")
    return jax.shard_map(
        on_device, mesh=mesh, in_specs=in_specs, out_specs=out_specs, check_vma=False
    )
```

profile of v0, /device:TPU:96, one launch (start us, length us, event | category | flops | bytes accessed | tf_op | source)
XLA Modules:
  0.0 562.6 jit_solution(8759587761792712818)
XLA Ops:
  6.5 0.0 copy-start
  6.5 0.0 all-gather.3.cloned.1.call-start
  6.5 0.7 all-gather.3.cloned.1.call-update
  7.3 0.0 all-gather.5.cloned.1.call-start
  7.3 20.2 %all_gather.9 = s32[4096,2]{0,1:T(2,128)S(1)} all-gather(s32[256,2]{0,1:T(2,128)} %param.7), channel_id=1, replica_groups=mesh['expert'=16,'hidden'=16] {'expert'}, dimensions={0}, use_global_device_ids=true | all-gather | bytes 34816 | tf_op jit(solution)/shard_map/all_gather | solution.py:20
  27.6 0.6 reduce-window.16
  28.2 0.2 slice_reduce_fusion
  28.4 0.1 bitcast_subtract_fusion
  28.5 28.4 %all-gather.3.cloned.1.call-done = bf16[4096,448]{0,1:T(8,128)(2,1)} async-done(((bf16[256,448]{0,1:T(8,128)(2,1)}), bf16[4096,448]{0,1:T(8,128)(2,1)}) %all-gather.3.cloned.1.call-update) | async-done | bytes 3670032 | tf_op jit(solution)/shard_map/all_gather | solution.py:19
  56.9 3.2 fusion.9
  60.1 1.1 copy.32
  61.1 0.0 all-gather.5.cloned.1.call-update
  61.2 0.0 reduce-scatter.2.cloned.1.call-start
  61.2 143.3 %all-gather.5.cloned.1.call-done = bf16[640,7168]{0,1:T(8,128)(2,1)} async-done(((bf16[640,448]{0,1:T(8,128)(2,1)}), bf16[640,7168]{0,1:T(8,128)(2,1)}) %all-gather.5.cloned.1.call-update) | async-done | bytes 9175056 | tf_op jit(solution)/shard_map/all_gather | solution.py:37
  204.6 6.7 %fusion.7 = f32[640,128]{1,0:T(8,128)S(1)} fusion(bf16[640,7168]{0,1:T(8,128)(2,1)} %all-gather.5.cloned.1.call-done, bf16[1,7168,128]{2,1,0:T(8,128)(2,1)} %param.9), kind=kOutput, calls=%fused_computation.7 | convolution fusion | flops 1174405120 | bytes 11337728 | tf_op jit(solution)/shard_map/dot_general | solution.py:38
  211.2 0.0 copy-done
  211.2 20.0 %fusion.3 = f32[640,7168]{0,1:T(8,128)} fusion(bf16[1,128,7168]{2,1,0:T(8,128)(2,1)S(1)} %copy-done, bf16[640,7168]{0,1:T(8,128)(2,1)} %all-gather.5.cloned.1.call-done, bf16[1,7168,128]{2,1,0:T(8,128)(2,1)} %param.10, f32[640,128]{1,0:T(8,128)S(1)} %fusion.7), kind=kOutput, calls=%fused_computation.3 | convolution fusion | flops 2349301760 | bytes 31522816 | tf_op jit(solution)/shard_map/dot_general | solution.py:41
  231.3 0.0 copy-start.1
  231.3 0.0 reduce-scatter.2.cloned.1.call-update
  231.3 0.7 copy-done.1
  232.0 0.0 copy-start.2
  232.0 0.6 reduce-window.14
  232.6 0.2 slice_reduce_fusion.1
  232.8 302.4 %reduce-scatter.2.cloned.1.call-done = f32[640,448]{0,1:T(8,128)} async-done(((f32[640,7168]{0,1:T(8,128)}), f32[640,448]{0,1:T(8,128)}) %reduce-scatter.2.cloned.1.call-update) | async-done | bytes 1146896 | tf_op jit(solution)/shard_map/reduce_scatter | solution.py:42
  535.2 1.3 convert_element_type.25
  536.6 1.1 copy.33
  537.7 4.4 all-to-all-start
  542.1 0.0 copy-done.2
  542.1 0.1 bitcast_subtract_fusion.1
  542.2 12.2 %all-to-all-done = bf16[16,40,448]{2,1,0:T(8,128)(2,1)S(1)} async-done(((bf16[16,40,448]{2,1,0:T(8,128)(2,1)}), bf16[16,40,448]{2,1,0:T(8,128)(2,1)S(1)}, u32[]{:S(2)}, u32[]{:S(2)}) %all-to-all-start) | async-done | bytes 573472 | tf_op jit(solution)/shard_map/all_to_all | solution.py:44
  554.4 1.7 fusion.12
  (12 shorter events, 0.2 us)
Async XLA Ops:
  6.5 204.7 %copy-start = (bf16[1,128,7168]{2,1,0:T(8,128)(2,1)S(1)}, bf16[1,128,7168]{2,1,0:T(8,128)(2,1)}, u32[]{:S(2)}) copy-start(bf16[1,128,7168]{2,1,0:T(8,128)(2,1)} %param.11) | copy-start | bytes 5505028
  6.5 50.4 %all-gather.3.cloned.1.call-start = ((), (), s32[]{:S(2)}) async-start(), calls=%async_computation.2 | async-start | bytes 3899392 | tf_op jit(solution)/shard_map/all_gather | solution.py:19
  7.3 197.3 %all-gather.5.cloned.1.call-start = ((), (), s32[]{:S(2)}) async-start(), calls=%async_computation.3 | async-start | bytes 9748480 | tf_op jit(solution)/shard_map/all_gather | solution.py:37
  61.2 474.1 %reduce-scatter.2.cloned.1.call-start = ((), (), s32[]{:S(2)}) async-start(), calls=%async_computation.4 | async-start | bytes 19496960 | tf_op jit(solution)/shard_map/reduce_scatter | solution.py:42
  231.3 0.7 copy-start.1
  232.0 310.1 %copy-start.2 = (f32[256,2]{0,1:T(2,128)S(1)}, f32[256,2]{0,1:T(2,128)}, u32[]{:S(2)}) copy-start(f32[256,2]{0,1:T(2,128)} %param.8) | copy-start | bytes 6148
  537.7 16.7 %all-to-all-start = ((bf16[16,40,448]{2,1,0:T(8,128)(2,1)}), bf16[16,40,448]{2,1,0:T(8,128)(2,1)S(1)}, u32[]{:S(2)}, u32[]{:S(2)}) async-start(bf16[16,40,448]{2,1,0:T(8,128)(2,1)} %bitcast.7), calls=%async_computation.1 | async-start | bytes 1310720 | tf_op jit(solution)/shard_map/all_to_all | solution.py:44
Sparse Core Ops, SparseCore 0:
  9.1 47.7 all-gather.2
  61.3 143.2 all-gather.4
  231.4 303.7 reduce-scatter.1
where the time goes:
time: 565 us; the launch traced here: 563 us
  waiting for transfers between devices  487 us (86%)
  matrix products  31.6 us (6%)
  blocking collectives  20.2 us (4%)
  between operations  13.2 us (2%)
    reduce_scatter x1, waiting for transfers between devices, on_device(): lax.psum_scatter(partials, 'hidden', scatter_dimension=1, tiled=True)  302 us
    all_gather x1, waiting for transfers between devices, on_device(): fragment = lax.all_gather(flat_rows, 'hidden', axis=1, tiled=True)  143 us
    all_gather x1, waiting for transfers between devices, on_device(): every_row = lax.all_gather(tokens, 'expert', axis=0, tiled=True)  28.4 us
    all_gather x1, blocking collectives, on_device(): every_route = lax.all_gather(route_ids, 'expert', axis=0, tiled=True)  20.2 us
    dot_general x1, matrix products, on_device(): partials = jnp.dot(hidden, down_w, preferred_element_type=jnp.float32)  20 us
    all_to_all x1, waiting for transfers between devices, on_device(): lax.all_to_all(produced, 'expert', split_axis=0, concat_axis=0, tiled=True)  12.2 us
  transfers between devices with their start and end apart: 4, of which 4 were waited for; matrix products, arithmetic and copies ran while one was open for 0% of the time, Pallas kernels for 0%

commit v1 on v0

v1 whole, which is shorter than its diff:
```python
import jax
import jax.numpy as jnp
from jax import lax
from jax.sharding import PartitionSpec as P

TOP = 2


def on_device(tokens, route_ids, route_weight, w_gate, w_up, w_down):
    experts = lax.axis_size("expert")
    parts = lax.axis_size("hidden")
    rows_dev, width = tokens.shape
    capacity = (rows_dev * TOP * 5 + 4 * experts - 1) // (4 * experts)
    slot_count = experts * capacity

    matches = route_ids[:, :, None] == jnp.arange(experts, dtype=jnp.int32)[None, None, :]
    chosen = jnp.any(matches, axis=1)
    before = jnp.arange(rows_dev)[:, None] > jnp.arange(rows_dev)[None, :]
    ranking = jnp.dot(
        before.astype(jnp.bfloat16), chosen.astype(jnp.bfloat16), preferred_element_type=jnp.float32
    )
    slot_of = jnp.arange(experts, dtype=jnp.float32)[None, :] * capacity + ranking
    slot_k = jnp.sum(jnp.where(matches, slot_of[:, None, :], 0.0), axis=2).astype(jnp.int32)
    slots = jnp.arange(slot_count, dtype=jnp.int32)
    picks_k = [slot_k[:, k][:, None] == slots[None, :] for k in range(TOP)]
    picks = (picks_k[0] | picks_k[1]).astype(jnp.bfloat16)

    down_w = lax.all_to_all(w_down[0], "hidden", split_axis=1, concat_axis=0, tiled=True)

    leaving = lax.dot_general(
        picks, tokens, (((0,), (0,)), ((), ())), preferred_element_type=jnp.float32
    ).astype(jnp.bfloat16)
    arrived = lax.all_to_all(
        leaving.reshape(experts, capacity, width), "expert", split_axis=0, concat_axis=0, tiled=True
    ).reshape(slot_count, width)
    rows = lax.all_gather(arrived, "hidden", axis=1, tiled=True)
    gate_sum = jnp.dot(rows, w_gate[0], preferred_element_type=jnp.float32)
    up_sum = jnp.dot(rows, w_up[0], preferred_element_type=jnp.float32)
    hidden = (jax.nn.silu(gate_sum) * up_sum).astype(jnp.bfloat16)
    every_hidden = lax.all_gather(hidden, "hidden", axis=1, tiled=True)
    produced = jnp.dot(every_hidden, down_w, preferred_element_type=jnp.float32).astype(jnp.bfloat16)
    returned = lax.all_to_all(
        produced.reshape(experts, capacity, width), "expert", split_axis=0, concat_axis=0, tiled=True
    ).reshape(slot_count, width)
    mixed = jnp.zeros((rows_dev, width), jnp.float32)
    for k in range(TOP):
        result = jnp.dot(
            picks_k[k].astype(jnp.bfloat16), returned, preferred_element_type=jnp.float32
        )
        mixed = mixed + route_weight[:, k][:, None] * result
    return mixed.astype(jnp.bfloat16)


def solution(mesh):
    in_specs = (
        P("expert", "hidden"),
        P("expert", None),
        P("expert", None),
        P("expert", None, "hidden"),
        P("expert", None, "hidden"),
        P("expert", "hidden", None),
    )
    out_specs = P("expert", "hidden")
    return jax.shard_map(
        on_device, mesh=mesh, in_specs=in_specs, out_specs=out_specs, check_vma=False
    )
```

time: 565 us -> 320 us (0.57)
  waiting for transfers between devices: 487 us -> 200 us
  blocking collectives: 20.2 us -> 73.5 us
  matrix products: 31.6 us -> 16.8 us
    reduce_scatter x1 -> x0, waiting for transfers between devices: 302 us -> none  [on_device(): lax.psum_scatter(partials, 'hidden', scatter_dimension=1, tiled=True)]
    all_to_all x0 -> x2, blocking collectives: none -> 73.5 us  [the longest x1 55.9 us: on_device(): lax.all_to_all(w_down[0], 'hidden', split_axis=1, concat_axis=0, tiled=True)]
    all_gather x1 -> x0, blocking collectives: 20.2 us -> none  [on_device(): every_route = lax.all_gather(route_ids, 'expert', axis=0, tiled=True)]
    all_gather x2, waiting for transfers between devices: 172 us -> 188 us  [the longest x1 143 us: on_device(): rows = lax.all_gather(arrived, 'hidden', axis=1, tiled=True)]
    dot_general x4 -> x7, matrix products: 31.6 us -> 16.8 us  [the longest x1 6.31 us: on_device(): gate_sum = jnp.dot(rows, w_gate[0], preferred_element_type=jnp.float32)]
  transfers between devices with their start and end apart: 4 -> 3, of which waited for: 4 -> 3; matrix products, arithmetic and copies ran while one was open for 0% -> 1% of each run, Pallas kernels for 0% -> 0%
where the time goes in v1:
time: 320 us; the launch traced here: 317 us
  waiting for transfers between devices  200 us (62%)
  blocking collectives  73.5 us (23%)
  matrix products  16.8 us (5%)
  between operations  13.5 us (4%)
  local copies, waits for them, and re-layouts  6.73 us (2%)
  starting transfers between devices  4.44 us (1%)
    all_gather x1, waiting for transfers between devices, on_device(): rows = lax.all_gather(arrived, 'hidden', axis=1, tiled=True)  143 us
    all_to_all x1, blocking collectives, on_device(): lax.all_to_all(w_down[0], 'hidden', split_axis=1, concat_axis=0, tiled=True)  55.9 us
    all_gather x1, waiting for transfers between devices, on_device(): every_hidden = lax.all_gather(hidden, 'hidden', axis=1, tiled=True)  45.2 us
    all_to_all x1, blocking collectives, on_device(): lax.all_to_all(leaving.reshape(experts, capacity, width), 'expert', split...  17.6 us
    all_to_all x1, waiting for transfers between devices, on_device(): lax.all_to_all(produced.reshape(experts, capacity, width), 'expert', spli...  12.3 us
  transfers between devices with their start and end apart: 3, of which 3 were waited for; matrix products, arithmetic and copies ran while one was open for 1% of the time, Pallas kernels for 0%

profile of v1, /device:TPU:96, one launch (start us, length us, event | category | flops | bytes accessed | tf_op | source)
XLA Modules:
  0.0 316.8 jit_solution(8556425088492365411)
XLA Ops:
  6.5 0.0 copy-start
  6.5 0.0 all-gather.3.cloned.1.call-start
  6.5 0.8 fusion.24
  7.4 0.2 convolution_add_fusion
  7.5 0.7 select_reduce_fusion
  8.3 1.5 convolution_convert_fusion
  9.8 0.3 copy.22
  10.1 17.6 %all_to_all.29 = bf16[16,40,448]{2,1,0:T(8,128)(2,1)S(1)} all-to-all(bf16[16,40,448]{2,1,0:T(8,128)(2,1)S(1)} %bitcast.39), channel_id=1, replica_groups=mesh['expert'=16,'hidden'=16] {'expert'}, dimensions={0} | all-to-all | bytes 1146880 | tf_op jit(solution)/shard_map/all_to_all | solution.py:33
  27.7 1.1 copy.23
  28.8 0.0 all-gather.3.cloned.1.call-update
  28.8 0.0 all-gather.5.cloned.1.call-start
  28.8 142.7 %all-gather.3.cloned.1.call-done = bf16[640,7168]{0,1:T(8,128)(2,1)} async-done(((bf16[640,448]{0,1:T(8,128)(2,1)}), bf16[640,7168]{0,1:T(8,128)(2,1)}) %all-gather.3.cloned.1.call-update) | async-done | bytes 9175056 | tf_op jit(solution)/shard_map/all_gather | solution.py:36
  171.5 0.0 copy-done
  171.5 0.0 copy-start.2
  171.5 0.0 copy-start.3
  171.5 6.3 %fusion.5 = f32[640,128]{1,0:T(8,128)S(1)} fusion(bf16[640,7168]{0,1:T(8,128)(2,1)} %all-gather.3.cloned.1.call-done, bf16[1,7168,128]{2,1,0:T(8,128)(2,1)S(1)} %copy-done), kind=kOutput, calls=%fused_computation.5 | convolution fusion | flops 1174405120 | bytes 11337728 | tf_op jit(solution)/shard_map/dot_general | solution.py:37
  177.8 0.0 copy-done.2
  177.9 0.4 copy-done.3
  178.2 3.2 %fusion.15 = bf16[640,128]{1,0:T(8,128)(2,1)} fusion(bf16[640,7168]{0,1:T(8,128)(2,1)S(1)} %copy-done.2, bf16[1,7168,128]{2,1,0:T(8,128)(2,1)S(1)} %copy-done.3, f32[640,128]{1,0:T(8,128)S(1)} %fusion.5), kind=kOutput, calls=%fused_computation.14 | convolution fusion | flops 1174896640 | bytes 11501568 | tf_op jit(solution)/shard_map/dot_general | solution.py:38
  181.5 0.0 all-gather.5.cloned.1.call-update
  181.5 3.9 %copy.24 = bf16[1,128,7168]{1,2,0:T(8,128)(2,1)} copy(bf16[1,128,7168]{2,1,0:T(8,128)(2,1)} %param.11) | data formatting | bytes 3670016 | tf_op args[5]
  185.4 55.9 %all_to_all.30 = bf16[128,16,448]{0,2,1:T(8,128)(2,1)} all-to-all(bf16[128,16,448]{0,2,1:T(8,128)(2,1)} %bitcast.36), channel_id=1, replica_groups=mesh['expert'=16,'hidden'=16] {'hidden'}, dimensions={1} | all-to-all | bytes 3670016 | tf_op jit(solution)/shard_map/all_to_all | solution.py:28
  241.3 45.2 %all-gather.5.cloned.1.call-done = bf16[640,2048]{1,0:T(8,128)(2,1)} async-done(((bf16[640,128]{1,0:T(8,128)(2,1)}), bf16[640,2048]{1,0:T(8,128)(2,1)}) %all-gather.5.cloned.1.call-update) | async-done | bytes 2621456 | tf_op jit(solution)/shard_map/all_gather | solution.py:40
  286.5 3.9 %fusion.7 = bf16[640,448]{0,1:T(8,128)(2,1)S(1)} fusion(bf16[640,2048]{1,0:T(8,128)(2,1)} %all-gather.5.cloned.1.call-done, bf16[128,16,448]{0,2,1:T(8,128)(2,1)} %all_to_all.30), kind=kOutput, calls=%fused_computation.7 | convolution fusion | flops 1174691840 | bytes 5029888 | tf_op jit(solution)/shard_map/dot_general | solution.py:41
  290.4 0.0 copy-start.1
  290.4 1.1 copy.26
  291.5 4.4 %all-to-all-start.2 = ((bf16[16,40,448]{2,1,0:T(8,128)(2,1)}), bf16[16,40,448]{2,1,0:T(8,128)(2,1)S(1)}, u32[]{:S(2)}, u32[]{:S(2)}) async-start(bf16[16,40,448]{2,1,0:T(8,128)(2,1)} %bitcast.9), calls=%async_computation.2 | async-start | bytes 1310720 | tf_op jit(solution)/shard_map/all_to_all | solution.py:42
  295.9 0.0 copy-done.1
  296.0 12.3 %all-to-all-done.2 = bf16[16,40,448]{2,1,0:T(8,128)(2,1)S(1)} async-done(((bf16[16,40,448]{2,1,0:T(8,128)(2,1)}), bf16[16,40,448]{2,1,0:T(8,128)(2,1)S(1)}, u32[]{:S(2)}, u32[]{:S(2)}) %all-to-all-start.2) | async-done | bytes 573472 | tf_op jit(solution)/shard_map/all_to_all | solution.py:42
  308.2 0.5 convolution_multiply_fusion.1
  308.7 1.2 fusion.11
  (4 shorter events, 0.0 us)
Async XLA Ops:
  6.5 165.0 %copy-start = (bf16[1,7168,128]{2,1,0:T(8,128)(2,1)S(1)}, bf16[1,7168,128]{2,1,0:T(8,128)(2,1)}, u32[]{:S(2)}) copy-start(bf16[1,7168,128]{2,1,0:T(8,128)(2,1)} %param.9) | copy-start | bytes 5505028
  6.5 165.0 %all-gather.3.cloned.1.call-start = ((), (), s32[]{:S(2)}) async-start(), calls=%async_computation.3 | async-start | bytes 9748480 | tf_op jit(solution)/shard_map/all_gather | solution.py:36
  28.8 257.7 %all-gather.5.cloned.1.call-start = ((), (), s32[]{:S(2)}) async-start(), calls=%async_computation.4 | async-start | bytes 2785280 | tf_op jit(solution)/shard_map/all_gather | solution.py:40
  171.5 6.3 %copy-start.2 = (bf16[640,7168]{0,1:T(8,128)(2,1)S(1)}, bf16[640,7168]{0,1:T(8,128)(2,1)}, u32[]{:S(2)}) copy-start(bf16[640,7168]{0,1:T(8,128)(2,1)} %all-gather.3.cloned.1.call-done) | copy-start | bytes 27525124
  171.5 6.7 %copy-start.3 = (bf16[1,7168,128]{2,1,0:T(8,128)(2,1)S(1)}, bf16[1,7168,128]{2,1,0:T(8,128)(2,1)}, u32[]{:S(2)}) copy-start(bf16[1,7168,128]{2,1,0:T(8,128)(2,1)} %param.10) | copy-start | bytes 5505028
  290.4 5.5 %copy-start.1 = (f32[256,2]{0,1:T(2,128)S(1)}, f32[256,2]{0,1:T(2,128)}, u32[]{:S(2)}) copy-start(f32[256,2]{0,1:T(2,128)} %param.8) | copy-start | bytes 6148
  291.5 16.7 %all-to-all-start.2 = ((bf16[16,40,448]{2,1,0:T(8,128)(2,1)}), bf16[16,40,448]{2,1,0:T(8,128)(2,1)S(1)}, u32[]{:S(2)}, u32[]{:S(2)}) async-start(bf16[16,40,448]{2,1,0:T(8,128)(2,1)} %bitcast.9), calls=%async_computation.2 | async-start | bytes 1310720 | tf_op jit(solution)/shard_map/all_to_all | solution.py:42
Sparse Core Ops, SparseCore 0:
  28.9 142.5 all-gather.2
  181.6 104.8 all-gather.4

commit v2 on v1

v2 whole, which is shorter than its diff:
```python
import jax
import jax.numpy as jnp
from jax import lax
from jax.experimental import pallas as pl
from jax.experimental.pallas import tpu as pltpu
from jax.sharding import Mesh, PartitionSpec as P

TOP = 2
SHAPE = (2, 4, 2, 8, 2)
NAMES = ("xl", "y", "core", "z", "xh")
PLANE = ("xl", "y", "xh")


def along_z(x, step):
    n = lax.axis_size("z")
    return lax.ppermute(x, "z", [(s, (s + step) % n) for s in range(n)])


def from_swapped(x):
    return lax.ppermute(x, ("core", "xh"), [(1, 2), (2, 1)])


def after(x, *others):
    return lax.optimization_barrier((x, others))[0]


def other_core(x):
    return lax.ppermute(x, "core", [(0, 1), (1, 0)])


def gate_up_body(tops, counts, first, last, units, *refs):
    n = len(counts)
    held, refs = refs[: len(tops)], refs[len(tops) :]
    weights, refs = refs[:2], refs[2:]
    before_ref, (out_ref, total) = (None, refs) if first else (refs[0], refs[1:])
    step = pl.program_id(0)

    @pl.when(step == 0)
    def _():
        total[...] = jnp.zeros_like(total) if first else before_ref[...]

    taken = 0
    for k in range(n):
        parts = [(held[j], tops[j]) for j in range(taken, taken + counts[k])]
        taken += counts[k]

        @pl.when(step == k)
        def _():
            w = jnp.concatenate([w_ref[...] for w_ref in weights], axis=1)
            for x_ref, top in parts:
                at = pl.ds(top, x_ref.shape[0])
                total[at, :] += jnp.dot(x_ref[...], w, preferred_element_type=jnp.float32)

    @pl.when(step == n - 1)
    def _():
        if not last:
            out_ref[...] = total[...]
            return
        for j in range(2):
            gate = total[:, 2 * j * units : (2 * j + 1) * units]
            up = total[:, (2 * j + 1) * units : (2 * j + 2) * units]
            act = gate / (1.0 + jnp.exp(-gate)) * up
            out_ref[:, j * units : (j + 1) * units] = act.astype(jnp.bfloat16)


def gate_up(blocks, weights, before=None, last=False):
    held = [x for parts in blocks for x, _ in parts]
    tops = [top for parts in blocks for _, top in parts]
    counts = [len(parts) for parts in blocks]
    n = len(blocks)
    units = weights[0].shape[1] // 2
    depth = held[0].shape[1]
    rows = sum(x.shape[0] for x, _ in blocks[0])
    whole = pl.BlockSpec(memory_space=pltpu.VMEM)
    w_spec = pl.BlockSpec((depth, 2 * units), lambda k: (k, 0))
    out = (rows, 2 * units) if last else (rows, 4 * units)
    return pl.pallas_call(
        lambda *refs: gate_up_body(tops, counts, before is None, last, units, *refs),
        grid=(n,),
        in_specs=[whole] * len(held) + [w_spec] * 2 + ([] if before is None else [whole]),
        out_specs=pl.BlockSpec(out, lambda k: (0, 0)),
        scratch_shapes=[pltpu.VMEM((rows, 4 * units), jnp.float32)],
        out_shape=jax.ShapeDtypeStruct(out, jnp.bfloat16 if last else jnp.float32),
        compiler_params=pltpu.CompilerParams(vmem_limit_bytes=24 << 20),
        cost_estimate=pl.CostEstimate(
            flops=8 * n * rows * depth * units,
            bytes_accessed=2 * n * depth * (rows + 4 * units),
            transcendentals=2 * rows * units if last else 0,
        ),
    )(*held, *weights, *([] if before is None else [before]))


def pack_gate_up_body(units, at_ref, gate_ref, up_ref, out_ref):
    out_ref[:, :units] = gate_ref[...]
    out_ref[:, units:] = up_ref[...]


def pack_gate_up(at, gate, up, depth):
    n, units = at.shape[0], gate.shape[1]
    spec = pl.BlockSpec((depth, units), lambda k, at_ref: (at_ref[k], 0))
    return pl.pallas_call(
        lambda *refs: pack_gate_up_body(units, *refs),
        grid_spec=pltpu.PrefetchScalarGridSpec(
            num_scalar_prefetch=1,
            grid=(n,),
            in_specs=[spec, spec],
            out_specs=pl.BlockSpec((depth, 2 * units), lambda k, at_ref: (k, 0)),
        ),
        out_shape=jax.ShapeDtypeStruct((n * depth, 2 * units), jnp.bfloat16),
        cost_estimate=pl.CostEstimate(
            flops=0, bytes_accessed=8 * n * depth * units, transcendentals=0
        ),
    )(at, gate, up)


def pack_down_body(at_ref, down_ref, out_ref):
    out_ref[0] = down_ref[...]


def pack_down(at, down, width):
    n, units = at.shape[0], down.shape[0]
    return pl.pallas_call(
        pack_down_body,
        grid_spec=pltpu.PrefetchScalarGridSpec(
            num_scalar_prefetch=1,
            grid=(n,),
            in_specs=[pl.BlockSpec((units, width), lambda k, at_ref: (0, at_ref[k]))],
            out_specs=pl.BlockSpec((1, units, width), lambda k, at_ref: (k, 0, 0)),
        ),
        out_shape=jax.ShapeDtypeStruct((n, units, width), jnp.bfloat16),
        cost_estimate=pl.CostEstimate(
            flops=0, bytes_accessed=4 * n * width * units, transcendentals=0
        ),
    )(at, down)


def on_device(tokens, route_ids, route_weight, w_gate, w_up, w_down):
    rows_dev, width = tokens.shape
    experts = lax.axis_size(PLANE)
    nz = lax.axis_size("z")
    z = lax.axis_index("z")
    capacity = (rows_dev * TOP * 5 + 4 * experts - 1) // (4 * experts)
    slot_count = experts * capacity
    owners = experts // 2
    units = w_gate.shape[2]

    matches = route_ids[:, :, None] == jnp.arange(experts, dtype=jnp.int32)[None, None, :]
    chosen = jnp.any(matches, axis=1)
    before = jnp.arange(rows_dev)[:, None] > jnp.arange(rows_dev)[None, :]
    ranking = jnp.dot(
        before.astype(jnp.bfloat16), chosen.astype(jnp.bfloat16), preferred_element_type=jnp.float32
    )
    slot_of = jnp.arange(experts, dtype=jnp.float32)[None, :] * capacity + ranking
    slot_k = jnp.sum(jnp.where(matches, slot_of[:, None, :], 0.0), axis=2).astype(jnp.int32)
    slots = jnp.arange(slot_count, dtype=jnp.int32)
    picks_k = [slot_k[:, k][:, None] == slots[None, :] for k in range(TOP)]
    picks = (picks_k[0] | picks_k[1]).astype(jnp.bfloat16)

    leaving = lax.dot_general(
        picks, tokens, (((0,), (0,)), ((), ())), preferred_element_type=jnp.float32
    ).astype(jnp.bfloat16)
    arrived = lax.all_to_all(
        leaving.reshape(experts, capacity, width), PLANE, split_axis=0, concat_axis=0, tiled=True
    )
    def at(places):
        return jnp.stack([(z + k) % nz for k in places]).astype(jnp.int32)

    def pick(mine, came):
        return jnp.where(lax.axis_index("core") == lax.axis_index("xh"), mine, came)

    mid = nz // 2
    near = list(range(mid - 1)) + list(range(2 - mid, 0))
    rest = [mid - 1, 1 - mid, mid]
    near_gu = pack_gate_up(at([-k for k in near]), w_gate[0], w_up[0], 2 * width)
    rest_gu = pack_gate_up(at([-k for k in rest]), w_gate[0], w_up[0], 2 * width)
    early_down = pack_down(at(rest), w_down[0], 2 * width)
    late_down = pack_down(at(near), w_down[0], 2 * width)
    arrived, near_gu, rest_gu = lax.optimization_barrier((arrived, near_gu, rest_gu))
    near_came = from_swapped(near_gu)

    half = owners // 2 * capacity
    rows = [
        part.transpose(0, 2, 1, 3).reshape(half, 2 * width)
        for part in jnp.split(arrived.reshape(owners, 2, capacity, width), 2)
    ]
    ups, downs = [rows], [rows]
    for _ in range(1, mid):
        ups.append([along_z(x, 1) for x in ups[-1]])
        downs.append([along_z(x, -1) for x in downs[-1]])
    far = [along_z(ups[-1][0], 1), along_z(downs[-1][1], -1)]
    held = {k: ups[k] for k in range(mid)} | {-k: downs[k] for k in range(1, mid)} | {mid: far}
    blocks = {k: [(x, j * half) for j, x in enumerate(held[k])] for k in held}

    rest_came = from_swapped(after(rest_gu, ups[1]))
    early_came = from_swapped(after(early_down, ups[2]))
    late_came = from_swapped(after(late_down, ups[3]))
    near_gu = pick(near_gu, after(near_came, ups[2]))
    near_other = other_core(near_gu)
    sums = gate_up([blocks[k] for k in near], [near_gu, near_other])
    rest_gu = pick(rest_gu, after(rest_came, ups[3], downs[3]))
    rest_other = other_core(rest_gu)
    hidden = gate_up([blocks[k] for k in rest], [rest_gu, rest_other], sums, last=True)

    early_down = pick(early_down, after(early_came, far))
    early_other = other_core(early_down)
    early_down = jnp.concatenate([early_down, early_other], axis=1)

    def share(w):
        return lax.optimization_barrier(jnp.dot(hidden, w, preferred_element_type=jnp.float32))

    def add(mine, j, came):
        return mine[j * half : (j + 1) * half] + came.astype(jnp.float32)

    first = share(early_down[rest.index(mid)])
    up = [along_z(first[:half].astype(jnp.bfloat16), 1), None]
    dn = [None, along_z(first[half:].astype(jnp.bfloat16), -1)]
    late_down = pick(late_down, after(late_came, up[0]))
    late_other = other_core(late_down)
    late_down = jnp.concatenate([late_down, late_other], axis=1)
    table = {k: early_down[j] for j, k in enumerate(rest)} | {k: late_down[j] for j, k in enumerate(near)}
    for k in range(mid - 1, 0, -1):
        for chain, step in ((up, 1), (dn, -1)):
            mine = share(table[k * step])
            for j in (0, 1) if step > 0 else (1, 0):
                sent = mine[j * half : (j + 1) * half] if chain[j] is None else add(mine, j, chain[j])
                chain[j] = along_z(sent.astype(jnp.bfloat16), step)
    mine = share(table[0])
    produced = jnp.concatenate([add(mine, j, up[j]) + dn[j].astype(jnp.float32) for j in (0, 1)], axis=0)
    produced = produced.astype(jnp.bfloat16)

    back = produced.reshape(owners, capacity, 2, width).transpose(0, 2, 1, 3)
    returned = lax.all_to_all(
        back.reshape(experts, capacity, width), PLANE, split_axis=0, concat_axis=0, tiled=True
    ).reshape(slot_count, width)
    mixed = jnp.zeros((rows_dev, width), jnp.float32)
    for k in range(TOP):
        result = jnp.dot(
            picks_k[k].astype(jnp.bfloat16), returned, preferred_element_type=jnp.float32
        )
        mixed = mixed + route_weight[:, k][:, None] * result
    return mixed.astype(jnp.bfloat16)


def solution(mesh):
    fine = Mesh(mesh.devices.reshape(SHAPE), NAMES)
    expert, hidden = ("xl", "y", "core"), ("z", "xh")
    in_specs = (
        P(expert, hidden),
        P(expert, None),
        P(expert, None),
        P(expert, None, hidden),
        P(expert, None, hidden),
        P(expert, hidden, None),
    )
    return jax.shard_map(
        on_device, mesh=fine, in_specs=in_specs, out_specs=P(expert, hidden), check_vma=False
    )
```

time: 320 us -> 197 us (0.62)
  waiting for transfers between devices: 200 us -> 79.7 us
  blocking collectives: 73.5 us -> 0 us
  starting transfers between devices: 4.44 us -> 58.6 us
  Pallas kernels: 0 us -> 26.4 us
  between operations: 13.5 us -> 0.52 us
  matrix products: 16.8 us -> 8.27 us
  other arithmetic: 1.57 us -> 9.34 us
  local copies, waits for them, and re-layouts: 6.73 us -> 13.2 us
    all_gather x2 -> x0, waiting for transfers between devices: 188 us -> none  [the longest x1 143 us: on_device(): rows = lax.all_gather(arrived, 'hidden', axis=1, tiled=True)]
    all_to_all x2 -> x0, blocking collectives: 73.5 us -> none  [the longest x1 55.9 us: on_device(): lax.all_to_all(w_down[0], 'hidden', split_axis=1, concat_axis=0, tiled=True)]
    ppermute x0 -> x36, waiting for transfers between devices: none -> 68.2 us  [the longest x28 68.1 us: along_z(): return lax.ppermute(x, 'z', [(s, (s + step) % n) for s in range(n)])]
    ppermute x0 -> x36, starting transfers between devices: none -> 44.3 us  [the longest x28 34.8 us: along_z(): return lax.ppermute(x, 'z', [(s, (s + step) % n) for s in range(n)])]
    pallas_call x0 -> x6, Pallas kernels: none -> 26.4 us  [the longest x2 9.52 us: pack_gate_up(): pl.pallas_call(lambda *refs: pack_gate_up_body(units, *refs), grid_spec=p...]
    all_to_all x1 -> x2, starting transfers between devices: 4.4 us -> 14.4 us  [the longest x1 7.36 us: on_device(): lax.all_to_all(back.reshape(experts, capacity, width), PLANE, split_axis=...]
    dot_general x3 -> x8, matrix products: 13.5 us -> 5.9 us  [share(): jnp.dot(hidden, w, preferred_element_type=jnp.float32)]
    select_n x0 -> x4, other arithmetic: none -> 5.6 us  [pick(): return jnp.where(lax.axis_index('core') == lax.axis_index('xh'), mine, came)]
  transfers between devices with their start and end apart: 3 -> 38, of which waited for: 3 -> 24; matrix products, arithmetic and copies ran while one was open for 1% -> 8% of each run, Pallas kernels for 0% -> 13%
where the time goes in v2:
time: 197 us; the launch traced here: 196 us
  waiting for transfers between devices  79.7 us (40%)
  starting transfers between devices  58.6 us (30%)
  Pallas kernels  26.4 us (13%)
  local copies, waits for them, and re-layouts  13.2 us (7%)
  other arithmetic  9.34 us (5%)
  matrix products  8.27 us (4%)
    ppermute x28, waiting for transfers between devices, along_z(): return lax.ppermute(x, 'z', [(s, (s + step) % n) for s in range(n)])  68.1 us
    ppermute x28, starting transfers between devices, along_z(): return lax.ppermute(x, 'z', [(s, (s + step) % n) for s in range(n)])  34.8 us
    all_to_all x1, waiting for transfers between devices, on_device(): lax.all_to_all(back.reshape(experts, capacity, width), PLANE, split_axis=...  10.2 us
    pallas_call x2, Pallas kernels, pack_gate_up(): pl.pallas_call(lambda *refs: pack_gate_up_body(units, *refs), grid_spec=p...  9.52 us
    pallas_call x2, Pallas kernels, gate_up(): pl.pallas_call(lambda *refs: gate_up_body(tops, counts, before is None, l...  8.78 us
    unnamed x32, local copies, waits for them, and re-layouts  8.2 us
    pallas_call x2, Pallas kernels, pack_down(): pl.pallas_call(pack_down_body, grid_spec=pltpu.PrefetchScalarGridSpec(num...  8.05 us
    all_to_all x1, starting transfers between devices, on_device(): lax.all_to_all(back.reshape(experts, capacity, width), PLANE, split_axis=...  7.36 us
  transfers between devices with their start and end apart: 38, of which 24 were waited for; matrix products, arithmetic and copies ran while one was open for 8% of the time, Pallas kernels for 13%

profile of v2, /device:TPU:96, one launch (start us, length us, event | category | flops | bytes accessed | tf_op | source)
XLA Modules:
  0.0 196.0 jit_solution(2988666637717923843)
XLA Ops:
  3.3 7.0 %all-to-all-start = ((bf16[16,40,448]{2,1,0:T(8,128)(2,1)}), bf16[16,40,448]{2,1,0:T(8,128)(2,1)S(1)}, u32[]{:S(2)}, u32[]{:S(2)}) async-start(bf16[16,40,448]{2,1,0:T(8,128)(2,1)} %bitcast.3), calls=%async_computation | async-start | bytes 1310720 | tf_op jit(solution)/shard_map/all_to_all | solution.py:162
  11.1 5.4 %shard_map.64 = bf16[4480,256]{1,0:T(8,128)(2,1)} custom-call(s32[5]{0:T(128)} %stack.51.refs_0_, bf16[7168,128]{1,0:T(8,128)(2,1)} %bitcast.65, bf16[7168,128]{1,0:T(8,128)(2,1)} %bitcast.67), custom_call_target="tpu_custom_call" | custom-call | bytes 4587520 | tf_op jit(solution)/shard_map/pallas_call | solution.py:101
  17.2 4.1 %shard_map.65 = bf16[2688,256]{1,0:T(8,128)(2,1)} custom-call(s32[3]{0:T(128)} %pad_add_fusion.refs_0_, bf16[7168,128]{1,0:T(8,128)(2,1)} %bitcast.66, bf16[7168,128]{1,0:T(8,128)(2,1)} %bitcast.68), custom_call_target="tpu_custom_call" | custom-call | bytes 2752512 | tf_op jit(solution)/shard_map/pallas_call | solution.py:101
  22.7 2.1 %collective-permute-start.16 = (bf16[4480,256]{1,0:T(8,128)(2,1)}, bf16[4480,256]{1,0:T(8,128)(2,1)}, u32[]{:S(2)}, u32[]{:S(2)}) collective-permute-start(bf16[4480,256]{1,0:T(8,128)(2,1)} %shard_map.64), channel_id=1, source_target_pairs={{1,16},{16,1},{3,18},{18,3},{5,20},{20,5},{7,22},{22,7},{9,24},{24... | collective-permute-start | bytes 6881288 | tf_op jit(solution)/shard_map/ppermute | solution.py:20
  25.4 3.2 %collective-permute-start = (bf16[160,896]{1,0:T(8,128)(2,1)S(1)}, bf16[160,896]{1,0:T(8,128)(2,1)S(1)}, u32[]{:S(2)}, u32[]{:S(2)}) collective-permute-start(bf16[160,896]{1,0:T(8,128)(2,1)S(1)} %reshape.29.refs_0_), channel_id=1, source_target_pairs={{0,2},{2,4},{4,6},{6,8},{8,10},{10,12},{12,14},{14,0},{1,3},{3,5},... | collective-permute-start | bytes 860168 | tf_op jit(solution)/shard_map/ppermute | solution.py:16
  31.2 3.7 %collective-permute-done.refs_2_ = bf16[160,896]{1,0:T(8,128)(2,1)S(1)} collective-permute-done((bf16[160,896]{1,0:T(8,128)(2,1)S(1)}, bf16[160,896]{1,0:T(8,128)(2,1)S(1)}, u32[]{:S(2)}, u32[]{:S(2)}) %collective-permute-start) | collective-permute-done | bytes 286752 | tf_op jit(solution)/shard_map/ppermute | solution.py:16
  34.9 3.7 %collective-permute-start.1 = (bf16[160,896]{1,0:T(8,128)(2,1)S(1)}, bf16[160,896]{1,0:T(8,128)(2,1)}, u32[]{:S(2)}, u32[]{:S(2)}) collective-permute-start(bf16[160,896]{1,0:T(8,128)(2,1)S(1)} %collective-permute-done.refs_2_), channel_id=1, source_target_pairs={{0,2},{2,4},{4,6},{6,8},{8,10},{10,12},{12,14},{14,0},{1,3},{3,5},... | collective-permute-start | bytes 860168 | tf_op jit(solution)/shard_map/ppermute | solution.py:16
  41.1 3.7 %collective-permute-start.4 = (bf16[160,896]{1,0:T(8,128)(2,1)S(1)}, bf16[160,896]{1,0:T(8,128)(2,1)}, u32[]{:S(2)}, u32[]{:S(2)}) collective-permute-start(bf16[160,896]{1,0:T(8,128)(2,1)S(1)} %collective-permute-done.3.refs_3_), channel_id=1, source_target_pairs={{0,2},{2,4},{4,6},{6,8},{8,10},{10,12},{12,14},{14,0},{1,3},{3,5},... | collective-permute-start | bytes 860168 | tf_op jit(solution)/shard_map/ppermute | solution.py:16
  49.5 3.9 %collective-permute-done.4.refs_5_ = bf16[160,896]{1,0:T(8,128)(2,1)} collective-permute-done((bf16[160,896]{1,0:T(8,128)(2,1)S(1)}, bf16[160,896]{1,0:T(8,128)(2,1)}, u32[]{:S(2)}, u32[]{:S(2)}) %collective-permute-start.4) | collective-permute-done | bytes 286752 | tf_op jit(solution)/shard_map/ppermute | solution.py:16
  53.3 3.8 %collective-permute-start.2 = (bf16[160,896]{1,0:T(8,128)(2,1)}, bf16[160,896]{1,0:T(8,128)(2,1)S(1)}, u32[]{:S(2)}, u32[]{:S(2)}) collective-permute-start(bf16[160,896]{1,0:T(8,128)(2,1)} %collective-permute-done.1.refs_4_), channel_id=1, source_target_pairs={{0,2},{2,4},{4,6},{6,8},{8,10},{10,12},{12,14},{14,0},{1,3},{3,5},... | collective-permute-start | bytes 860168 | tf_op jit(solution)/shard_map/ppermute | solution.py:16
  57.1 4.8 %collective-permute-done.7.refs_6_ = bf16[160,896]{1,0:T(8,128)(2,1)} collective-permute-done((bf16[160,896]{1,0:T(8,128)(2,1)S(1)}, bf16[160,896]{1,0:T(8,128)(2,1)}, u32[]{:S(2)}, u32[]{:S(2)}) %collective-permute-start.7) | collective-permute-done | bytes 286752 | tf_op jit(solution)/shard_map/ppermute | solution.py:16
  67.2 3.5 %shard_map.69 = bf16[3,128,896]{2,1,0:T(8,128)(2,1)} custom-call(s32[3]{0:T(128)} %pad_add_fusion.1.at_ref, bf16[128,7168]{1,0:T(8,128)(2,1)} %bitcast.63), custom_call_target="tpu_custom_call" | custom-call | bytes 1376256 | tf_op jit(solution)/shard_map/pallas_call | solution.py:122
  71.7 2.8 %collective-permute-done.8.refs_2_ = bf16[160,896]{1,0:T(8,128)(2,1)} collective-permute-done((bf16[160,896]{1,0:T(8,128)(2,1)}, bf16[160,896]{1,0:T(8,128)(2,1)}, u32[]{:S(2)}, u32[]{:S(2)}) %collective-permute-start.8) | collective-permute-done | bytes 286752 | tf_op jit(solution)/shard_map/ppermute | solution.py:16
  74.6 2.6 %broadcast_select_fusion.1.refs_6_ = bf16[2688,256]{1,0:T(8,128)(2,1)} fusion(bf16[2688,256]{1,0:T(8,128)(2,1)} %shard_map.65, bf16[2688,256]{1,0:T(8,128)(2,1)} %collective-permute-done.14, pred[]{:T(512)S(6)} %eq.77), kind=kLoop, calls=%fused_computation.13 | loop fusion | flops 688128 | bytes 4128769 | tf_op jit(solution)/shard_map/jit(_where)/select_n | solution.py:169
  79.4 7.1 %collective-permute-done.12.refs_4_ = bf16[160,896]{1,0:T(8,128)(2,1)S(1)} collective-permute-done((bf16[160,896]{1,0:T(8,128)(2,1)S(1)}, bf16[160,896]{1,0:T(8,128)(2,1)S(1)}, u32[]{:S(2)}, u32[]{:S(2)}) %collective-permute-start.12) | collective-permute-done | bytes 286752 | tf_op jit(solution)/shard_map/ppermute | solution.py:16
  90.6 4.6 %shard_map.68 = bf16[5,128,896]{2,1,0:T(8,128)(2,1)} custom-call(s32[5]{0:T(128)} %stack.56.at_ref, bf16[128,7168]{1,0:T(8,128)(2,1)} %bitcast.64), custom_call_target="tpu_custom_call" | custom-call | bytes 2293760 | tf_op jit(solution)/shard_map/pallas_call | solution.py:122
  99.9 5.1 %shard_map.66.refs_8_ = f32[320,512]{1,0:T(8,128)S(1)} custom-call(bf16[160,896]{1,0:T(8,128)(2,1)S(1)} %reshape.29.refs_0_, bf16[160,896]{1,0:T(8,128)(2,1)S(1)} %reshape.30.refs_1_, bf16[160,896]{1,0:T(8,128)(2,1)S(1)} %copy-done.6, bf16[160,896]{1,0:T(8,128)(2,1)S(1)} %copy-done.8, bf16[160,896]{1,0:T(8,128)(2,1)} %collective-permute-done.1.refs_4_, ...), custom_call_target="tpu_custom_call" | custom-call | flops 1468006400 | bytes 7454720 | tf_op jit(solution)/shard_map/pallas_call | solution.py:77
  105.0 3.7 %shard_map.67 = bf16[320,256]{1,0:T(8,128)(2,1)S(1)} custom-call(bf16[160,896]{1,0:T(8,128)(2,1)S(1)} %collective-permute-done.2.refs_0_, bf16[160,896]{1,0:T(8,128)(2,1)} %collective-permute-done.5.refs_1_, bf16[160,896]{1,0:T(8,128)(2,1)} %collective-permute-done.8.refs_2_, bf16[160,896]{1,0:T(8,128)(2,1)} %collective-permute-done.11.refs_3_, ...), custom_call_target="tpu_custom_call" | custom-call | flops 880803840 | bytes 4472832 | tf_op jit(solution)/shard_map/pallas_call | solution.py:77
  111.1 5.8 %collective-permute-done.21 = bf16[160,896]{1,0:T(8,128)(2,1)S(1)} collective-permute-done((bf16[160,896]{1,0:T(8,128)(2,1)S(1)}, bf16[160,896]{1,0:T(8,128)(2,1)S(1)}, u32[]{:S(2)}, u32[]{:S(2)}) %collective-permute-start.21) | collective-permute-done | bytes 286752 | tf_op jit(solution)/shard_map/ppermute | solution.py:16
  117.2 3.0 %collective-permute-start.22 = (bf16[5,128,896]{2,1,0:T(8,128)(2,1)S(1)}, bf16[5,128,896]{2,1,0:T(8,128)(2,1)S(1)}, u32[]{:S(2)}, u32[]{:S(2)}) collective-permute-start(bf16[5,128,896]{2,1,0:T(8,128)(2,1)S(1)} %broadcast_select_fusion.2), channel_id=1, source_target_pairs={{0,16},{16,0},{1,17},{17,1},{2,18},{18,2},{3,19},{19,3},{4,20},{20... | collective-permute-start | bytes 3440648 | tf_op jit(solution)/shard_map/ppermute | solution.py:28
  125.3 3.5 %collective-permute-start.23 = (bf16[160,896]{1,0:T(8,128)(2,1)S(1)}, bf16[160,896]{1,0:T(8,128)(2,1)S(1)}, u32[]{:S(2)}, u32[]{:S(2)}) collective-permute-start(bf16[160,896]{1,0:T(8,128)(2,1)S(1)} %fusion.13), channel_id=1, source_target_pairs={{0,2},{2,4},{4,6},{6,8},{8,10},{10,12},{12,14},{14,0},{1,3},{3,5},... | collective-permute-start | bytes 860168 | tf_op jit(solution)/shard_map/ppermute | solution.py:16
  128.8 5.8 %collective-permute-done.32 = bf16[160,896]{1,0:T(8,128)(2,1)S(1)} collective-permute-done((bf16[160,896]{1,0:T(8,128)(2,1)S(1)}, bf16[160,896]{1,0:T(8,128)(2,1)S(1)}, u32[]{:S(2)}, u32[]{:S(2)}) %collective-permute-start.32) | collective-permute-done | bytes 286752 | tf_op jit(solution)/shard_map/ppermute | solution.py:16
  136.7 3.3 %collective-permute-start.24 = (bf16[160,896]{1,0:T(8,128)(2,1)S(1)}, bf16[160,896]{1,0:T(8,128)(2,1)S(1)}, u32[]{:S(2)}, u32[]{:S(2)}) collective-permute-start(bf16[160,896]{1,0:T(8,128)(2,1)S(1)} %get-tuple-element.29), channel_id=1, source_target_pairs={{0,2},{2,4},{4,6},{6,8},{8,10},{10,12},{12,14},{14,0},{1,3},{3,5},... | collective-permute-start | bytes 860168 | tf_op jit(solution)/shard_map/ppermute | solution.py:16
  140.8 4.9 %collective-permute-done.33 = bf16[160,896]{1,0:T(8,128)(2,1)S(1)} collective-permute-done((bf16[160,896]{1,0:T(8,128)(2,1)S(1)}, bf16[160,896]{1,0:T(8,128)(2,1)S(1)}, u32[]{:S(2)}, u32[]{:S(2)}) %collective-permute-start.33) | collective-permute-done | bytes 286752 | tf_op jit(solution)/shard_map/ppermute | solution.py:16
  147.3 4.3 %collective-permute-done.30 = bf16[160,896]{1,0:T(8,128)(2,1)S(1)} collective-permute-done((bf16[160,896]{1,0:T(8,128)(2,1)S(1)}, bf16[160,896]{1,0:T(8,128)(2,1)S(1)}, u32[]{:S(2)}, u32[]{:S(2)}) %collective-permute-start.30) | collective-permute-done | bytes 286752 | tf_op jit(solution)/shard_map/ppermute | solution.py:16
  151.7 3.8 %collective-permute-start.25 = (bf16[160,896]{1,0:T(8,128)(2,1)S(1)}, bf16[160,896]{1,0:T(8,128)(2,1)S(1)}, u32[]{:S(2)}, u32[]{:S(2)}) collective-permute-start(bf16[160,896]{1,0:T(8,128)(2,1)S(1)} %get-tuple-element.27), channel_id=1, source_target_pairs={{0,2},{2,4},{4,6},{6,8},{8,10},{10,12},{12,14},{14,0},{1,3},{3,5},... | collective-permute-start | bytes 860168 | tf_op jit(solution)/shard_map/ppermute | solution.py:16
  156.9 4.0 %collective-permute-done.34 = bf16[160,896]{1,0:T(8,128)(2,1)S(1)} collective-permute-done((bf16[160,896]{1,0:T(8,128)(2,1)S(1)}, bf16[160,896]{1,0:T(8,128)(2,1)S(1)}, u32[]{:S(2)}, u32[]{:S(2)}) %collective-permute-start.34) | collective-permute-done | bytes 286752 | tf_op jit(solution)/shard_map/ppermute | solution.py:16
  162.8 3.4 %collective-permute-done.31 = bf16[160,896]{1,0:T(8,128)(2,1)S(1)} collective-permute-done((bf16[160,896]{1,0:T(8,128)(2,1)S(1)}, bf16[160,896]{1,0:T(8,128)(2,1)S(1)}, u32[]{:S(2)}, u32[]{:S(2)}) %collective-permute-start.31) | collective-permute-done | bytes 286752 | tf_op jit(solution)/shard_map/ppermute | solution.py:16
  166.2 5.8 %collective-permute-done.28 = bf16[160,896]{1,0:T(8,128)(2,1)S(1)} collective-permute-done((bf16[160,896]{1,0:T(8,128)(2,1)S(1)}, bf16[160,896]{1,0:T(8,128)(2,1)S(1)}, u32[]{:S(2)}, u32[]{:S(2)}) %collective-permute-start.28) | collective-permute-done | bytes 286752 | tf_op jit(solution)/shard_map/ppermute | solution.py:16
  172.0 3.1 %collective-permute-done.35 = bf16[160,896]{1,0:T(8,128)(2,1)S(1)} collective-permute-done((bf16[160,896]{1,0:T(8,128)(2,1)S(1)}, bf16[160,896]{1,0:T(8,128)(2,1)S(1)}, u32[]{:S(2)}, u32[]{:S(2)}) %collective-permute-start.35) | collective-permute-done | bytes 286752 | tf_op jit(solution)/shard_map/ppermute | solution.py:16
  176.8 7.4 %all-to-all-start.1 = ((bf16[16,40,448]{2,1,0:T(8,128)(2,1)}), bf16[16,40,448]{2,1,0:T(8,128)(2,1)S(1)}, u32[]{:S(2)}, u32[]{:S(2)}) async-start(bf16[16,40,448]{2,1,0:T(8,128)(2,1)} %bitcast.29), calls=%async_computation.1 | async-start | bytes 1310720 | tf_op jit(solution)/shard_map/all_to_all | solution.py:232
  184.2 10.2 %all-to-all-done.1 = bf16[16,40,448]{2,1,0:T(8,128)(2,1)S(1)} async-done(((bf16[16,40,448]{2,1,0:T(8,128)(2,1)}), bf16[16,40,448]{2,1,0:T(8,128)(2,1)S(1)}, u32[]{:S(2)}, u32[]{:S(2)}) %all-to-all-start.1) | async-done | bytes 573472 | tf_op jit(solution)/shard_map/all_to_all | solution.py:232
  (127 shorter events, 52.6 us)
Async XLA Ops:
  3.3 19.3 %all-to-all-start = ((bf16[16,40,448]{2,1,0:T(8,128)(2,1)}), bf16[16,40,448]{2,1,0:T(8,128)(2,1)S(1)}, u32[]{:S(2)}, u32[]{:S(2)}) async-start(bf16[16,40,448]{2,1,0:T(8,128)(2,1)} %bitcast.3), calls=%async_computation | async-start | bytes 1310720 | tf_op jit(solution)/shard_map/all_to_all | solution.py:162
  22.7 39.2 %collective-permute-start.16 = (bf16[4480,256]{1,0:T(8,128)(2,1)}, bf16[4480,256]{1,0:T(8,128)(2,1)}, u32[]{:S(2)}, u32[]{:S(2)}) collective-permute-start(bf16[4480,256]{1,0:T(8,128)(2,1)} %shard_map.64), channel_id=1, source_target_pairs={{1,16},{16,1},{3,18},{18,3},{5,20},{20,5},{7,22},{22,7},{9,24},{24... | collective-permute-start | bytes 6881288 | tf_op jit(solution)/shard_map/ppermute | solution.py:20
  29.1 12.0 %collective-permute-start.3 = (bf16[160,896]{1,0:T(8,128)(2,1)S(1)}, bf16[160,896]{1,0:T(8,128)(2,1)S(1)}, u32[]{:S(2)}, u32[]{:S(2)}) collective-permute-start(bf16[160,896]{1,0:T(8,128)(2,1)S(1)} %reshape.30.refs_1_), channel_id=1, source_target_pairs={{0,2},{2,4},{4,6},{6,8},{8,10},{10,12},{12,14},{14,0},{1,3},{3,5},... | collective-permute-start | bytes 860168 | tf_op jit(solution)/shard_map/ppermute | solution.py:16
  30.2 15.3 %collective-permute-start.9 = (bf16[160,896]{1,0:T(8,128)(2,1)S(1)}, bf16[160,896]{1,0:T(8,128)(2,1)S(1)}, u32[]{:S(2)}, u32[]{:S(2)}) collective-permute-start(bf16[160,896]{1,0:T(8,128)(2,1)S(1)} %reshape.30.refs_1_), channel_id=1, source_target_pairs={{0,14},{2,0},{4,2},{6,4},{8,6},{10,8},{12,10},{14,12},{1,15},{3,1}... | collective-permute-start | bytes 860168 | tf_op jit(solution)/shard_map/ppermute | solution.py:16
  31.2 15.8 %collective-permute-start.6 = (bf16[160,896]{1,0:T(8,128)(2,1)S(1)}, bf16[160,896]{1,0:T(8,128)(2,1)S(1)}, u32[]{:S(2)}, u32[]{:S(2)}) collective-permute-start(bf16[160,896]{1,0:T(8,128)(2,1)S(1)} %reshape.29.refs_0_), channel_id=1, source_target_pairs={{0,14},{2,0},{4,2},{6,4},{8,6},{10,8},{12,10},{14,12},{1,15},{3,1}... | collective-permute-start | bytes 860168 | tf_op jit(solution)/shard_map/ppermute | solution.py:16
  34.9 12.8 %collective-permute-start.1 = (bf16[160,896]{1,0:T(8,128)(2,1)S(1)}, bf16[160,896]{1,0:T(8,128)(2,1)}, u32[]{:S(2)}, u32[]{:S(2)}) collective-permute-start(bf16[160,896]{1,0:T(8,128)(2,1)S(1)} %collective-permute-done.refs_2_), channel_id=1, source_target_pairs={{0,2},{2,4},{4,6},{6,8},{8,10},{10,12},{12,14},{14,0},{1,3},{3,5},... | collective-permute-start | bytes 860168 | tf_op jit(solution)/shard_map/ppermute | solution.py:16
  41.1 12.3 %collective-permute-start.4 = (bf16[160,896]{1,0:T(8,128)(2,1)S(1)}, bf16[160,896]{1,0:T(8,128)(2,1)}, u32[]{:S(2)}, u32[]{:S(2)}) collective-permute-start(bf16[160,896]{1,0:T(8,128)(2,1)S(1)} %collective-permute-done.3.refs_3_), channel_id=1, source_target_pairs={{0,2},{2,4},{4,6},{6,8},{8,10},{10,12},{12,14},{14,0},{1,3},{3,5},... | collective-permute-start | bytes 860168 | tf_op jit(solution)/shard_map/ppermute | solution.py:16
  45.5 11.7 %collective-permute-start.10 = (bf16[160,896]{1,0:T(8,128)(2,1)S(1)}, bf16[160,896]{1,0:T(8,128)(2,1)}, u32[]{:S(2)}, u32[]{:S(2)}) collective-permute-start(bf16[160,896]{1,0:T(8,128)(2,1)S(1)} %collective-permute-done.9.refs_9_), channel_id=1, source_target_pairs={{0,14},{2,0},{4,2},{6,4},{8,6},{10,8},{12,10},{14,12},{1,15},{3,1}... | collective-permute-start | bytes 860168 | tf_op jit(solution)/shard_map/ppermute | solution.py:16
  47.0 14.9 %collective-permute-start.7 = (bf16[160,896]{1,0:T(8,128)(2,1)S(1)}, bf16[160,896]{1,0:T(8,128)(2,1)}, u32[]{:S(2)}, u32[]{:S(2)}) collective-permute-start(bf16[160,896]{1,0:T(8,128)(2,1)S(1)} %collective-permute-done.6.refs_8_), channel_id=1, source_target_pairs={{0,14},{2,0},{4,2},{6,4},{8,6},{10,8},{12,10},{14,12},{1,15},{3,1}... | collective-permute-start | bytes 860168 | tf_op jit(solution)/shard_map/ppermute | solution.py:16
  47.7 26.9 %collective-permute-start.14 = (bf16[2688,256]{1,0:T(8,128)(2,1)}, bf16[2688,256]{1,0:T(8,128)(2,1)}, u32[]{:S(2)}, u32[]{:S(2)}) collective-permute-start(bf16[2688,256]{1,0:T(8,128)(2,1)} %shard_map.65), channel_id=1, source_target_pairs={{1,16},{16,1},{3,18},{18,3},{5,20},{20,5},{7,22},{22,7},{9,24},{24... | collective-permute-start | bytes 4128776 | tf_op jit(solution)/shard_map/ppermute | solution.py:20
  53.3 12.5 %collective-permute-start.2 = (bf16[160,896]{1,0:T(8,128)(2,1)}, bf16[160,896]{1,0:T(8,128)(2,1)S(1)}, u32[]{:S(2)}, u32[]{:S(2)}) collective-permute-start(bf16[160,896]{1,0:T(8,128)(2,1)} %collective-permute-done.1.refs_4_), channel_id=1, source_target_pairs={{0,2},{2,4},{4,6},{6,8},{8,10},{10,12},{12,14},{14,0},{1,3},{3,5},... | collective-permute-start | bytes 860168 | tf_op jit(solution)/shard_map/ppermute | solution.py:16
  57.1 13.5 %collective-permute-start.11 = (bf16[160,896]{1,0:T(8,128)(2,1)}, bf16[160,896]{1,0:T(8,128)(2,1)}, u32[]{:S(2)}, u32[]{:S(2)}) collective-permute-start(bf16[160,896]{1,0:T(8,128)(2,1)} %collective-permute-done.10.refs_7_), channel_id=1, source_target_pairs={{0,14},{2,0},{4,2},{6,4},{8,6},{10,8},{12,10},{14,12},{1,15},{3,1}... | collective-permute-start | bytes 860168 | tf_op jit(solution)/shard_map/ppermute | solution.py:16
  61.9 12.7 %collective-permute-start.8 = (bf16[160,896]{1,0:T(8,128)(2,1)}, bf16[160,896]{1,0:T(8,128)(2,1)}, u32[]{:S(2)}, u32[]{:S(2)}) collective-permute-start(bf16[160,896]{1,0:T(8,128)(2,1)} %collective-permute-done.7.refs_6_), channel_id=1, source_target_pairs={{0,14},{2,0},{4,2},{6,4},{8,6},{10,8},{12,10},{14,12},{1,15},{3,1}... | collective-permute-start | bytes 860168 | tf_op jit(solution)/shard_map/ppermute | solution.py:16
  65.8 30.2 %collective-permute-start.17 = (bf16[4480,256]{1,0:T(8,128)(2,1)S(1)}, bf16[4480,256]{1,0:T(8,128)(2,1)}, u32[]{:S(2)}, u32[]{:S(2)}) collective-permute-start(bf16[4480,256]{1,0:T(8,128)(2,1)S(1)} %broadcast_select_fusion.refs_10_), channel_id=1, source_target_pairs={{0,16},{16,0},{1,17},{17,1},{2,18},{18,2},{3,19},{19,3},{4,20},{20... | collective-permute-start | bytes 6881288 | tf_op jit(solution)/shard_map/ppermute | solution.py:28
  70.7 18.4 %collective-permute-start.19 = (bf16[3,128,896]{2,1,0:T(8,128)(2,1)}, bf16[3,128,896]{2,1,0:T(8,128)(2,1)S(1)}, u32[]{:S(2)}, u32[]{:S(2)}) collective-permute-start(bf16[3,128,896]{2,1,0:T(8,128)(2,1)} %shard_map.69), channel_id=1, source_target_pairs={{1,16},{16,1},{3,18},{18,3},{5,20},{20,5},{7,22},{22,7},{9,24},{24... | collective-permute-start | bytes 2064392 | tf_op jit(solution)/shard_map/ppermute | solution.py:20
  77.2 27.8 %collective-permute-start.15 = (bf16[2688,256]{1,0:T(8,128)(2,1)}, bf16[2688,256]{1,0:T(8,128)(2,1)}, u32[]{:S(2)}, u32[]{:S(2)}) collective-permute-start(bf16[2688,256]{1,0:T(8,128)(2,1)} %broadcast_select_fusion.1.refs_6_), channel_id=1, source_target_pairs={{0,16},{16,0},{1,17},{17,1},{2,18},{18,2},{3,19},{19,3},{4,20},{20... | collective-permute-start | bytes 4128776 | tf_op jit(solution)/shard_map/ppermute | solution.py:28
  90.0 18.7 %collective-permute-start.20 = (bf16[3,128,896]{2,1,0:T(8,128)(2,1)}, bf16[3,128,896]{2,1,0:T(8,128)(2,1)}, u32[]{:S(2)}, u32[]{:S(2)}) collective-permute-start(bf16[3,128,896]{2,1,0:T(8,128)(2,1)} %broadcast_select_fusion.3), channel_id=1, source_target_pairs={{0,16},{16,0},{1,17},{17,1},{2,18},{18,2},{3,19},{19,3},{4,20},{20... | collective-permute-start | bytes 2064392 | tf_op jit(solution)/shard_map/ppermute | solution.py:28
  95.2 16.0 %collective-permute-start.18 = (bf16[5,128,896]{2,1,0:T(8,128)(2,1)}, bf16[5,128,896]{2,1,0:T(8,128)(2,1)S(1)}, u32[]{:S(2)}, u32[]{:S(2)}) collective-permute-start(bf16[5,128,896]{2,1,0:T(8,128)(2,1)} %shard_map.68), channel_id=1, source_target_pairs={{1,16},{16,1},{3,18},{18,3},{5,20},{20,5},{7,22},{22,7},{9,24},{24... | collective-permute-start | bytes 3440648 | tf_op jit(solution)/shard_map/ppermute | solution.py:20
  117.2 17.6 %collective-permute-start.22 = (bf16[5,128,896]{2,1,0:T(8,128)(2,1)S(1)}, bf16[5,128,896]{2,1,0:T(8,128)(2,1)S(1)}, u32[]{:S(2)}, u32[]{:S(2)}) collective-permute-start(bf16[5,128,896]{2,1,0:T(8,128)(2,1)S(1)} %broadcast_select_fusion.2), channel_id=1, source_target_pairs={{0,16},{16,0},{1,17},{17,1},{2,18},{18,2},{3,19},{19,3},{4,20},{20... | collective-permute-start | bytes 3440648 | tf_op jit(solution)/shard_map/ppermute | solution.py:28
  121.6 13.5 %collective-permute-start.29 = (bf16[160,896]{1,0:T(8,128)(2,1)S(1)}, bf16[160,896]{1,0:T(8,128)(2,1)S(1)}, u32[]{:S(2)}, u32[]{:S(2)}) collective-permute-start(bf16[160,896]{1,0:T(8,128)(2,1)S(1)} %slice.250), channel_id=1, source_target_pairs={{0,2},{2,4},{4,6},{6,8},{8,10},{10,12},{12,14},{14,0},{1,3},{3,5},... | collective-permute-start | bytes 860168 | tf_op jit(solution)/shard_map/ppermute | solution.py:16
  123.7 11.0 %collective-permute-start.32 = (bf16[160,896]{1,0:T(8,128)(2,1)S(1)}, bf16[160,896]{1,0:T(8,128)(2,1)S(1)}, u32[]{:S(2)}, u32[]{:S(2)}) collective-permute-start(bf16[160,896]{1,0:T(8,128)(2,1)S(1)} %get-tuple-element.37), channel_id=1, source_target_pairs={{0,14},{2,0},{4,2},{6,4},{8,6},{10,8},{12,10},{14,12},{1,15},{3,1}... | collective-permute-start | bytes 860168 | tf_op jit(solution)/shard_map/ppermute | solution.py:16
  125.1 15.7 %collective-permute-start.26 = (bf16[160,896]{1,0:T(8,128)(2,1)S(1)}, bf16[160,896]{1,0:T(8,128)(2,1)S(1)}, u32[]{:S(2)}, u32[]{:S(2)}) collective-permute-start(bf16[160,896]{1,0:T(8,128)(2,1)S(1)} %slice.251), channel_id=1, source_target_pairs={{0,14},{2,0},{4,2},{6,4},{8,6},{10,8},{12,10},{14,12},{1,15},{3,1}... | collective-permute-start | bytes 860168 | tf_op jit(solution)/shard_map/ppermute | solution.py:16
  125.3 11.3 %collective-permute-start.23 = (bf16[160,896]{1,0:T(8,128)(2,1)S(1)}, bf16[160,896]{1,0:T(8,128)(2,1)S(1)}, u32[]{:S(2)}, u32[]{:S(2)}) collective-permute-start(bf16[160,896]{1,0:T(8,128)(2,1)S(1)} %fusion.13), channel_id=1, source_target_pairs={{0,2},{2,4},{4,6},{6,8},{8,10},{10,12},{12,14},{14,0},{1,3},{3,5},... | collective-permute-start | bytes 860168 | tf_op jit(solution)/shard_map/ppermute | solution.py:16
  134.7 11.0 %collective-permute-start.33 = (bf16[160,896]{1,0:T(8,128)(2,1)S(1)}, bf16[160,896]{1,0:T(8,128)(2,1)S(1)}, u32[]{:S(2)}, u32[]{:S(2)}) collective-permute-start(bf16[160,896]{1,0:T(8,128)(2,1)S(1)} %fusion.4), channel_id=1, source_target_pairs={{0,14},{2,0},{4,2},{6,4},{8,6},{10,8},{12,10},{14,12},{1,15},{3,1}... | collective-permute-start | bytes 860168 | tf_op jit(solution)/shard_map/ppermute | solution.py:16
  140.0 11.6 %collective-permute-start.30 = (bf16[160,896]{1,0:T(8,128)(2,1)S(1)}, bf16[160,896]{1,0:T(8,128)(2,1)S(1)}, u32[]{:S(2)}, u32[]{:S(2)}) collective-permute-start(bf16[160,896]{1,0:T(8,128)(2,1)S(1)} %get-tuple-element.30), channel_id=1, source_target_pairs={{0,2},{2,4},{4,6},{6,8},{8,10},{10,12},{12,14},{14,0},{1,3},{3,5},... | collective-permute-start | bytes 860168 | tf_op jit(solution)/shard_map/ppermute | solution.py:16
  145.8 11.1 %collective-permute-start.27 = (bf16[160,896]{1,0:T(8,128)(2,1)S(1)}, bf16[160,896]{1,0:T(8,128)(2,1)S(1)}, u32[]{:S(2)}, u32[]{:S(2)}) collective-permute-start(bf16[160,896]{1,0:T(8,128)(2,1)S(1)} %get-tuple-element.33), channel_id=1, source_target_pairs={{0,14},{2,0},{4,2},{6,4},{8,6},{10,8},{12,10},{14,12},{1,15},{3,1}... | collective-permute-start | bytes 860168 | tf_op jit(solution)/shard_map/ppermute | solution.py:16
  145.9 14.9 %collective-permute-start.34 = (bf16[160,896]{1,0:T(8,128)(2,1)S(1)}, bf16[160,896]{1,0:T(8,128)(2,1)S(1)}, u32[]{:S(2)}, u32[]{:S(2)}) collective-permute-start(bf16[160,896]{1,0:T(8,128)(2,1)S(1)} %get-tuple-element.34), channel_id=1, source_target_pairs={{0,14},{2,0},{4,2},{6,4},{8,6},{10,8},{12,10},{14,12},{1,15},{3,1}... | collective-permute-start | bytes 860168 | tf_op jit(solution)/shard_map/ppermute | solution.py:16
  151.7 11.1 %collective-permute-start.25 = (bf16[160,896]{1,0:T(8,128)(2,1)S(1)}, bf16[160,896]{1,0:T(8,128)(2,1)S(1)}, u32[]{:S(2)}, u32[]{:S(2)}) collective-permute-start(bf16[160,896]{1,0:T(8,128)(2,1)S(1)} %get-tuple-element.27), channel_id=1, source_target_pairs={{0,2},{2,4},{4,6},{6,8},{8,10},{10,12},{12,14},{14,0},{1,3},{3,5},... | collective-permute-start | bytes 860168 | tf_op jit(solution)/shard_map/ppermute | solution.py:16
  155.5 10.6 %collective-permute-start.31 = (bf16[160,896]{1,0:T(8,128)(2,1)S(1)}, bf16[160,896]{1,0:T(8,128)(2,1)S(1)}, u32[]{:S(2)}, u32[]{:S(2)}) collective-permute-start(bf16[160,896]{1,0:T(8,128)(2,1)S(1)} %get-tuple-element.28), channel_id=1, source_target_pairs={{0,2},{2,4},{4,6},{6,8},{8,10},{10,12},{12,14},{14,0},{1,3},{3,5},... | collective-permute-start | bytes 860168 | tf_op jit(solution)/shard_map/ppermute | solution.py:16
  160.9 11.0 %collective-permute-start.28 = (bf16[160,896]{1,0:T(8,128)(2,1)S(1)}, bf16[160,896]{1,0:T(8,128)(2,1)S(1)}, u32[]{:S(2)}, u32[]{:S(2)}) collective-permute-start(bf16[160,896]{1,0:T(8,128)(2,1)S(1)} %get-tuple-element.31), channel_id=1, source_target_pairs={{0,14},{2,0},{4,2},{6,4},{8,6},{10,8},{12,10},{14,12},{1,15},{3,1}... | collective-permute-start | bytes 860168 | tf_op jit(solution)/shard_map/ppermute | solution.py:16
  161.0 14.0 %collective-permute-start.35 = (bf16[160,896]{1,0:T(8,128)(2,1)S(1)}, bf16[160,896]{1,0:T(8,128)(2,1)S(1)}, u32[]{:S(2)}, u32[]{:S(2)}) collective-permute-start(bf16[160,896]{1,0:T(8,128)(2,1)S(1)} %get-tuple-element.32), channel_id=1, source_target_pairs={{0,14},{2,0},{4,2},{6,4},{8,6},{10,8},{12,10},{14,12},{1,15},{3,1}... | collective-permute-start | bytes 860168 | tf_op jit(solution)/shard_map/ppermute | solution.py:16
  176.8 17.6 %all-to-all-start.1 = ((bf16[16,40,448]{2,1,0:T(8,128)(2,1)}), bf16[16,40,448]{2,1,0:T(8,128)(2,1)S(1)}, u32[]{:S(2)}, u32[]{:S(2)}) async-start(bf16[16,40,448]{2,1,0:T(8,128)(2,1)} %bitcast.29), calls=%async_computation.1 | async-start | bytes 1310720 | tf_op jit(solution)/shard_map/all_to_all | solution.py:232
  (22 other events, 120.1 us)

commit v3 on v2

v3 whole, which is shorter than its diff:
```python
import jax
import jax.numpy as jnp
from jax import lax
from jax.experimental import pallas as pl
from jax.experimental.pallas import tpu as pltpu
from jax.sharding import Mesh, PartitionSpec as P

TOP = 2
SHAPE = (2, 4, 2, 8, 2)
NAMES = ("xl", "y", "core", "z", "xh")
PLANE = ("xl", "y", "xh")


def along_z(x, step):
    n = lax.axis_size("z")
    return lax.ppermute(x, "z", [(s, (s + step) % n) for s in range(n)])


def from_swapped(x):
    return lax.ppermute(x, ("core", "xh"), [(1, 2), (2, 1)])


def after(x, *others):
    return lax.optimization_barrier((x, others))[0]


def other_core(x):
    return lax.ppermute(x, "core", [(0, 1), (1, 0)])


def add_blocks(tops, counts, units, held, weights, total):
    step = pl.program_id(0)
    taken = 0
    for k, count in enumerate(counts):
        parts = [(held[j], tops[j]) for j in range(taken, taken + count)]
        taken += count

        @pl.when(step == k)
        def _():
            w = jnp.concatenate([w_ref[...] for w_ref in weights], axis=1)
            for x_ref, top in parts:
                at = pl.ds(top, x_ref.shape[0])
                total[at, :] += jnp.dot(x_ref[...], w, preferred_element_type=jnp.float32)


def near_body(tops, counts, units, *refs):
    held, (own_ref, other_ref, *before, out_ref) = refs[: len(tops)], refs[len(tops) :]

    @pl.when(pl.program_id(0) == 0)
    def _():
        out_ref[...] = before[0][...] if before else jnp.zeros_like(out_ref)

    add_blocks(tops, counts, units, held, (own_ref, other_ref), out_ref)


def rest_body(tops, counts, units, n, at_ref, *refs):
    held, refs = refs[: len(tops)], refs[len(tops) :]
    own_ref, other_ref, before_ref = refs[:3]
    down_refs, refs = refs[3 : 3 + 2 * n], refs[3 + 2 * n :]
    hidden_ref, first_ref, share_refs, total = refs[0], refs[1], refs[2:-1], refs[-1]
    step = pl.program_id(0)

    @pl.when(step == 0)
    def _():
        total[...] = before_ref[...]

    add_blocks(tops, counts, units, held, (own_ref, other_ref), total)

    @pl.when(step == len(counts) - 1)
    def _():
        for j in range(2):
            gate = total[:, 2 * j * units : (2 * j + 1) * units]
            up = total[:, (2 * j + 1) * units : (2 * j + 2) * units]
            act = gate / (1.0 + jnp.exp(-gate)) * up
            hidden_ref[:, j * units : (j + 1) * units] = act.astype(jnp.bfloat16)
        hidden = hidden_ref[...]
        for j in range(n):
            w = jnp.concatenate([down_refs[2 * j][...], down_refs[2 * j + 1][...]], axis=0)
            out = jnp.dot(hidden, w, preferred_element_type=jnp.float32)
            if j == 0:
                first_ref[...] = out.astype(jnp.bfloat16)
            else:
                share_refs[j - 1][...] = out


WHOLE = pl.BlockSpec(memory_space=pltpu.VMEM)


def sizes(blocks, weights):
    held = [x for parts in blocks for x, _ in parts]
    tops = [top for parts in blocks for _, top in parts]
    counts = [len(parts) for parts in blocks]
    units = weights[0].shape[1] // 2
    w_spec = pl.BlockSpec((held[0].shape[1], 2 * units), lambda k: (k, 0))
    return held, tops, counts, units, w_spec


def gate_up_near(blocks, weights, before=()):
    held, tops, counts, units, w_spec = sizes(blocks, weights)
    rows, depth = held[0].shape
    out = (rows, 4 * units)
    return pl.pallas_call(
        lambda *refs: near_body(tops, counts, units, *refs),
        grid=(len(blocks),),
        in_specs=[WHOLE] * len(held) + [w_spec] * 2 + [WHOLE] * len(before),
        out_specs=pl.BlockSpec(out, lambda k: (0, 0)),
        out_shape=jax.ShapeDtypeStruct(out, jnp.float32),
        compiler_params=pltpu.CompilerParams(vmem_limit_bytes=24 << 20),
        cost_estimate=pl.CostEstimate(
            flops=8 * len(blocks) * rows * depth * units,
            bytes_accessed=2 * len(blocks) * depth * (rows + 4 * units),
            transcendentals=0,
        ),
    )(*held, *weights, *before)


def gate_up_rest(blocks, skipped, weights, before, at, n, down):
    held, tops, counts, units, w_spec = sizes(blocks, weights)
    rows, depth = before.shape[0], held[0].shape[1]
    w_spec = pl.BlockSpec(w_spec.block_shape, lambda k, at_ref: (k + skipped, 0))
    d_specs = [
        pl.BlockSpec((units, depth), lambda k, at_ref, j=j: (0, at_ref[j])) for j in range(n) for _ in down
    ]
    out_shape = [
        jax.ShapeDtypeStruct((rows, 2 * units), jnp.bfloat16),
        jax.ShapeDtypeStruct((rows, depth), jnp.bfloat16),
    ] + [jax.ShapeDtypeStruct((rows, depth), jnp.float32)] * (n - 1)
    return pl.pallas_call(
        lambda *refs: rest_body(tops, counts, units, n, *refs),
        grid_spec=pltpu.PrefetchScalarGridSpec(
            num_scalar_prefetch=1,
            grid=(len(blocks),),
            in_specs=[WHOLE] * len(held) + [w_spec] * 2 + [WHOLE] + d_specs,
            out_specs=[pl.BlockSpec(o.shape, lambda k, at_ref: (0, 0)) for o in out_shape],
            scratch_shapes=[pltpu.VMEM((rows, 4 * units), jnp.float32)],
        ),
        out_shape=out_shape,
        compiler_params=pltpu.CompilerParams(vmem_limit_bytes=32 << 20),
        cost_estimate=pl.CostEstimate(
            flops=8 * len(blocks) * rows * depth * units + 4 * n * rows * units * depth,
            bytes_accessed=2 * len(blocks) * depth * (rows + 4 * units) + 8 * n * units * depth,
            transcendentals=2 * rows * units,
        ),
    )(at, *held, *weights, before, *(list(down) * n))


def shares_body(at_ref, hidden_ref, own_ref, other_ref, *out_refs):
    w = jnp.concatenate([own_ref[...], other_ref[...]], axis=0)
    out = jnp.dot(hidden_ref[...], w, preferred_element_type=jnp.float32)
    for k, out_ref in enumerate(out_refs):

        @pl.when(pl.program_id(0) == k)
        def _():
            out_ref[...] = out


def shares(hidden, at, n, width, down):
    rows, units = hidden.shape[0], down[0].shape[0]
    last = at.shape[0] - n
    spec = pl.BlockSpec((units, width), lambda k, at_ref: (0, at_ref[k + n]))
    return pl.pallas_call(
        shares_body,
        grid_spec=pltpu.PrefetchScalarGridSpec(
            num_scalar_prefetch=1,
            grid=(last,),
            in_specs=[WHOLE, spec, spec],
            out_specs=[pl.BlockSpec((rows, width), lambda k, at_ref: (0, 0))] * last,
        ),
        out_shape=[jax.ShapeDtypeStruct((rows, width), jnp.float32)] * last,
        compiler_params=pltpu.CompilerParams(vmem_limit_bytes=32 << 20),
        cost_estimate=pl.CostEstimate(
            flops=4 * last * rows * units * width,
            bytes_accessed=4 * last * (units + rows) * width,
            transcendentals=0,
        ),
    )(at, hidden, *down)


def pack_gate_up_body(units, at_ref, gate_ref, up_ref, out_ref):
    out_ref[:, :units] = gate_ref[...]
    out_ref[:, units:] = up_ref[...]


def pack_gate_up(at, gate, up, depth):
    n, units = at.shape[0], gate.shape[1]
    spec = pl.BlockSpec((depth, units), lambda k, at_ref: (at_ref[k], 0))
    return pl.pallas_call(
        lambda *refs: pack_gate_up_body(units, *refs),
        grid_spec=pltpu.PrefetchScalarGridSpec(
            num_scalar_prefetch=1,
            grid=(n,),
            in_specs=[spec, spec],
            out_specs=pl.BlockSpec((depth, 2 * units), lambda k, at_ref: (k, 0)),
        ),
        out_shape=jax.ShapeDtypeStruct((n * depth, 2 * units), jnp.bfloat16),
        cost_estimate=pl.CostEstimate(
            flops=0, bytes_accessed=8 * n * depth * units, transcendentals=0
        ),
    )(at, gate, up)


def on_device(tokens, route_ids, route_weight, w_gate, w_up, w_down):
    rows_dev, width = tokens.shape
    experts = lax.axis_size(PLANE)
    nz = lax.axis_size("z")
    z = lax.axis_index("z")
    capacity = (rows_dev * TOP * 5 + 4 * experts - 1) // (4 * experts)
    slot_count = experts * capacity
    owners = experts // 2
    units = w_gate.shape[2]

    matches = route_ids[:, :, None] == jnp.arange(experts, dtype=jnp.int32)[None, None, :]
    chosen = jnp.any(matches, axis=1)
    before = jnp.arange(rows_dev)[:, None] > jnp.arange(rows_dev)[None, :]
    ranking = jnp.dot(
        before.astype(jnp.bfloat16), chosen.astype(jnp.bfloat16), preferred_element_type=jnp.float32
    )
    slot_of = jnp.arange(experts, dtype=jnp.float32)[None, :] * capacity + ranking
    slot_k = jnp.sum(jnp.where(matches, slot_of[:, None, :], 0.0), axis=2).astype(jnp.int32)
    slots = jnp.arange(slot_count, dtype=jnp.int32)
    picks_k = [slot_k[:, k][:, None] == slots[None, :] for k in range(TOP)]
    picks = (picks_k[0] | picks_k[1]).astype(jnp.bfloat16)

    leaving = lax.dot_general(
        picks, tokens, (((0,), (0,)), ((), ())), preferred_element_type=jnp.float32
    ).astype(jnp.bfloat16)
    arrived = lax.all_to_all(
        leaving.reshape(experts, capacity, width), PLANE, split_axis=0, concat_axis=0, tiled=True
    )
    def at(places):
        return jnp.stack([(z + k) % nz for k in places]).astype(jnp.int32)

    def pick(mine, came):
        return jnp.where(lax.axis_index("core") == lax.axis_index("xh"), mine, came)

    mid = nz // 2
    near = [0, 1, -1]
    rest = [k for n in range(2, mid) for k in (n, -n)] + [mid]
    early = [mid, mid - 1, 1 - mid]
    late = [k for n in range(mid - 2, 0, -1) for k in (n, -n)] + [0]
    near_gu = pack_gate_up(at([-k for k in near]), w_gate[0], w_up[0], 2 * width)
    rest_gu = pack_gate_up(at([-k for k in rest]), w_gate[0], w_up[0], 2 * width)
    arrived, near_gu, rest_gu = lax.optimization_barrier((arrived, near_gu, rest_gu))
    near_came = from_swapped(near_gu)

    rows = arrived.reshape(owners, 2, capacity, width).transpose(0, 2, 1, 3)
    rows = rows.reshape(owners * capacity, 2 * width)
    half = owners * capacity // 2
    up1, down1 = along_z(rows, 1), along_z(rows, -1)

    rest_came = from_swapped(rest_gu)
    near_gu = pick(near_gu, near_came)
    up1, down1, near_gu = lax.optimization_barrier((up1, down1, near_gu))
    down_came = from_swapped(after(w_down[0], up1))
    up2, down2 = along_z(up1, 1), along_z(down1, -1)
    near_other = other_core(near_gu)
    block = {0: [(rows, 0)], 1: [(up1, 0)], -1: [(down1, 0)]}
    sums = gate_up_near([block[k] for k in near], [near_gu, near_other])

    up2, down2, sums = lax.optimization_barrier((up2, down2, sums))
    up3, down3 = along_z(up2, 1), along_z(down2, -1)
    rest_gu = pick(rest_gu, rest_came)
    own_down = pick(w_down[0], down_came)

    up3, down3, rest_gu, own_down = lax.optimization_barrier((up3, down3, rest_gu, own_down))
    far = [along_z(up3[:half], 1), along_z(down3[half:], -1)]
    rest_other = other_core(rest_gu)
    down_w = [own_down, other_core(own_down)]
    block |= {2: [(up2, 0)], -2: [(down2, 0)], 3: [(up3, 0)], -3: [(down3, 0)]}
    block[mid] = [(far[0], 0), (far[1], half)]
    to = at(early + late)
    rest_w = [rest_gu, rest_other]
    sums = gate_up_near([block[k] for k in rest[:-1]], rest_w, [sums])
    hidden, first, *early_sums = gate_up_rest(
        [block[mid]], len(rest) - 1, rest_w, sums, to, len(early), down_w
    )

    up, dn = along_z(first[:half], 1), along_z(first[half:], -1)
    late_sums = shares(hidden, to, len(early), 2 * width, down_w)
    table = {k: early_sums[j - 1] for j, k in enumerate(early)} | {k: late_sums[j] for j, k in enumerate(late)}
    for k in range(mid - 1, 0, -1):
        mine, theirs = table[k], table[-k]
        if k == mid - 1:
            mine = jnp.concatenate([mine[:half] + up.astype(jnp.float32), mine[half:]], axis=0)
            theirs = jnp.concatenate([theirs[:half], theirs[half:] + dn.astype(jnp.float32)], axis=0)
        else:
            mine, theirs = mine + up.astype(jnp.float32), theirs + dn.astype(jnp.float32)
        up = along_z(mine.astype(jnp.bfloat16), 1)
        dn = along_z(theirs.astype(jnp.bfloat16), -1)
    produced = table[0] + up.astype(jnp.float32) + dn.astype(jnp.float32)
    produced = produced.astype(jnp.bfloat16)

    back = produced.reshape(owners, capacity, 2, width).transpose(0, 2, 1, 3)
    returned = lax.all_to_all(
        back.reshape(experts, capacity, width), PLANE, split_axis=0, concat_axis=0, tiled=True
    ).reshape(slot_count, width)
    mixed = jnp.zeros((rows_dev, width), jnp.float32)
    for k in range(TOP):
        result = jnp.dot(
            picks_k[k].astype(jnp.bfloat16), returned, preferred_element_type=jnp.float32
        )
        mixed = mixed + route_weight[:, k][:, None] * result
    return mixed.astype(jnp.bfloat16)


def solution(mesh):
    fine = Mesh(mesh.devices.reshape(SHAPE), NAMES)
    expert, hidden = ("xl", "y", "core"), ("z", "xh")
    in_specs = (
        P(expert, hidden),
        P(expert, None),
        P(expert, None),
        P(expert, None, hidden),
        P(expert, None, hidden),
        P(expert, hidden, None),
    )
    return jax.shard_map(
        on_device, mesh=fine, in_specs=in_specs, out_specs=P(expert, hidden), check_vma=False
    )
```

time: 197 us -> 183 us (0.929)
  waiting for transfers between devices: 79.7 us -> 90.4 us
  starting transfers between devices: 58.6 us -> 50.7 us
  matrix products: 8.27 us -> 2.37 us
  local copies, waits for them, and re-layouts: 13.2 us -> 9.07 us
  Pallas kernels: 26.4 us -> 23.1 us
  other arithmetic: 9.34 us -> 6.62 us
    ppermute x28 -> x16, starting transfers between devices: 34.8 us -> 25.1 us  [along_z(): return lax.ppermute(x, 'z', [(s, (s + step) % n) for s in range(n)])]
    ppermute x28 -> x16, waiting for transfers between devices: 68.1 us -> 76.8 us  [along_z(): return lax.ppermute(x, 'z', [(s, (s + step) % n) for s in range(n)])]
    dot_general x8 -> x0, matrix products: 5.9 us -> none  [share(): jnp.dot(hidden, w, preferred_element_type=jnp.float32)]
    unnamed x32 -> x20, local copies, waits for them, and re-layouts: 8.2 us -> 3.21 us
    ppermute x4 -> x3, starting transfers between devices: 3.88 us -> 7.72 us  [other_core(): return lax.ppermute(x, 'core', [(0, 1), (1, 0)])]
    pallas_call x4, Pallas kernels: 16.8 us -> 13.5 us  [the longest x2 5.54 us: gate_up_near(): pl.pallas_call(lambda *refs: near_body(tops, counts, units, *refs), grid=...]
    select_n x4 -> x3, other arithmetic: 5.6 us -> 3.65 us  [pick(): return jnp.where(lax.axis_index('core') == lax.axis_index('xh'), mine, came)]
    ppermute x4 -> x3, starting transfers between devices: 5.53 us -> 4.56 us  [from_swapped(): return lax.ppermute(x, ('core', 'xh'), [(1, 2), (2, 1)])]
  transfers between devices with their start and end apart: 38 -> 24, of which waited for: 24 -> 14; matrix products, arithmetic and copies ran while one was open for 8% -> 4% of each run, Pallas kernels for 13% -> 11%
where the time goes in v3:
time: 183 us
  waiting for transfers between devices  90.4 us (49%)
  starting transfers between devices  50.7 us (28%)
  Pallas kernels  23.1 us (13%)
  local copies, waits for them, and re-layouts  9.07 us (5%)
  other arithmetic  6.62 us (4%)
  matrix products  2.37 us (1%)
    ppermute x16, waiting for transfers between devices, along_z(): return lax.ppermute(x, 'z', [(s, (s + step) % n) for s in range(n)])  76.8 us
    ppermute x16, starting transfers between devices, along_z(): return lax.ppermute(x, 'z', [(s, (s + step) % n) for s in range(n)])  25.1 us
    all_to_all x1, waiting for transfers between devices, on_device(): lax.all_to_all(back.reshape(experts, capacity, width), PLANE, split_axis=...  10.2 us
    pallas_call x2, Pallas kernels, pack_gate_up(): pl.pallas_call(lambda *refs: pack_gate_up_body(units, *refs), grid_spec=p...  9.53 us
    ppermute x3, starting transfers between devices, other_core(): return lax.ppermute(x, 'core', [(0, 1), (1, 0)])  7.72 us
    all_to_all x1, starting transfers between devices, on_device(): lax.all_to_all(leaving.reshape(experts, capacity, width), PLANE, split_ax...  7.04 us
    all_to_all x1, starting transfers between devices, on_device(): lax.all_to_all(back.reshape(experts, capacity, width), PLANE, split_axis=...  6.3 us
    pallas_call x2, Pallas kernels, gate_up_near(): pl.pallas_call(lambda *refs: near_body(tops, counts, units, *refs), grid=...  5.54 us
  transfers between devices with their start and end apart: 24, of which 14 were waited for; matrix products, arithmetic and copies ran while one was open for 4% of the time, Pallas kernels for 11%

profile of v3, /device:TPU:96, one launch (start us, length us, event | category | flops | bytes accessed | tf_op | source)
XLA Modules:
  0.0 182.6 jit_solution(10015944373805209570)
XLA Ops:
  3.3 7.0 %all-to-all-start = ((bf16[16,40,448]{2,1,0:T(8,128)(2,1)}), bf16[16,40,448]{2,1,0:T(8,128)(2,1)S(1)}, u32[]{:S(2)}, u32[]{:S(2)}) async-start(bf16[16,40,448]{2,1,0:T(8,128)(2,1)} %bitcast.11), calls=%async_computation | async-start | bytes 1310720 | tf_op jit(solution)/shard_map/all_to_all | solution.py:227
  11.1 5.4 %shard_map.65 = bf16[4480,256]{1,0:T(8,128)(2,1)} custom-call(s32[5]{0:T(128)} %stack.54.refs_0_, bf16[7168,128]{1,0:T(8,128)(2,1)} %bitcast.29, bf16[7168,128]{1,0:T(8,128)(2,1)} %bitcast.31), custom_call_target="tpu_custom_call" | custom-call | bytes 4587520 | tf_op jit(solution)/shard_map/pallas_call | solution.py:187
  17.1 4.1 %shard_map.64 = bf16[2688,256]{1,0:T(8,128)(2,1)} custom-call(s32[3]{0:T(128)} %pad_add_fusion.refs_0_, bf16[7168,128]{1,0:T(8,128)(2,1)} %bitcast.30, bf16[7168,128]{1,0:T(8,128)(2,1)} %bitcast.32), custom_call_target="tpu_custom_call" | custom-call | bytes 2752512 | tf_op jit(solution)/shard_map/pallas_call | solution.py:187
  22.7 1.7 collective-permute-start.2
  24.4 2.1 %collective-permute-start.8 = (bf16[4480,256]{1,0:T(8,128)(2,1)}, bf16[4480,256]{1,0:T(8,128)(2,1)}, u32[]{:S(2)}, u32[]{:S(2)}) collective-permute-start(bf16[4480,256]{1,0:T(8,128)(2,1)} %shard_map.65), channel_id=1, source_target_pairs={{1,16},{16,1},{3,18},{18,3},{5,20},{20,5},{7,22},{22,7},{9,24},{24... | collective-permute-start | bytes 6881288 | tf_op jit(solution)/shard_map/ppermute | solution.py:20
  27.5 3.2 %collective-permute-start = (bf16[320,896]{1,0:T(8,128)(2,1)S(1)}, bf16[320,896]{1,0:T(8,128)(2,1)S(1)}, u32[]{:S(2)}, u32[]{:S(2)}) collective-permute-start(bf16[320,896]{1,0:T(8,128)(2,1)S(1)} %reshape.27.refs_0_), channel_id=1, source_target_pairs={{0,2},{2,4},{4,6},{6,8},{8,10},{10,12},{12,14},{14,0},{1,3},{3,5},... | collective-permute-start | bytes 1720328 | tf_op jit(solution)/shard_map/ppermute | solution.py:16
  30.9 12.1 %collective-permute-done.refs_1_ = bf16[320,896]{1,0:T(8,128)(2,1)S(1)} collective-permute-done((bf16[320,896]{1,0:T(8,128)(2,1)S(1)}, bf16[320,896]{1,0:T(8,128)(2,1)S(1)}, u32[]{:S(2)}, u32[]{:S(2)}) %collective-permute-start) | collective-permute-done | bytes 573472 | tf_op jit(solution)/shard_map/ppermute | solution.py:16
  43.1 4.0 %collective-permute-done.1.refs_2_ = bf16[320,896]{1,0:T(8,128)(2,1)S(1)} collective-permute-done((bf16[320,896]{1,0:T(8,128)(2,1)S(1)}, bf16[320,896]{1,0:T(8,128)(2,1)S(1)}, u32[]{:S(2)}, u32[]{:S(2)}) %collective-permute-start.1) | collective-permute-done | bytes 573472 | tf_op jit(solution)/shard_map/ppermute | solution.py:16
  47.8 1.9 %collective-permute-start.5 = (bf16[2688,256]{1,0:T(8,128)(2,1)S(1)}, bf16[2688,256]{1,0:T(8,128)(2,1)S(1)}, u32[]{:S(2)}, u32[]{:S(2)}) collective-permute-start(bf16[2688,256]{1,0:T(8,128)(2,1)S(1)} %broadcast_select_fusion.2.refs_3_), channel_id=1, source_target_pairs={{0,16},{16,0},{1,17},{17,1},{2,18},{18,2},{3,19},{19,3},{4,20},{20... | collective-permute-start | bytes 4128776 | tf_op jit(solution)/shard_map/ppermute | solution.py:28
  49.8 2.9 %collective-permute-start.3 = (bf16[320,896]{1,0:T(8,128)(2,1)S(1)}, bf16[320,896]{1,0:T(8,128)(2,1)S(1)}, u32[]{:S(2)}, u32[]{:S(2)}) collective-permute-start(bf16[320,896]{1,0:T(8,128)(2,1)S(1)} %collective-permute-done.refs_1_), channel_id=1, source_target_pairs={{0,2},{2,4},{4,6},{6,8},{8,10},{10,12},{12,14},{14,0},{1,3},{3,5},... | collective-permute-start | bytes 1720328 | tf_op jit(solution)/shard_map/ppermute | solution.py:16
  52.7 3.3 %broadcast_select_fusion.refs_4_.refs_3_ = bf16[4480,256]{1,0:T(8,128)(2,1)} fusion(bf16[4480,256]{1,0:T(8,128)(2,1)} %shard_map.65, bf16[4480,256]{1,0:T(8,128)(2,1)} %collective-permute-done.8, pred[]{:T(512)S(6)} %eq.76), kind=kLoop, calls=%fused_computation | loop fusion | flops 1146880 | bytes 6881281 | tf_op jit(solution)/shard_map/jit(_where)/select_n | solution.py:234
  57.6 7.6 %collective-permute-done.3.refs_0_ = bf16[320,896]{1,0:T(8,128)(2,1)S(1)} collective-permute-done((bf16[320,896]{1,0:T(8,128)(2,1)S(1)}, bf16[320,896]{1,0:T(8,128)(2,1)S(1)}, u32[]{:S(2)}, u32[]{:S(2)}) %collective-permute-start.3) | collective-permute-done | bytes 573472 | tf_op jit(solution)/shard_map/ppermute | solution.py:16
  65.2 3.4 %collective-permute-done.4.refs_1_ = bf16[320,896]{1,0:T(8,128)(2,1)S(1)} collective-permute-done((bf16[320,896]{1,0:T(8,128)(2,1)S(1)}, bf16[320,896]{1,0:T(8,128)(2,1)S(1)}, u32[]{:S(2)}, u32[]{:S(2)}) %collective-permute-start.4) | collective-permute-done | bytes 573472 | tf_op jit(solution)/shard_map/ppermute | solution.py:16
  69.0 1.7 collective-permute-start.7
  70.9 10.7 %collective-permute-done.6.refs_2_ = bf16[320,896]{1,0:T(8,128)(2,1)S(1)} collective-permute-done((bf16[320,896]{1,0:T(8,128)(2,1)S(1)}, bf16[320,896]{1,0:T(8,128)(2,1)S(1)}, u32[]{:S(2)}, u32[]{:S(2)}) %collective-permute-start.6) | collective-permute-done | bytes 573472 | tf_op jit(solution)/shard_map/ppermute | solution.py:16
  81.6 5.7 %collective-permute-start.12 = (bf16[4480,256]{1,0:T(8,128)(2,1)}, bf16[4480,256]{1,0:T(8,128)(2,1)}, u32[]{:S(2)}, u32[]{:S(2)}) collective-permute-start(bf16[4480,256]{1,0:T(8,128)(2,1)} %broadcast_select_fusion.refs_4_.refs_3_), channel_id=1, source_target_pairs={{0,16},{16,0},{1,17},{17,1},{2,18},{18,2},{3,19},{19,3},{4,20},{20... | collective-permute-start | bytes 6881288 | tf_op jit(solution)/shard_map/ppermute | solution.py:28
  88.1 3.1 %collective-permute-start.10 = (bf16[160,896]{1,0:T(8,128)(2,1)}, bf16[160,896]{1,0:T(8,128)(2,1)}, u32[]{:S(2)}, u32[]{:S(2)}) collective-permute-start(bf16[160,896]{1,0:T(8,128)(2,1)} %slice.41), channel_id=1, source_target_pairs={{0,2},{2,4},{4,6},{6,8},{8,10},{10,12},{12,14},{14,0},{1,3},{3,5},... | collective-permute-start | bytes 860168 | tf_op jit(solution)/shard_map/ppermute | solution.py:16
  92.1 1.9 %collective-permute-done.12.refs_5_.refs_4_ = bf16[4480,256]{1,0:T(8,128)(2,1)} collective-permute-done((bf16[4480,256]{1,0:T(8,128)(2,1)}, bf16[4480,256]{1,0:T(8,128)(2,1)}, u32[]{:S(2)}, u32[]{:S(2)}) %collective-permute-start.12) | collective-permute-done | bytes 2293792 | tf_op jit(solution)/shard_map/ppermute | solution.py:28
  97.2 4.0 %shard_map.67.refs_5_ = f32[320,512]{1,0:T(8,128)S(1)} custom-call(bf16[320,896]{1,0:T(8,128)(2,1)S(1)} %copy-done.4, bf16[320,896]{1,0:T(8,128)(2,1)S(1)} %copy-done.6, bf16[320,896]{1,0:T(8,128)(2,1)S(1)} %collective-permute-done.6.refs_2_, bf16[320,896]{1,0:T(8,128)(2,1)S(1)} %copy-done.2, bf16[4480,256]{1,0:T(8,128)(2,1)} %broadcast_select_fusion.refs_4_.refs_3_, ...), custom_call_target="tpu_custom_call" | custom-call | flops 1174405120 | bytes 5963776 | tf_op jit(solution)/shard_map/pallas_call | solution.py:102
  102.4 3.2 %shard_map.68 = (bf16[320,256]{1,0:T(8,128)(2,1)S(1)}, bf16[320,896]{1,0:T(8,128)(2,1)S(1)}, f32[320,896]{1,0:T(8,128)S(1)}, f32[320,896]{1,0:T(8,128)S(1)}) custom-call(s32[8]{0:T(128)S(1)} %stack.51.refs_0_.at_ref, bf16[160,896]{1,0:T(8,128)(2,1)} %collective-permute-done.10.refs_1_, bf16[160,896]{1,0:T(8,128)(2,1)} %collective-permute-done.11.refs_2_, ...), custom_call_target="tpu_custom_call" | custom-call | flops 734003200 | bytes 4243456 | tf_op jit(solution)/shard_map/pallas_call | solution.py:128
  105.7 2.0 %collective-permute-start.14 = (bf16[160,896]{1,0:T(8,128)(2,1)S(1)}, bf16[160,896]{1,0:T(8,128)(2,1)S(1)}, u32[]{:S(2)}, u32[]{:S(2)}) collective-permute-start(bf16[160,896]{1,0:T(8,128)(2,1)S(1)} %get-tuple-element.51), channel_id=1, source_target_pairs={{0,2},{2,4},{4,6},{6,8},{8,10},{10,12},{12,14},{14,0},{1,3},{3,5},... | collective-permute-start | bytes 860168 | tf_op jit(solution)/shard_map/ppermute | solution.py:16
  107.9 6.3 %collective-permute-done.14 = bf16[160,896]{1,0:T(8,128)(2,1)S(1)} collective-permute-done((bf16[160,896]{1,0:T(8,128)(2,1)S(1)}, bf16[160,896]{1,0:T(8,128)(2,1)S(1)}, u32[]{:S(2)}, u32[]{:S(2)}) %collective-permute-start.14) | collective-permute-done | bytes 286752 | tf_op jit(solution)/shard_map/ppermute | solution.py:16
  114.4 3.8 %collective-permute-start.15 = (bf16[320,896]{1,0:T(8,128)(2,1)S(1)}, bf16[320,896]{1,0:T(8,128)(2,1)S(1)}, u32[]{:S(2)}, u32[]{:S(2)}) collective-permute-start(bf16[320,896]{1,0:T(8,128)(2,1)S(1)} %pad_maximum_fusion), channel_id=1, source_target_pairs={{0,2},{2,4},{4,6},{6,8},{8,10},{10,12},{12,14},{14,0},{1,3},{3,5},... | collective-permute-start | bytes 1720328 | tf_op jit(solution)/shard_map/ppermute | solution.py:16
  118.4 4.8 %shard_map.69 = (f32[320,896]{1,0:T(8,128)S(1)}, f32[320,896]{1,0:T(8,128)S(1)}, f32[320,896]{1,0:T(8,128)S(1)}, f32[320,896]{1,0:T(8,128)S(1)}, f32[320,896]{1,0:T(8,128)S(1)}) custom-call(s32[8]{0:T(128)S(1)} %stack.51.refs_0_.at_ref, bf16[320,256]{1,0:T(8,128)(2,1)S(1)} %get-tuple-element.42.hidden_ref, ...), custom_call_target="tpu_custom_call" | custom-call | flops 734003200 | bytes 8028160 | tf_op jit(solution)/shard_map/pallas_call | solution.py:161
  123.1 7.0 %collective-permute-done.15 = bf16[320,896]{1,0:T(8,128)(2,1)S(1)} collective-permute-done((bf16[320,896]{1,0:T(8,128)(2,1)S(1)}, bf16[320,896]{1,0:T(8,128)(2,1)S(1)}, u32[]{:S(2)}, u32[]{:S(2)}) %collective-permute-start.15) | collective-permute-done | bytes 573472 | tf_op jit(solution)/shard_map/ppermute | solution.py:16
  130.2 3.8 %collective-permute-start.16 = (bf16[320,896]{1,0:T(8,128)(2,1)S(1)}, bf16[320,896]{1,0:T(8,128)(2,1)S(1)}, u32[]{:S(2)}, u32[]{:S(2)}) collective-permute-start(bf16[320,896]{1,0:T(8,128)(2,1)S(1)} %add_convert_fusion.4), channel_id=1, source_target_pairs={{0,2},{2,4},{4,6},{6,8},{8,10},{10,12},{12,14},{14,0},{1,3},{3,5},... | collective-permute-start | bytes 1720328 | tf_op jit(solution)/shard_map/ppermute | solution.py:16
  134.2 10.8 %collective-permute-done.16 = bf16[320,896]{1,0:T(8,128)(2,1)S(1)} collective-permute-done((bf16[320,896]{1,0:T(8,128)(2,1)S(1)}, bf16[320,896]{1,0:T(8,128)(2,1)S(1)}, u32[]{:S(2)}, u32[]{:S(2)}) %collective-permute-start.16) | collective-permute-done | bytes 573472 | tf_op jit(solution)/shard_map/ppermute | solution.py:16
  145.2 3.8 %collective-permute-start.17 = (bf16[320,896]{1,0:T(8,128)(2,1)S(1)}, bf16[320,896]{1,0:T(8,128)(2,1)S(1)}, u32[]{:S(2)}, u32[]{:S(2)}) collective-permute-start(bf16[320,896]{1,0:T(8,128)(2,1)S(1)} %add_convert_fusion.3), channel_id=1, source_target_pairs={{0,2},{2,4},{4,6},{6,8},{8,10},{10,12},{12,14},{14,0},{1,3},{3,5},... | collective-permute-start | bytes 1720328 | tf_op jit(solution)/shard_map/ppermute | solution.py:16
  149.1 9.9 %collective-permute-done.17 = bf16[320,896]{1,0:T(8,128)(2,1)S(1)} collective-permute-done((bf16[320,896]{1,0:T(8,128)(2,1)S(1)}, bf16[320,896]{1,0:T(8,128)(2,1)S(1)}, u32[]{:S(2)}, u32[]{:S(2)}) %collective-permute-start.17) | collective-permute-done | bytes 573472 | tf_op jit(solution)/shard_map/ppermute | solution.py:16
  159.1 3.6 %collective-permute-done.21 = bf16[320,896]{1,0:T(8,128)(2,1)S(1)} collective-permute-done((bf16[320,896]{1,0:T(8,128)(2,1)S(1)}, bf16[320,896]{1,0:T(8,128)(2,1)S(1)}, u32[]{:S(2)}, u32[]{:S(2)}) %collective-permute-start.21) | collective-permute-done | bytes 573472 | tf_op jit(solution)/shard_map/ppermute | solution.py:16
  164.4 6.3 %all-to-all-start.1 = ((bf16[16,40,448]{2,1,0:T(8,128)(2,1)}), bf16[16,40,448]{2,1,0:T(8,128)(2,1)S(1)}, u32[]{:S(2)}, u32[]{:S(2)}) async-start(bf16[16,40,448]{2,1,0:T(8,128)(2,1)} %bitcast.19), calls=%async_computation.1 | async-start | bytes 1310720 | tf_op jit(solution)/shard_map/all_to_all | solution.py:294
  170.7 10.2 %all-to-all-done.1 = bf16[16,40,448]{2,1,0:T(8,128)(2,1)S(1)} async-done(((bf16[16,40,448]{2,1,0:T(8,128)(2,1)}), bf16[16,40,448]{2,1,0:T(8,128)(2,1)S(1)}, u32[]{:S(2)}, u32[]{:S(2)}) %all-to-all-start.1) | async-done | bytes 573472 | tf_op jit(solution)/shard_map/all_to_all | solution.py:294
  (77 shorter events, 20.8 us)
Async XLA Ops:
  0.0 1.7 copy-start
  3.3 19.3 %all-to-all-start = ((bf16[16,40,448]{2,1,0:T(8,128)(2,1)}), bf16[16,40,448]{2,1,0:T(8,128)(2,1)S(1)}, u32[]{:S(2)}, u32[]{:S(2)}) async-start(bf16[16,40,448]{2,1,0:T(8,128)(2,1)} %bitcast.11), calls=%async_computation | async-start | bytes 1310720 | tf_op jit(solution)/shard_map/all_to_all | solution.py:227
  22.7 8.1 %collective-permute-start.2 = (bf16[2688,256]{1,0:T(8,128)(2,1)}, bf16[2688,256]{1,0:T(8,128)(2,1)}, u32[]{:S(2)}, u32[]{:S(2)}) collective-permute-start(bf16[2688,256]{1,0:T(8,128)(2,1)} %shard_map.64), channel_id=1, source_target_pairs={{1,16},{16,1},{3,18},{18,3},{5,20},{20,5},{7,22},{22,7},{9,24},{24... | collective-permute-start | bytes 4128776 | tf_op jit(solution)/shard_map/ppermute | solution.py:20
  24.4 28.3 %collective-permute-start.8 = (bf16[4480,256]{1,0:T(8,128)(2,1)}, bf16[4480,256]{1,0:T(8,128)(2,1)}, u32[]{:S(2)}, u32[]{:S(2)}) collective-permute-start(bf16[4480,256]{1,0:T(8,128)(2,1)} %shard_map.65), channel_id=1, source_target_pairs={{1,16},{16,1},{3,18},{18,3},{5,20},{20,5},{7,22},{22,7},{9,24},{24... | collective-permute-start | bytes 6881288 | tf_op jit(solution)/shard_map/ppermute | solution.py:20
  26.5 4.3 %copy-start.7 = (bf16[2688,256]{1,0:T(8,128)(2,1)S(1)}, bf16[2688,256]{1,0:T(8,128)(2,1)}, u32[]{:S(2)}) copy-start(bf16[2688,256]{1,0:T(8,128)(2,1)} %shard_map.64) | copy-start | bytes 4128772
  27.5 19.5 %copy-start.8 = (bf16[1,128,7168]{2,1,0:T(8,128)(2,1)S(1)}, bf16[1,128,7168]{2,1,0:T(8,128)(2,1)}, u32[]{:S(2)}) copy-start(bf16[1,128,7168]{2,1,0:T(8,128)(2,1)} %param.11) | copy-start | bytes 5505028
  27.5 15.5 %collective-permute-start = (bf16[320,896]{1,0:T(8,128)(2,1)S(1)}, bf16[320,896]{1,0:T(8,128)(2,1)S(1)}, u32[]{:S(2)}, u32[]{:S(2)}) collective-permute-start(bf16[320,896]{1,0:T(8,128)(2,1)S(1)} %reshape.27.refs_0_), channel_id=1, source_target_pairs={{0,2},{2,4},{4,6},{6,8},{8,10},{10,12},{12,14},{14,0},{1,3},{3,5},... | collective-permute-start | bytes 1720328 | tf_op jit(solution)/shard_map/ppermute | solution.py:16
  30.7 16.3 %collective-permute-start.1 = (bf16[320,896]{1,0:T(8,128)(2,1)S(1)}, bf16[320,896]{1,0:T(8,128)(2,1)S(1)}, u32[]{:S(2)}, u32[]{:S(2)}) collective-permute-start(bf16[320,896]{1,0:T(8,128)(2,1)S(1)} %reshape.27.refs_0_), channel_id=1, source_target_pairs={{0,14},{2,0},{4,2},{6,4},{8,6},{10,8},{12,10},{14,12},{1,15},{3,1}... | collective-permute-start | bytes 1720328 | tf_op jit(solution)/shard_map/ppermute | solution.py:16
  47.1 23.6 %collective-permute-start.9 = (bf16[128,7168]{1,0:T(8,128)(2,1)S(1)}, bf16[128,7168]{1,0:T(8,128)(2,1)S(1)}, u32[]{:S(2)}, u32[]{:S(2)}) collective-permute-start(bf16[128,7168]{1,0:T(8,128)(2,1)S(1)} %bitcast.36), channel_id=1, source_target_pairs={{1,16},{16,1},{3,18},{18,3},{5,20},{20,5},{7,22},{22,7},{9,24},{24... | collective-permute-start | bytes 5505032 | tf_op jit(solution)/shard_map/ppermute | solution.py:20
  47.8 8.2 %collective-permute-start.5 = (bf16[2688,256]{1,0:T(8,128)(2,1)S(1)}, bf16[2688,256]{1,0:T(8,128)(2,1)S(1)}, u32[]{:S(2)}, u32[]{:S(2)}) collective-permute-start(bf16[2688,256]{1,0:T(8,128)(2,1)S(1)} %broadcast_select_fusion.2.refs_3_), channel_id=1, source_target_pairs={{0,16},{16,0},{1,17},{17,1},{2,18},{18,2},{3,19},{19,3},{4,20},{20... | collective-permute-start | bytes 4128776 | tf_op jit(solution)/shard_map/ppermute | solution.py:28
  49.8 15.4 %collective-permute-start.3 = (bf16[320,896]{1,0:T(8,128)(2,1)S(1)}, bf16[320,896]{1,0:T(8,128)(2,1)S(1)}, u32[]{:S(2)}, u32[]{:S(2)}) collective-permute-start(bf16[320,896]{1,0:T(8,128)(2,1)S(1)} %collective-permute-done.refs_1_), channel_id=1, source_target_pairs={{0,2},{2,4},{4,6},{6,8},{8,10},{10,12},{12,14},{14,0},{1,3},{3,5},... | collective-permute-start | bytes 1720328 | tf_op jit(solution)/shard_map/ppermute | solution.py:16
  52.7 15.9 %collective-permute-start.4 = (bf16[320,896]{1,0:T(8,128)(2,1)S(1)}, bf16[320,896]{1,0:T(8,128)(2,1)S(1)}, u32[]{:S(2)}, u32[]{:S(2)}) collective-permute-start(bf16[320,896]{1,0:T(8,128)(2,1)S(1)} %collective-permute-done.1.refs_2_), channel_id=1, source_target_pairs={{0,14},{2,0},{4,2},{6,4},{8,6},{10,8},{12,10},{14,12},{1,15},{3,1}... | collective-permute-start | bytes 1720328 | tf_op jit(solution)/shard_map/ppermute | solution.py:16
  65.2 5.6 %copy-start.3 = (bf16[320,896]{1,0:T(8,128)(2,1)}, bf16[320,896]{1,0:T(8,128)(2,1)S(1)}, u32[]{:S(2)}) copy-start(bf16[320,896]{1,0:T(8,128)(2,1)S(1)} %collective-permute-done.3.refs_0_) | copy-start | bytes 1720324
  68.6 2.2 %copy-start.5 = (bf16[320,896]{1,0:T(8,128)(2,1)}, bf16[320,896]{1,0:T(8,128)(2,1)S(1)}, u32[]{:S(2)}) copy-start(bf16[320,896]{1,0:T(8,128)(2,1)S(1)} %collective-permute-done.4.refs_1_) | copy-start | bytes 1720324
  68.6 13.0 %collective-permute-start.6 = (bf16[320,896]{1,0:T(8,128)(2,1)S(1)}, bf16[320,896]{1,0:T(8,128)(2,1)S(1)}, u32[]{:S(2)}, u32[]{:S(2)}) collective-permute-start(bf16[320,896]{1,0:T(8,128)(2,1)S(1)} %collective-permute-done.3.refs_0_), channel_id=1, source_target_pairs={{0,2},{2,4},{4,6},{6,8},{8,10},{10,12},{12,14},{14,0},{1,3},{3,5},... | collective-permute-start | bytes 1720328 | tf_op jit(solution)/shard_map/ppermute | solution.py:16
  69.0 12.6 %collective-permute-start.7 = (bf16[320,896]{1,0:T(8,128)(2,1)S(1)}, bf16[320,896]{1,0:T(8,128)(2,1)S(1)}, u32[]{:S(2)}, u32[]{:S(2)}) collective-permute-start(bf16[320,896]{1,0:T(8,128)(2,1)S(1)} %collective-permute-done.4.refs_1_), channel_id=1, source_target_pairs={{0,14},{2,0},{4,2},{6,4},{8,6},{10,8},{12,10},{14,12},{1,15},{3,1}... | collective-permute-start | bytes 1720328 | tf_op jit(solution)/shard_map/ppermute | solution.py:16
  81.6 9.7 %copy-start.1 = (bf16[320,896]{1,0:T(8,128)(2,1)}, bf16[320,896]{1,0:T(8,128)(2,1)S(1)}, u32[]{:S(2)}) copy-start(bf16[320,896]{1,0:T(8,128)(2,1)S(1)} %collective-permute-done.7.refs_3_) | copy-start | bytes 1720324
  81.6 12.4 %collective-permute-start.12 = (bf16[4480,256]{1,0:T(8,128)(2,1)}, bf16[4480,256]{1,0:T(8,128)(2,1)}, u32[]{:S(2)}, u32[]{:S(2)}) collective-permute-start(bf16[4480,256]{1,0:T(8,128)(2,1)} %broadcast_select_fusion.refs_4_.refs_3_), channel_id=1, source_target_pairs={{0,16},{16,0},{1,17},{17,1},{2,18},{18,2},{3,19},{19,3},{4,20},{20... | collective-permute-start | bytes 6881288 | tf_op jit(solution)/shard_map/ppermute | solution.py:28
  87.3 15.1 %collective-permute-start.13 = (bf16[128,7168]{1,0:T(8,128)(2,1)S(1)}, bf16[128,7168]{1,0:T(8,128)(2,1)}, u32[]{:S(2)}, u32[]{:S(2)}) collective-permute-start(bf16[128,7168]{1,0:T(8,128)(2,1)S(1)} %broadcast_select_fusion.1.refs_6_.refs_8_.refs_10_.own_ref), channel_id=1, source_target_pairs={{0,16},{16,0},{1,17},{17,1},{2,18},{18,2},{3,19},{19,3},{4,20},{20... | collective-permute-start | bytes 5505032 | tf_op jit(solution)/shard_map/ppermute | solution.py:28
  88.1 13.0 %collective-permute-start.10 = (bf16[160,896]{1,0:T(8,128)(2,1)}, bf16[160,896]{1,0:T(8,128)(2,1)}, u32[]{:S(2)}, u32[]{:S(2)}) collective-permute-start(bf16[160,896]{1,0:T(8,128)(2,1)} %slice.41), channel_id=1, source_target_pairs={{0,2},{2,4},{4,6},{6,8},{8,10},{10,12},{12,14},{14,0},{1,3},{3,5},... | collective-permute-start | bytes 860168 | tf_op jit(solution)/shard_map/ppermute | solution.py:16
  92.0 10.4 %collective-permute-start.11 = (bf16[160,896]{1,0:T(8,128)(2,1)}, bf16[160,896]{1,0:T(8,128)(2,1)}, u32[]{:S(2)}, u32[]{:S(2)}) collective-permute-start(bf16[160,896]{1,0:T(8,128)(2,1)} %slice.42), channel_id=1, source_target_pairs={{0,14},{2,0},{4,2},{6,4},{8,6},{10,8},{12,10},{14,12},{1,15},{3,1}... | collective-permute-start | bytes 860168 | tf_op jit(solution)/shard_map/ppermute | solution.py:16
  95.0 1.1 copy-start.4
  105.7 8.6 %collective-permute-start.14 = (bf16[160,896]{1,0:T(8,128)(2,1)S(1)}, bf16[160,896]{1,0:T(8,128)(2,1)S(1)}, u32[]{:S(2)}, u32[]{:S(2)}) collective-permute-start(bf16[160,896]{1,0:T(8,128)(2,1)S(1)} %get-tuple-element.51), channel_id=1, source_target_pairs={{0,2},{2,4},{4,6},{6,8},{8,10},{10,12},{12,14},{14,0},{1,3},{3,5},... | collective-permute-start | bytes 860168 | tf_op jit(solution)/shard_map/ppermute | solution.py:16
  107.7 10.5 %collective-permute-start.18 = (bf16[160,896]{1,0:T(8,128)(2,1)S(1)}, bf16[160,896]{1,0:T(8,128)(2,1)S(1)}, u32[]{:S(2)}, u32[]{:S(2)}) collective-permute-start(bf16[160,896]{1,0:T(8,128)(2,1)S(1)} %get-tuple-element.52), channel_id=1, source_target_pairs={{0,14},{2,0},{4,2},{6,4},{8,6},{10,8},{12,10},{14,12},{1,15},{3,1}... | collective-permute-start | bytes 860168 | tf_op jit(solution)/shard_map/ppermute | solution.py:16
  114.4 15.7 %collective-permute-start.15 = (bf16[320,896]{1,0:T(8,128)(2,1)S(1)}, bf16[320,896]{1,0:T(8,128)(2,1)S(1)}, u32[]{:S(2)}, u32[]{:S(2)}) collective-permute-start(bf16[320,896]{1,0:T(8,128)(2,1)S(1)} %pad_maximum_fusion), channel_id=1, source_target_pairs={{0,2},{2,4},{4,6},{6,8},{8,10},{10,12},{12,14},{14,0},{1,3},{3,5},... | collective-permute-start | bytes 1720328 | tf_op jit(solution)/shard_map/ppermute | solution.py:16
  118.3 15.7 %collective-permute-start.19 = (bf16[320,896]{1,0:T(8,128)(2,1)S(1)}, bf16[320,896]{1,0:T(8,128)(2,1)S(1)}, u32[]{:S(2)}, u32[]{:S(2)}) collective-permute-start(bf16[320,896]{1,0:T(8,128)(2,1)S(1)} %pad_maximum_fusion.1), channel_id=1, source_target_pairs={{0,14},{2,0},{4,2},{6,4},{8,6},{10,8},{12,10},{14,12},{1,15},{3,1}... | collective-permute-start | bytes 1720328 | tf_op jit(solution)/shard_map/ppermute | solution.py:16
  130.2 14.8 %collective-permute-start.16 = (bf16[320,896]{1,0:T(8,128)(2,1)S(1)}, bf16[320,896]{1,0:T(8,128)(2,1)S(1)}, u32[]{:S(2)}, u32[]{:S(2)}) collective-permute-start(bf16[320,896]{1,0:T(8,128)(2,1)S(1)} %add_convert_fusion.4), channel_id=1, source_target_pairs={{0,2},{2,4},{4,6},{6,8},{8,10},{10,12},{12,14},{14,0},{1,3},{3,5},... | collective-permute-start | bytes 1720328 | tf_op jit(solution)/shard_map/ppermute | solution.py:16
  134.1 14.8 %collective-permute-start.20 = (bf16[320,896]{1,0:T(8,128)(2,1)S(1)}, bf16[320,896]{1,0:T(8,128)(2,1)S(1)}, u32[]{:S(2)}, u32[]{:S(2)}) collective-permute-start(bf16[320,896]{1,0:T(8,128)(2,1)S(1)} %add_convert_fusion.2), channel_id=1, source_target_pairs={{0,14},{2,0},{4,2},{6,4},{8,6},{10,8},{12,10},{14,12},{1,15},{3,1}... | collective-permute-start | bytes 1720328 | tf_op jit(solution)/shard_map/ppermute | solution.py:16
  145.2 13.9 %collective-permute-start.17 = (bf16[320,896]{1,0:T(8,128)(2,1)S(1)}, bf16[320,896]{1,0:T(8,128)(2,1)S(1)}, u32[]{:S(2)}, u32[]{:S(2)}) collective-permute-start(bf16[320,896]{1,0:T(8,128)(2,1)S(1)} %add_convert_fusion.3), channel_id=1, source_target_pairs={{0,2},{2,4},{4,6},{6,8},{8,10},{10,12},{12,14},{14,0},{1,3},{3,5},... | collective-permute-start | bytes 1720328 | tf_op jit(solution)/shard_map/ppermute | solution.py:16
  149.1 13.6 %collective-permute-start.21 = (bf16[320,896]{1,0:T(8,128)(2,1)S(1)}, bf16[320,896]{1,0:T(8,128)(2,1)S(1)}, u32[]{:S(2)}, u32[]{:S(2)}) collective-permute-start(bf16[320,896]{1,0:T(8,128)(2,1)S(1)} %add_convert_fusion.1), channel_id=1, source_target_pairs={{0,14},{2,0},{4,2},{6,4},{8,6},{10,8},{12,10},{14,12},{1,15},{3,1}... | collective-permute-start | bytes 1720328 | tf_op jit(solution)/shard_map/ppermute | solution.py:16
  163.4 7.2 %copy-start.9 = (f32[256,2]{0,1:T(2,128)S(1)}, f32[256,2]{0,1:T(2,128)}, u32[]{:S(2)}) copy-start(f32[256,2]{0,1:T(2,128)} %param.8) | copy-start | bytes 6148
  164.4 16.5 %all-to-all-start.1 = ((bf16[16,40,448]{2,1,0:T(8,128)(2,1)}), bf16[16,40,448]{2,1,0:T(8,128)(2,1)S(1)}, u32[]{:S(2)}, u32[]{:S(2)}) async-start(bf16[16,40,448]{2,1,0:T(8,128)(2,1)} %bitcast.19), calls=%async_computation.1 | async-start | bytes 1310720 | tf_op jit(solution)/shard_map/all_to_all | solution.py:294
  (2 other events, 2.1 us)

commit v4 on v3

--- a/solution.py
+++ b/solution.py
@@ -57,7 +57,7 @@
     held, refs = refs[: len(tops)], refs[len(tops) :]
     own_ref, other_ref, before_ref = refs[:3]
     down_refs, refs = refs[3 : 3 + 2 * n], refs[3 + 2 * n :]
-    hidden_ref, first_ref, share_refs, total = refs[0], refs[1], refs[2:-1], refs[-1]
+    hidden_ref, out_refs, total = refs[0], refs[1:-1], refs[-1]
     step = pl.program_id(0)
 
     @pl.when(step == 0)
@@ -77,10 +77,13 @@
         for j in range(n):
             w = jnp.concatenate([down_refs[2 * j][...], down_refs[2 * j + 1][...]], axis=0)
             out = jnp.dot(hidden, w, preferred_element_type=jnp.float32)
-            if j == 0:
-                first_ref[...] = out.astype(jnp.bfloat16)
-            else:
-                share_refs[j - 1][...] = out
+            put_halves(out, out_refs[2 * j : 2 * j + 2])
+
+
+def put_halves(out, refs):
+    half = refs[0].shape[0]
+    for j, ref in enumerate(refs):
+        ref[...] = out[j * half : (j + 1) * half].astype(ref.dtype)
 
 
 WHOLE = pl.BlockSpec(memory_space=pltpu.VMEM)
@@ -114,17 +117,16 @@
     )(*held, *weights, *before)
 
 
-def gate_up_rest(blocks, skipped, weights, before, at, n, down):
+def gate_up_rest(blocks, skipped, weights, before, at, types, down):
+    n = len(types)
     held, tops, counts, units, w_spec = sizes(blocks, weights)
     rows, depth = before.shape[0], held[0].shape[1]
     w_spec = pl.BlockSpec(w_spec.block_shape, lambda k, at_ref: (k + skipped, 0))
     d_specs = [
         pl.BlockSpec((units, depth), lambda k, at_ref, j=j: (0, at_ref[j])) for j in range(n) for _ in down
     ]
-    out_shape = [
-        jax.ShapeDtypeStruct((rows, 2 * units), jnp.bfloat16),
-        jax.ShapeDtypeStruct((rows, depth), jnp.bfloat16),
-    ] + [jax.ShapeDtypeStruct((rows, depth), jnp.float32)] * (n - 1)
+    out_shape = [jax.ShapeDtypeStruct((rows, 2 * units), jnp.bfloat16)]
+    out_shape += [jax.ShapeDtypeStruct((rows // 2, depth), t) for pair in types for t in pair]
     return pl.pallas_call(
         lambda *refs: rest_body(tops, counts, units, n, *refs),
         grid_spec=pltpu.PrefetchScalarGridSpec(
@@ -147,11 +149,11 @@
 def shares_body(at_ref, hidden_ref, own_ref, other_ref, *out_refs):
     w = jnp.concatenate([own_ref[...], other_ref[...]], axis=0)
     out = jnp.dot(hidden_ref[...], w, preferred_element_type=jnp.float32)
-    for k, out_ref in enumerate(out_refs):
+    for k in range(len(out_refs) // 2):
 
         @pl.when(pl.program_id(0) == k)
         def _():
-            out_ref[...] = out
+            put_halves(out, out_refs[2 * k : 2 * k + 2])
 
 
 def shares(hidden, at, n, width, down):
@@ -164,9 +166,9 @@
             num_scalar_prefetch=1,
             grid=(last,),
             in_specs=[WHOLE, spec, spec],
-            out_specs=[pl.BlockSpec((rows, width), lambda k, at_ref: (0, 0))] * last,
-        ),
-        out_shape=[jax.ShapeDtypeStruct((rows, width), jnp.float32)] * last,
+            out_specs=[pl.BlockSpec((rows // 2, width), lambda k, at_ref: (0, 0))] * (2 * last),
+        ),
+        out_shape=[jax.ShapeDtypeStruct((rows // 2, width), jnp.float32)] * (2 * last),
         compiler_params=pltpu.CompilerParams(vmem_limit_bytes=32 << 20),
         cost_estimate=pl.CostEstimate(
             flops=4 * last * rows * units * width,
@@ -262,7 +264,7 @@
     rest_gu = pick(rest_gu, rest_came)
     own_down = pick(w_down[0], down_came)
 
-    up3, down3, rest_gu, own_down = lax.optimization_barrier((up3, down3, rest_gu, own_down))
+    up3, down3, rest_gu = lax.optimization_barrier((up3, down3, rest_gu))
     far = [along_z(up3[:half], 1), along_z(down3[half:], -1)]
     rest_other = other_core(rest_gu)
     down_w = [own_down, other_core(own_down)]
@@ -271,24 +273,27 @@
     to = at(early + late)
     rest_w = [rest_gu, rest_other]
     sums = gate_up_near([block[k] for k in rest[:-1]], rest_w, [sums])
-    hidden, first, *early_sums = gate_up_rest(
-        [block[mid]], len(rest) - 1, rest_w, sums, to, len(early), down_w
-    )
-
-    up, dn = along_z(first[:half], 1), along_z(first[half:], -1)
+    wide, short = jnp.float32, jnp.bfloat16
+    hidden, *sums = gate_up_rest(
+        [block[mid]], len(rest) - 1, rest_w, sums, to, [(short, short), (wide, short), (short, wide)], down_w
+    )
+
+    def add(mine, came):
+        return (mine + came.astype(jnp.float32)).astype(jnp.bfloat16)
+
+    ups = [along_z(sums[0], 1), along_z(sums[3], 1)]
+    downs = [along_z(sums[4], -1), along_z(sums[1], -1)]
     late_sums = shares(hidden, to, len(early), 2 * width, down_w)
-    table = {k: early_sums[j - 1] for j, k in enumerate(early)} | {k: late_sums[j] for j, k in enumerate(late)}
-    for k in range(mid - 1, 0, -1):
-        mine, theirs = table[k], table[-k]
-        if k == mid - 1:
-            mine = jnp.concatenate([mine[:half] + up.astype(jnp.float32), mine[half:]], axis=0)
-            theirs = jnp.concatenate([theirs[:half], theirs[half:] + dn.astype(jnp.float32)], axis=0)
-        else:
-            mine, theirs = mine + up.astype(jnp.float32), theirs + dn.astype(jnp.float32)
-        up = along_z(mine.astype(jnp.bfloat16), 1)
-        dn = along_z(theirs.astype(jnp.bfloat16), -1)
-    produced = table[0] + up.astype(jnp.float32) + dn.astype(jnp.float32)
-    produced = produced.astype(jnp.bfloat16)
+    table = {k: late_sums[2 * j : 2 * j + 2] for j, k in enumerate(late)}
+    ups[0] = along_z(add(sums[2], ups[0]), 1)
+    downs[1] = along_z(add(sums[5], downs[1]), -1)
+    for k in range(mid - 2, 0, -1):
+        for j in (0, 1):
+            ups[1 - j] = along_z(add(table[k][1 - j], ups[1 - j]), 1)
+            downs[j] = along_z(add(table[-k][j], downs[j]), -1)
+    produced = jnp.concatenate(
+        [add(mine + up.astype(jnp.float32), dn) for mine, up, dn in zip(table[0], ups, downs)], axis=0
+    )
 
     back = produced.reshape(owners, capacity, 2, width).transpose(0, 2, 1, 3)
     returned = lax.all_to_all(

time: 183 us -> 178 us (0.973); the launches traced: 183 us -> 175 us
  waiting for transfers between devices: 90.4 us -> 73.3 us
  starting transfers between devices: 50.7 us -> 60.1 us
    ppermute x16 -> x22, waiting for transfers between devices: 76.8 us -> 61.7 us  [along_z(): return lax.ppermute(x, 'z', [(s, (s + step) % n) for s in range(n)])]
    ppermute x16 -> x22, starting transfers between devices: 25.1 us -> 31.9 us  [along_z(): return lax.ppermute(x, 'z', [(s, (s + step) % n) for s in range(n)])]
    ppermute x3, waiting for transfers between devices: 1.89 us -> 0.01 us  [other_core(): return lax.ppermute(x, 'core', [(0, 1), (1, 0)])]
  transfers between devices with their start and end apart: 24 -> 30, of which waited for: 14 -> 16; matrix products, arithmetic and copies ran while one was open for 4% -> 5% of each run, Pallas kernels for 11% -> 11%
where the time goes in v4:
time: 178 us; the launch traced here: 175 us
  waiting for transfers between devices  73.3 us (41%)
  starting transfers between devices  60.1 us (34%)
  Pallas kernels  23.1 us (13%)
  local copies, waits for them, and re-layouts  9.02 us (5%)
  other arithmetic  6.61 us (4%)
  matrix products  2.37 us (1%)
    ppermute x22, waiting for transfers between devices, along_z(): return lax.ppermute(x, 'z', [(s, (s + step) % n) for s in range(n)])  61.7 us
    ppermute x22, starting transfers between devices, along_z(): return lax.ppermute(x, 'z', [(s, (s + step) % n) for s in range(n)])  31.9 us
    all_to_all x1, waiting for transfers between devices, on_device(): lax.all_to_all(back.reshape(experts, capacity, width), PLANE, split_axis=...  10.2 us
    pallas_call x2, Pallas kernels, pack_gate_up(): pl.pallas_call(lambda *refs: pack_gate_up_body(units, *refs), grid_spec=p...  9.54 us
    ppermute x3, starting transfers between devices, other_core(): return lax.ppermute(x, 'core', [(0, 1), (1, 0)])  8.72 us
    all_to_all x1, starting transfers between devices, on_device(): lax.all_to_all(back.reshape(experts, capacity, width), PLANE, split_axis=...  7.91 us
    all_to_all x1, starting transfers between devices, on_device(): lax.all_to_all(leaving.reshape(experts, capacity, width), PLANE, split_ax...  7.04 us
    pallas_call x2, Pallas kernels, gate_up_near(): pl.pallas_call(lambda *refs: near_body(tops, counts, units, *refs), grid=...  5.56 us
  transfers between devices with their start and end apart: 30, of which 16 were waited for; matrix products, arithmetic and copies ran while one was open for 5% of the time, Pallas kernels for 11%

profile of v4, /device:TPU:96, one launch (start us, length us, event | category | flops | bytes accessed | tf_op | source)
XLA Modules:
  0.0 175.0 jit_solution(9757346989392584167)
XLA Ops:
  3.3 7.0 %all-to-all-start = ((bf16[16,40,448]{2,1,0:T(8,128)(2,1)}), bf16[16,40,448]{2,1,0:T(8,128)(2,1)S(1)}, u32[]{:S(2)}, u32[]{:S(2)}) async-start(bf16[16,40,448]{2,1,0:T(8,128)(2,1)} %bitcast.11), calls=%async_computation | async-start | bytes 1310720 | tf_op jit(solution)/shard_map/all_to_all | solution.py:229
  11.1 5.5 %shard_map.65 = bf16[4480,256]{1,0:T(8,128)(2,1)} custom-call(s32[5]{0:T(128)} %stack.54.refs_0_, bf16[7168,128]{1,0:T(8,128)(2,1)} %bitcast.29, bf16[7168,128]{1,0:T(8,128)(2,1)} %bitcast.31), custom_call_target="tpu_custom_call" | custom-call | bytes 4587520 | tf_op jit(solution)/shard_map/pallas_call | solution.py:189
  17.1 4.1 %shard_map.64 = bf16[2688,256]{1,0:T(8,128)(2,1)} custom-call(s32[3]{0:T(128)} %pad_add_fusion.refs_0_, bf16[7168,128]{1,0:T(8,128)(2,1)} %bitcast.30, bf16[7168,128]{1,0:T(8,128)(2,1)} %bitcast.32), custom_call_target="tpu_custom_call" | custom-call | bytes 2752512 | tf_op jit(solution)/shard_map/pallas_call | solution.py:189
  22.7 1.7 collective-permute-start.2
  24.4 2.1 %collective-permute-start.8 = (bf16[4480,256]{1,0:T(8,128)(2,1)}, bf16[4480,256]{1,0:T(8,128)(2,1)}, u32[]{:S(2)}, u32[]{:S(2)}) collective-permute-start(bf16[4480,256]{1,0:T(8,128)(2,1)} %shard_map.65), channel_id=1, source_target_pairs={{1,16},{16,1},{3,18},{18,3},{5,20},{20,5},{7,22},{22,7},{9,24},{24... | collective-permute-start | bytes 6881288 | tf_op jit(solution)/shard_map/ppermute | solution.py:20
  27.5 3.2 %collective-permute-start = (bf16[320,896]{1,0:T(8,128)(2,1)S(1)}, bf16[320,896]{1,0:T(8,128)(2,1)S(1)}, u32[]{:S(2)}, u32[]{:S(2)}) collective-permute-start(bf16[320,896]{1,0:T(8,128)(2,1)S(1)} %reshape.27.refs_0_), channel_id=1, source_target_pairs={{0,2},{2,4},{4,6},{6,8},{8,10},{10,12},{12,14},{14,0},{1,3},{3,5},... | collective-permute-start | bytes 1720328 | tf_op jit(solution)/shard_map/ppermute | solution.py:16
  30.9 12.0 %collective-permute-done.refs_1_ = bf16[320,896]{1,0:T(8,128)(2,1)S(1)} collective-permute-done((bf16[320,896]{1,0:T(8,128)(2,1)S(1)}, bf16[320,896]{1,0:T(8,128)(2,1)S(1)}, u32[]{:S(2)}, u32[]{:S(2)}) %collective-permute-start) | collective-permute-done | bytes 573472 | tf_op jit(solution)/shard_map/ppermute | solution.py:16
  42.9 4.0 %collective-permute-done.1.refs_2_ = bf16[320,896]{1,0:T(8,128)(2,1)S(1)} collective-permute-done((bf16[320,896]{1,0:T(8,128)(2,1)S(1)}, bf16[320,896]{1,0:T(8,128)(2,1)S(1)}, u32[]{:S(2)}, u32[]{:S(2)}) %collective-permute-start.1) | collective-permute-done | bytes 573472 | tf_op jit(solution)/shard_map/ppermute | solution.py:16
  47.7 1.9 %collective-permute-start.4 = (bf16[320,896]{1,0:T(8,128)(2,1)S(1)}, bf16[320,896]{1,0:T(8,128)(2,1)S(1)}, u32[]{:S(2)}, u32[]{:S(2)}) collective-permute-start(bf16[320,896]{1,0:T(8,128)(2,1)S(1)} %collective-permute-done.1.refs_2_), channel_id=1, source_target_pairs={{0,14},{2,0},{4,2},{6,4},{8,6},{10,8},{12,10},{14,12},{1,15},{3,1}... | collective-permute-start | bytes 1720328 | tf_op jit(solution)/shard_map/ppermute | solution.py:16
  52.0 10.5 %collective-permute-done.3.refs_0_ = bf16[320,896]{1,0:T(8,128)(2,1)S(1)} collective-permute-done((bf16[320,896]{1,0:T(8,128)(2,1)S(1)}, bf16[320,896]{1,0:T(8,128)(2,1)S(1)}, u32[]{:S(2)}, u32[]{:S(2)}) %collective-permute-start.3) | collective-permute-done | bytes 573472 | tf_op jit(solution)/shard_map/ppermute | solution.py:16
  64.1 1.7 collective-permute-start.7
  65.8 3.3 %broadcast_select_fusion.refs_4_.refs_3_ = bf16[4480,256]{1,0:T(8,128)(2,1)} fusion(bf16[4480,256]{1,0:T(8,128)(2,1)} %shard_map.65, bf16[4480,256]{1,0:T(8,128)(2,1)} %collective-permute-done.8, pred[]{:T(512)S(6)} %eq.76), kind=kLoop, calls=%fused_computation | loop fusion | flops 1146880 | bytes 6881281 | tf_op jit(solution)/shard_map/jit(_where)/select_n | solution.py:236
  69.1 8.6 %collective-permute-done.6.refs_2_ = bf16[320,896]{1,0:T(8,128)(2,1)S(1)} collective-permute-done((bf16[320,896]{1,0:T(8,128)(2,1)S(1)}, bf16[320,896]{1,0:T(8,128)(2,1)S(1)}, u32[]{:S(2)}, u32[]{:S(2)}) %collective-permute-start.6) | collective-permute-done | bytes 573472 | tf_op jit(solution)/shard_map/ppermute | solution.py:16
  79.5 8.0 %collective-permute-start.13 = (bf16[128,7168]{1,0:T(8,128)(2,1)S(1)}, bf16[128,7168]{1,0:T(8,128)(2,1)}, u32[]{:S(2)}, u32[]{:S(2)}) collective-permute-start(bf16[128,7168]{1,0:T(8,128)(2,1)S(1)} %broadcast_select_fusion.1.refs_6_.refs_8_.refs_10_.own_ref), channel_id=1, source_target_pairs={{0,16},{16,0},{1,17},{17,1},{2,18},{18,2},{3,19},{19,3},{4,20},{20... | collective-permute-start | bytes 5505032 | tf_op jit(solution)/shard_map/ppermute | solution.py:28
  89.0 3.1 %collective-permute-start.9 = (bf16[160,896]{1,0:T(8,128)(2,1)}, bf16[160,896]{1,0:T(8,128)(2,1)}, u32[]{:S(2)}, u32[]{:S(2)}) collective-permute-start(bf16[160,896]{1,0:T(8,128)(2,1)} %slice.21), channel_id=1, source_target_pairs={{0,2},{2,4},{4,6},{6,8},{8,10},{10,12},{12,14},{14,0},{1,3},{3,5},... | collective-permute-start | bytes 860168 | tf_op jit(solution)/shard_map/ppermute | solution.py:16
  95.4 4.0 %shard_map.67.refs_5_ = f32[320,512]{1,0:T(8,128)S(1)} custom-call(bf16[320,896]{1,0:T(8,128)(2,1)S(1)} %copy-done.4, bf16[320,896]{1,0:T(8,128)(2,1)S(1)} %copy-done.6, bf16[320,896]{1,0:T(8,128)(2,1)S(1)} %collective-permute-done.6.refs_2_, bf16[320,896]{1,0:T(8,128)(2,1)S(1)} %copy-done.2, bf16[4480,256]{1,0:T(8,128)(2,1)} %broadcast_select_fusion.refs_4_.refs_3_, ...), custom_call_target="tpu_custom_call" | custom-call | flops 1174405120 | bytes 5963776 | tf_op jit(solution)/shard_map/pallas_call | solution.py:105
  99.4 3.2 %shard_map.68 = (bf16[320,256]{1,0:T(8,128)(2,1)S(1)}, bf16[160,896]{1,0:T(8,128)(2,1)S(1)}, bf16[160,896]{1,0:T(8,128)(2,1)S(1)}, f32[160,896]{1,0:T(8,128)S(1)...) custom-call(s32[8]{0:T(128)S(1)} %stack.51.refs_0_.at_ref, ...), custom_call_target="tpu_custom_call" | custom-call | flops 734003200 | bytes 4243456 | tf_op jit(solution)/shard_map/pallas_call | solution.py:130
  102.7 3.0 %collective-permute-start.14 = (bf16[160,896]{1,0:T(8,128)(2,1)S(1)}, bf16[160,896]{1,0:T(8,128)(2,1)S(1)}, u32[]{:S(2)}, u32[]{:S(2)}) collective-permute-start(bf16[160,896]{1,0:T(8,128)(2,1)S(1)} %get-tuple-element.53), channel_id=1, source_target_pairs={{0,2},{2,4},{4,6},{6,8},{8,10},{10,12},{12,14},{14,0},{1,3},{3,5},... | collective-permute-start | bytes 860168 | tf_op jit(solution)/shard_map/ppermute | solution.py:16
  105.6 3.2 %collective-permute-start.21 = (bf16[160,896]{1,0:T(8,128)(2,1)S(1)}, bf16[160,896]{1,0:T(8,128)(2,1)S(1)}, u32[]{:S(2)}, u32[]{:S(2)}) collective-permute-start(bf16[160,896]{1,0:T(8,128)(2,1)S(1)} %get-tuple-element.60), channel_id=1, source_target_pairs={{0,2},{2,4},{4,6},{6,8},{8,10},{10,12},{12,14},{14,0},{1,3},{3,5},... | collective-permute-start | bytes 860168 | tf_op jit(solution)/shard_map/ppermute | solution.py:16
  108.9 4.8 %shard_map.69 = (f32[160,896]{1,0:T(8,128)S(1)}, f32[160,896]{1,0:T(8,128)S(1)}, f32[160,896]{1,0:T(8,128)S(1)}, f32[160,896]{1,0:T(8,128)S(1)}, f32[160,896]{1,...) custom-call(s32[8]{0:T(128)S(1)} %stack.51.refs_0_.at_ref, ...), custom_call_target="tpu_custom_call" | custom-call | flops 734003200 | bytes 8028160 | tf_op jit(solution)/shard_map/pallas_call | solution.py:163
  113.7 3.3 %collective-permute-start.15 = (bf16[160,896]{1,0:T(8,128)(2,1)S(1)}, bf16[160,896]{1,0:T(8,128)(2,1)S(1)}, u32[]{:S(2)}, u32[]{:S(2)}) collective-permute-start(bf16[160,896]{1,0:T(8,128)(2,1)S(1)} %add_convert_fusion.11), channel_id=1, source_target_pairs={{0,2},{2,4},{4,6},{6,8},{8,10},{10,12},{12,14},{14,0},{1,3},{3,5},... | collective-permute-start | bytes 860168 | tf_op jit(solution)/shard_map/ppermute | solution.py:16
  117.2 1.8 %collective-permute-done.21 = bf16[160,896]{1,0:T(8,128)(2,1)S(1)} collective-permute-done((bf16[160,896]{1,0:T(8,128)(2,1)S(1)}, bf16[160,896]{1,0:T(8,128)(2,1)S(1)}, u32[]{:S(2)}, u32[]{:S(2)}) %collective-permute-start.21) | collective-permute-done | bytes 286752 | tf_op jit(solution)/shard_map/ppermute | solution.py:16
  119.1 3.8 %collective-permute-start.22 = (bf16[160,896]{1,0:T(8,128)(2,1)S(1)}, bf16[160,896]{1,0:T(8,128)(2,1)S(1)}, u32[]{:S(2)}, u32[]{:S(2)}) collective-permute-start(bf16[160,896]{1,0:T(8,128)(2,1)S(1)} %add_convert_fusion.5), channel_id=1, source_target_pairs={{0,2},{2,4},{4,6},{6,8},{8,10},{10,12},{12,14},{14,0},{1,3},{3,5},... | collective-permute-start | bytes 860168 | tf_op jit(solution)/shard_map/ppermute | solution.py:16
  123.0 2.1 %collective-permute-done.15 = bf16[160,896]{1,0:T(8,128)(2,1)S(1)} collective-permute-done((bf16[160,896]{1,0:T(8,128)(2,1)S(1)}, bf16[160,896]{1,0:T(8,128)(2,1)S(1)}, u32[]{:S(2)}, u32[]{:S(2)}) %collective-permute-start.15) | collective-permute-done | bytes 286752 | tf_op jit(solution)/shard_map/ppermute | solution.py:16
  125.2 3.8 %collective-permute-start.16 = (bf16[160,896]{1,0:T(8,128)(2,1)S(1)}, bf16[160,896]{1,0:T(8,128)(2,1)S(1)}, u32[]{:S(2)}, u32[]{:S(2)}) collective-permute-start(bf16[160,896]{1,0:T(8,128)(2,1)S(1)} %add_convert_fusion.10), channel_id=1, source_target_pairs={{0,2},{2,4},{4,6},{6,8},{8,10},{10,12},{12,14},{14,0},{1,3},{3,5},... | collective-permute-start | bytes 860168 | tf_op jit(solution)/shard_map/ppermute | solution.py:16
  129.1 5.4 %collective-permute-done.25 = bf16[160,896]{1,0:T(8,128)(2,1)S(1)} collective-permute-done((bf16[160,896]{1,0:T(8,128)(2,1)S(1)}, bf16[160,896]{1,0:T(8,128)(2,1)S(1)}, u32[]{:S(2)}, u32[]{:S(2)}) %collective-permute-start.25) | collective-permute-done | bytes 286752 | tf_op jit(solution)/shard_map/ppermute | solution.py:16
  135.8 3.8 %collective-permute-start.17 = (bf16[160,896]{1,0:T(8,128)(2,1)S(1)}, bf16[160,896]{1,0:T(8,128)(2,1)S(1)}, u32[]{:S(2)}, u32[]{:S(2)}) collective-permute-start(bf16[160,896]{1,0:T(8,128)(2,1)S(1)} %add_convert_fusion.9), channel_id=1, source_target_pairs={{0,2},{2,4},{4,6},{6,8},{8,10},{10,12},{12,14},{14,0},{1,3},{3,5},... | collective-permute-start | bytes 860168 | tf_op jit(solution)/shard_map/ppermute | solution.py:16
  139.8 5.3 %collective-permute-done.26 = bf16[160,896]{1,0:T(8,128)(2,1)S(1)} collective-permute-done((bf16[160,896]{1,0:T(8,128)(2,1)S(1)}, bf16[160,896]{1,0:T(8,128)(2,1)S(1)}, u32[]{:S(2)}, u32[]{:S(2)}) %collective-permute-start.26) | collective-permute-done | bytes 286752 | tf_op jit(solution)/shard_map/ppermute | solution.py:16
  147.0 3.2 %collective-permute-done.23 = bf16[160,896]{1,0:T(8,128)(2,1)S(1)} collective-permute-done((bf16[160,896]{1,0:T(8,128)(2,1)S(1)}, bf16[160,896]{1,0:T(8,128)(2,1)S(1)}, u32[]{:S(2)}, u32[]{:S(2)}) %collective-permute-start.23) | collective-permute-done | bytes 286752 | tf_op jit(solution)/shard_map/ppermute | solution.py:16
  150.2 3.3 %collective-permute-done.27 = bf16[160,896]{1,0:T(8,128)(2,1)S(1)} collective-permute-done((bf16[160,896]{1,0:T(8,128)(2,1)S(1)}, bf16[160,896]{1,0:T(8,128)(2,1)S(1)}, u32[]{:S(2)}, u32[]{:S(2)}) %collective-permute-start.27) | collective-permute-done | bytes 286752 | tf_op jit(solution)/shard_map/ppermute | solution.py:16
  155.2 7.9 %all-to-all-start.1 = ((bf16[16,40,448]{2,1,0:T(8,128)(2,1)}), bf16[16,40,448]{2,1,0:T(8,128)(2,1)S(1)}, u32[]{:S(2)}, u32[]{:S(2)}) async-start(bf16[16,40,448]{2,1,0:T(8,128)(2,1)} %bitcast.19), calls=%async_computation.1 | async-start | bytes 1310720 | tf_op jit(solution)/shard_map/all_to_all | solution.py:299
  163.1 10.2 %all-to-all-done.1 = bf16[16,40,448]{2,1,0:T(8,128)(2,1)S(1)} async-done(((bf16[16,40,448]{2,1,0:T(8,128)(2,1)}), bf16[16,40,448]{2,1,0:T(8,128)(2,1)S(1)}, u32[]{:S(2)}, u32[]{:S(2)}) %all-to-all-start.1) | async-done | bytes 573472 | tf_op jit(solution)/shard_map/all_to_all | solution.py:299
  (90 shorter events, 25.8 us)
Async XLA Ops:
  3.3 19.3 %all-to-all-start = ((bf16[16,40,448]{2,1,0:T(8,128)(2,1)}), bf16[16,40,448]{2,1,0:T(8,128)(2,1)S(1)}, u32[]{:S(2)}, u32[]{:S(2)}) async-start(bf16[16,40,448]{2,1,0:T(8,128)(2,1)} %bitcast.11), calls=%async_computation | async-start | bytes 1310720 | tf_op jit(solution)/shard_map/all_to_all | solution.py:229
  21.2 9.5 %copy-start.7 = (bf16[2688,256]{1,0:T(8,128)(2,1)S(1)}, bf16[2688,256]{1,0:T(8,128)(2,1)}, u32[]{:S(2)}) copy-start(bf16[2688,256]{1,0:T(8,128)(2,1)} %shard_map.64) | copy-start | bytes 4128772
  22.7 8.1 %collective-permute-start.2 = (bf16[2688,256]{1,0:T(8,128)(2,1)}, bf16[2688,256]{1,0:T(8,128)(2,1)}, u32[]{:S(2)}, u32[]{:S(2)}) collective-permute-start(bf16[2688,256]{1,0:T(8,128)(2,1)} %shard_map.64), channel_id=1, source_target_pairs={{1,16},{16,1},{3,18},{18,3},{5,20},{20,5},{7,22},{22,7},{9,24},{24... | collective-permute-start | bytes 4128776 | tf_op jit(solution)/shard_map/ppermute | solution.py:20
  24.4 41.3 %collective-permute-start.8 = (bf16[4480,256]{1,0:T(8,128)(2,1)}, bf16[4480,256]{1,0:T(8,128)(2,1)}, u32[]{:S(2)}, u32[]{:S(2)}) collective-permute-start(bf16[4480,256]{1,0:T(8,128)(2,1)} %shard_map.65), channel_id=1, source_target_pairs={{1,16},{16,1},{3,18},{18,3},{5,20},{20,5},{7,22},{22,7},{9,24},{24... | collective-permute-start | bytes 6881288 | tf_op jit(solution)/shard_map/ppermute | solution.py:20
  27.5 22.1 %copy-start.8 = (bf16[1,128,7168]{2,1,0:T(8,128)(2,1)S(1)}, bf16[1,128,7168]{2,1,0:T(8,128)(2,1)}, u32[]{:S(2)}) copy-start(bf16[1,128,7168]{2,1,0:T(8,128)(2,1)} %param.11) | copy-start | bytes 5505028
  27.5 15.3 %collective-permute-start = (bf16[320,896]{1,0:T(8,128)(2,1)S(1)}, bf16[320,896]{1,0:T(8,128)(2,1)S(1)}, u32[]{:S(2)}, u32[]{:S(2)}) collective-permute-start(bf16[320,896]{1,0:T(8,128)(2,1)S(1)} %reshape.27.refs_0_), channel_id=1, source_target_pairs={{0,2},{2,4},{4,6},{6,8},{8,10},{10,12},{12,14},{14,0},{1,3},{3,5},... | collective-permute-start | bytes 1720328 | tf_op jit(solution)/shard_map/ppermute | solution.py:16
  30.7 16.1 %collective-permute-start.1 = (bf16[320,896]{1,0:T(8,128)(2,1)S(1)}, bf16[320,896]{1,0:T(8,128)(2,1)S(1)}, u32[]{:S(2)}, u32[]{:S(2)}) collective-permute-start(bf16[320,896]{1,0:T(8,128)(2,1)S(1)} %reshape.27.refs_0_), channel_id=1, source_target_pairs={{0,14},{2,0},{4,2},{6,4},{8,6},{10,8},{12,10},{14,12},{1,15},{3,1}... | collective-permute-start | bytes 1720328 | tf_op jit(solution)/shard_map/ppermute | solution.py:16
  46.9 3.5 %collective-permute-start.5 = (bf16[2688,256]{1,0:T(8,128)(2,1)S(1)}, bf16[2688,256]{1,0:T(8,128)(2,1)S(1)}, u32[]{:S(2)}, u32[]{:S(2)}) collective-permute-start(bf16[2688,256]{1,0:T(8,128)(2,1)S(1)} %broadcast_select_fusion.2.refs_3_), channel_id=1, source_target_pairs={{0,16},{16,0},{1,17},{17,1},{2,18},{18,2},{3,19},{19,3},{4,20},{20... | collective-permute-start | bytes 4128776 | tf_op jit(solution)/shard_map/ppermute | solution.py:28
  47.6 14.9 %collective-permute-start.3 = (bf16[320,896]{1,0:T(8,128)(2,1)S(1)}, bf16[320,896]{1,0:T(8,128)(2,1)S(1)}, u32[]{:S(2)}, u32[]{:S(2)}) collective-permute-start(bf16[320,896]{1,0:T(8,128)(2,1)S(1)} %collective-permute-done.refs_1_), channel_id=1, source_target_pairs={{0,2},{2,4},{4,6},{6,8},{8,10},{10,12},{12,14},{14,0},{1,3},{3,5},... | collective-permute-start | bytes 1720328 | tf_op jit(solution)/shard_map/ppermute | solution.py:16
  47.7 16.0 %collective-permute-start.4 = (bf16[320,896]{1,0:T(8,128)(2,1)S(1)}, bf16[320,896]{1,0:T(8,128)(2,1)S(1)}, u32[]{:S(2)}, u32[]{:S(2)}) collective-permute-start(bf16[320,896]{1,0:T(8,128)(2,1)S(1)} %collective-permute-done.1.refs_2_), channel_id=1, source_target_pairs={{0,14},{2,0},{4,2},{6,4},{8,6},{10,8},{12,10},{14,12},{1,15},{3,1}... | collective-permute-start | bytes 1720328 | tf_op jit(solution)/shard_map/ppermute | solution.py:16
  49.7 29.6 %collective-permute-start.12 = (bf16[128,7168]{1,0:T(8,128)(2,1)S(1)}, bf16[128,7168]{1,0:T(8,128)(2,1)S(1)}, u32[]{:S(2)}, u32[]{:S(2)}) collective-permute-start(bf16[128,7168]{1,0:T(8,128)(2,1)S(1)} %bitcast.36), channel_id=1, source_target_pairs={{1,16},{16,1},{3,18},{18,3},{5,20},{20,5},{7,22},{22,7},{9,24},{24... | collective-permute-start | bytes 5505032 | tf_op jit(solution)/shard_map/ppermute | solution.py:20
  63.7 13.9 %collective-permute-start.6 = (bf16[320,896]{1,0:T(8,128)(2,1)S(1)}, bf16[320,896]{1,0:T(8,128)(2,1)S(1)}, u32[]{:S(2)}, u32[]{:S(2)}) collective-permute-start(bf16[320,896]{1,0:T(8,128)(2,1)S(1)} %collective-permute-done.3.refs_0_), channel_id=1, source_target_pairs={{0,2},{2,4},{4,6},{6,8},{8,10},{10,12},{12,14},{14,0},{1,3},{3,5},... | collective-permute-start | bytes 1720328 | tf_op jit(solution)/shard_map/ppermute | solution.py:16
  64.1 15.2 %collective-permute-start.7 = (bf16[320,896]{1,0:T(8,128)(2,1)S(1)}, bf16[320,896]{1,0:T(8,128)(2,1)S(1)}, u32[]{:S(2)}, u32[]{:S(2)}) collective-permute-start(bf16[320,896]{1,0:T(8,128)(2,1)S(1)} %collective-permute-done.4.refs_1_), channel_id=1, source_target_pairs={{0,14},{2,0},{4,2},{6,4},{8,6},{10,8},{12,10},{14,12},{1,15},{3,1}... | collective-permute-start | bytes 1720328 | tf_op jit(solution)/shard_map/ppermute | solution.py:16
  79.2 13.0 %collective-permute-start.11 = (bf16[4480,256]{1,0:T(8,128)(2,1)}, bf16[4480,256]{1,0:T(8,128)(2,1)}, u32[]{:S(2)}, u32[]{:S(2)}) collective-permute-start(bf16[4480,256]{1,0:T(8,128)(2,1)} %broadcast_select_fusion.refs_4_.refs_3_), channel_id=1, source_target_pairs={{0,16},{16,0},{1,17},{17,1},{2,18},{18,2},{3,19},{19,3},{4,20},{20... | collective-permute-start | bytes 6881288 | tf_op jit(solution)/shard_map/ppermute | solution.py:28
  79.5 20.0 %collective-permute-start.13 = (bf16[128,7168]{1,0:T(8,128)(2,1)S(1)}, bf16[128,7168]{1,0:T(8,128)(2,1)}, u32[]{:S(2)}, u32[]{:S(2)}) collective-permute-start(bf16[128,7168]{1,0:T(8,128)(2,1)S(1)} %broadcast_select_fusion.1.refs_6_.refs_8_.refs_10_.own_ref), channel_id=1, source_target_pairs={{0,16},{16,0},{1,17},{17,1},{2,18},{18,2},{3,19},{19,3},{4,20},{20... | collective-permute-start | bytes 5505032 | tf_op jit(solution)/shard_map/ppermute | solution.py:28
  88.2 11.2 %collective-permute-start.10 = (bf16[160,896]{1,0:T(8,128)(2,1)}, bf16[160,896]{1,0:T(8,128)(2,1)}, u32[]{:S(2)}, u32[]{:S(2)}) collective-permute-start(bf16[160,896]{1,0:T(8,128)(2,1)} %slice.22), channel_id=1, source_target_pairs={{0,14},{2,0},{4,2},{6,4},{8,6},{10,8},{12,10},{14,12},{1,15},{3,1}... | collective-permute-start | bytes 860168 | tf_op jit(solution)/shard_map/ppermute | solution.py:16
  89.0 10.4 %collective-permute-start.9 = (bf16[160,896]{1,0:T(8,128)(2,1)}, bf16[160,896]{1,0:T(8,128)(2,1)}, u32[]{:S(2)}, u32[]{:S(2)}) collective-permute-start(bf16[160,896]{1,0:T(8,128)(2,1)} %slice.21), channel_id=1, source_target_pairs={{0,2},{2,4},{4,6},{6,8},{8,10},{10,12},{12,14},{14,0},{1,3},{3,5},... | collective-permute-start | bytes 860168 | tf_op jit(solution)/shard_map/ppermute | solution.py:16
  102.7 11.0 %collective-permute-start.14 = (bf16[160,896]{1,0:T(8,128)(2,1)S(1)}, bf16[160,896]{1,0:T(8,128)(2,1)S(1)}, u32[]{:S(2)}, u32[]{:S(2)}) collective-permute-start(bf16[160,896]{1,0:T(8,128)(2,1)S(1)} %get-tuple-element.53), channel_id=1, source_target_pairs={{0,2},{2,4},{4,6},{6,8},{8,10},{10,12},{12,14},{14,0},{1,3},{3,5},... | collective-permute-start | bytes 860168 | tf_op jit(solution)/shard_map/ppermute | solution.py:16
  105.6 11.4 %collective-permute-start.18 = (bf16[160,896]{1,0:T(8,128)(2,1)S(1)}, bf16[160,896]{1,0:T(8,128)(2,1)S(1)}, u32[]{:S(2)}, u32[]{:S(2)}) collective-permute-start(bf16[160,896]{1,0:T(8,128)(2,1)S(1)} %get-tuple-element.56), channel_id=1, source_target_pairs={{0,14},{2,0},{4,2},{6,4},{8,6},{10,8},{12,10},{14,12},{1,15},{3,1}... | collective-permute-start | bytes 860168 | tf_op jit(solution)/shard_map/ppermute | solution.py:16
  105.6 13.4 %collective-permute-start.21 = (bf16[160,896]{1,0:T(8,128)(2,1)S(1)}, bf16[160,896]{1,0:T(8,128)(2,1)S(1)}, u32[]{:S(2)}, u32[]{:S(2)}) collective-permute-start(bf16[160,896]{1,0:T(8,128)(2,1)S(1)} %get-tuple-element.60), channel_id=1, source_target_pairs={{0,2},{2,4},{4,6},{6,8},{8,10},{10,12},{12,14},{14,0},{1,3},{3,5},... | collective-permute-start | bytes 860168 | tf_op jit(solution)/shard_map/ppermute | solution.py:16
  108.9 14.0 %collective-permute-start.24 = (bf16[160,896]{1,0:T(8,128)(2,1)S(1)}, bf16[160,896]{1,0:T(8,128)(2,1)S(1)}, u32[]{:S(2)}, u32[]{:S(2)}) collective-permute-start(bf16[160,896]{1,0:T(8,128)(2,1)S(1)} %get-tuple-element.64), channel_id=1, source_target_pairs={{0,14},{2,0},{4,2},{6,4},{8,6},{10,8},{12,10},{14,12},{1,15},{3,1}... | collective-permute-start | bytes 860168 | tf_op jit(solution)/shard_map/ppermute | solution.py:16
  113.7 11.4 %collective-permute-start.15 = (bf16[160,896]{1,0:T(8,128)(2,1)S(1)}, bf16[160,896]{1,0:T(8,128)(2,1)S(1)}, u32[]{:S(2)}, u32[]{:S(2)}) collective-permute-start(bf16[160,896]{1,0:T(8,128)(2,1)S(1)} %add_convert_fusion.11), channel_id=1, source_target_pairs={{0,2},{2,4},{4,6},{6,8},{8,10},{10,12},{12,14},{14,0},{1,3},{3,5},... | collective-permute-start | bytes 860168 | tf_op jit(solution)/shard_map/ppermute | solution.py:16
  117.1 11.8 %collective-permute-start.19 = (bf16[160,896]{1,0:T(8,128)(2,1)S(1)}, bf16[160,896]{1,0:T(8,128)(2,1)S(1)}, u32[]{:S(2)}, u32[]{:S(2)}) collective-permute-start(bf16[160,896]{1,0:T(8,128)(2,1)S(1)} %add_convert_fusion.8), channel_id=1, source_target_pairs={{0,14},{2,0},{4,2},{6,4},{8,6},{10,8},{12,10},{14,12},{1,15},{3,1}... | collective-permute-start | bytes 860168 | tf_op jit(solution)/shard_map/ppermute | solution.py:16
  119.1 20.5 %collective-permute-start.22 = (bf16[160,896]{1,0:T(8,128)(2,1)S(1)}, bf16[160,896]{1,0:T(8,128)(2,1)S(1)}, u32[]{:S(2)}, u32[]{:S(2)}) collective-permute-start(bf16[160,896]{1,0:T(8,128)(2,1)S(1)} %add_convert_fusion.5), channel_id=1, source_target_pairs={{0,2},{2,4},{4,6},{6,8},{8,10},{10,12},{12,14},{14,0},{1,3},{3,5},... | collective-permute-start | bytes 860168 | tf_op jit(solution)/shard_map/ppermute | solution.py:16
  122.9 11.6 %collective-permute-start.25 = (bf16[160,896]{1,0:T(8,128)(2,1)S(1)}, bf16[160,896]{1,0:T(8,128)(2,1)S(1)}, u32[]{:S(2)}, u32[]{:S(2)}) collective-permute-start(bf16[160,896]{1,0:T(8,128)(2,1)S(1)} %add_convert_fusion.3), channel_id=1, source_target_pairs={{0,14},{2,0},{4,2},{6,4},{8,6},{10,8},{12,10},{14,12},{1,15},{3,1}... | collective-permute-start | bytes 860168 | tf_op jit(solution)/shard_map/ppermute | solution.py:16
  125.2 10.5 %collective-permute-start.16 = (bf16[160,896]{1,0:T(8,128)(2,1)S(1)}, bf16[160,896]{1,0:T(8,128)(2,1)S(1)}, u32[]{:S(2)}, u32[]{:S(2)}) collective-permute-start(bf16[160,896]{1,0:T(8,128)(2,1)S(1)} %add_convert_fusion.10), channel_id=1, source_target_pairs={{0,2},{2,4},{4,6},{6,8},{8,10},{10,12},{12,14},{14,0},{1,3},{3,5},... | collective-permute-start | bytes 860168 | tf_op jit(solution)/shard_map/ppermute | solution.py:16
  129.0 16.2 %collective-permute-start.20 = (bf16[160,896]{1,0:T(8,128)(2,1)S(1)}, bf16[160,896]{1,0:T(8,128)(2,1)S(1)}, u32[]{:S(2)}, u32[]{:S(2)}) collective-permute-start(bf16[160,896]{1,0:T(8,128)(2,1)S(1)} %add_convert_fusion.7), channel_id=1, source_target_pairs={{0,14},{2,0},{4,2},{6,4},{8,6},{10,8},{12,10},{14,12},{1,15},{3,1}... | collective-permute-start | bytes 860168 | tf_op jit(solution)/shard_map/ppermute | solution.py:16
  134.6 10.5 %collective-permute-start.26 = (bf16[160,896]{1,0:T(8,128)(2,1)S(1)}, bf16[160,896]{1,0:T(8,128)(2,1)S(1)}, u32[]{:S(2)}, u32[]{:S(2)}) collective-permute-start(bf16[160,896]{1,0:T(8,128)(2,1)S(1)} %add_convert_fusion.2), channel_id=1, source_target_pairs={{0,14},{2,0},{4,2},{6,4},{8,6},{10,8},{12,10},{14,12},{1,15},{3,1}... | collective-permute-start | bytes 860168 | tf_op jit(solution)/shard_map/ppermute | solution.py:16
  135.8 11.1 %collective-permute-start.17 = (bf16[160,896]{1,0:T(8,128)(2,1)S(1)}, bf16[160,896]{1,0:T(8,128)(2,1)S(1)}, u32[]{:S(2)}, u32[]{:S(2)}) collective-permute-start(bf16[160,896]{1,0:T(8,128)(2,1)S(1)} %add_convert_fusion.9), channel_id=1, source_target_pairs={{0,2},{2,4},{4,6},{6,8},{8,10},{10,12},{12,14},{14,0},{1,3},{3,5},... | collective-permute-start | bytes 860168 | tf_op jit(solution)/shard_map/ppermute | solution.py:16
  139.7 10.5 %collective-permute-start.23 = (bf16[160,896]{1,0:T(8,128)(2,1)S(1)}, bf16[160,896]{1,0:T(8,128)(2,1)S(1)}, u32[]{:S(2)}, u32[]{:S(2)}) collective-permute-start(bf16[160,896]{1,0:T(8,128)(2,1)S(1)} %add_convert_fusion.4), channel_id=1, source_target_pairs={{0,2},{2,4},{4,6},{6,8},{8,10},{10,12},{12,14},{14,0},{1,3},{3,5},... | collective-permute-start | bytes 860168 | tf_op jit(solution)/shard_map/ppermute | solution.py:16
  145.1 8.4 %collective-permute-start.27 = (bf16[160,896]{1,0:T(8,128)(2,1)S(1)}, bf16[160,896]{1,0:T(8,128)(2,1)S(1)}, u32[]{:S(2)}, u32[]{:S(2)}) collective-permute-start(bf16[160,896]{1,0:T(8,128)(2,1)S(1)} %add_convert_fusion.1), channel_id=1, source_target_pairs={{0,14},{2,0},{4,2},{6,4},{8,6},{10,8},{12,10},{14,12},{1,15},{3,1}... | collective-permute-start | bytes 860168 | tf_op jit(solution)/shard_map/ppermute | solution.py:16
  155.2 18.1 %all-to-all-start.1 = ((bf16[16,40,448]{2,1,0:T(8,128)(2,1)}), bf16[16,40,448]{2,1,0:T(8,128)(2,1)S(1)}, u32[]{:S(2)}, u32[]{:S(2)}) async-start(bf16[16,40,448]{2,1,0:T(8,128)(2,1)} %bitcast.19), calls=%async_computation.1 | async-start | bytes 1310720 | tf_op jit(solution)/shard_map/all_to_all | solution.py:299
  (8 other events, 34.4 us)

commit v5 on v4

--- a/solution.py
+++ b/solution.py
@@ -242,7 +242,11 @@
     late = [k for n in range(mid - 2, 0, -1) for k in (n, -n)] + [0]
     near_gu = pack_gate_up(at([-k for k in near]), w_gate[0], w_up[0], 2 * width)
     rest_gu = pack_gate_up(at([-k for k in rest]), w_gate[0], w_up[0], 2 * width)
-    arrived, near_gu, rest_gu = lax.optimization_barrier((arrived, near_gu, rest_gu))
+    part = units // 2
+    down_came = [from_swapped(w_down[0, :part])]
+    arrived, near_gu, rest_gu, down_came[0] = lax.optimization_barrier(
+        (arrived, near_gu, rest_gu, down_came[0])
+    )
     near_came = from_swapped(near_gu)
 
     rows = arrived.reshape(owners, 2, capacity, width).transpose(0, 2, 1, 3)
@@ -250,10 +254,10 @@
     half = owners * capacity // 2
     up1, down1 = along_z(rows, 1), along_z(rows, -1)
 
-    rest_came = from_swapped(rest_gu)
+    rest_came = from_swapped(after(rest_gu, rows))
     near_gu = pick(near_gu, near_came)
     up1, down1, near_gu = lax.optimization_barrier((up1, down1, near_gu))
-    down_came = from_swapped(after(w_down[0], up1))
+    down_came.append(from_swapped(after(w_down[0], up1)[part:]))
     up2, down2 = along_z(up1, 1), along_z(down1, -1)
     near_other = other_core(near_gu)
     block = {0: [(rows, 0)], 1: [(up1, 0)], -1: [(down1, 0)]}
@@ -262,7 +266,8 @@
     up2, down2, sums = lax.optimization_barrier((up2, down2, sums))
     up3, down3 = along_z(up2, 1), along_z(down2, -1)
     rest_gu = pick(rest_gu, rest_came)
-    own_down = pick(w_down[0], down_came)
+    down_came = after(down_came, up2, down2)
+    own_down = pick(w_down[0], jnp.concatenate(down_came, axis=0))
 
     up3, down3, rest_gu = lax.optimization_barrier((up3, down3, rest_gu))
     far = [along_z(up3[:half], 1), along_z(down3[half:], -1)]

time: 178 us -> 173 us (0.972)
  starting transfers between devices: 60.1 us -> 55 us
  waiting for transfers between devices: 73.3 us -> 70.7 us
  local copies, waits for them, and re-layouts: 9.02 us -> 11.3 us
    ppermute x3, starting transfers between devices: 8.72 us -> 2.96 us  [other_core(): return lax.ppermute(x, 'core', [(0, 1), (1, 0)])]
    ppermute x22, waiting for transfers between devices: 61.7 us -> 57.7 us  [along_z(): return lax.ppermute(x, 'z', [(s, (s + step) % n) for s in range(n)])]
    all_to_all x1, starting transfers between devices: 7.91 us -> 4.19 us  [on_device(): lax.all_to_all(back.reshape(experts, capacity, width), PLANE, split_axis=...]
    squeeze x0 -> x1, local copies, waits for them, and re-layouts: none -> 2.22 us  [on_device(): down_came = [from_swapped(w_down[0, :part])]]
    ppermute x22, starting transfers between devices: 31.9 us -> 33.8 us  [along_z(): return lax.ppermute(x, 'z', [(s, (s + step) % n) for s in range(n)])]
    ppermute x3 -> x4, starting transfers between devices: 4.55 us -> 6.1 us  [from_swapped(): return lax.ppermute(x, ('core', 'xh'), [(1, 2), (2, 1)])]
  transfers between devices with their start and end apart: 30 -> 31, of which waited for: 16 -> 16; matrix products, arithmetic and copies ran while one was open for 5% -> 7% of each run, Pallas kernels for 11% -> 12%
where the time goes in v5:
time: 173 us; the launch traced here: 170 us
  waiting for transfers between devices  70.7 us (41%)
  starting transfers between devices  55 us (32%)
  Pallas kernels  23.2 us (13%)
  local copies, waits for them, and re-layouts  11.3 us (7%)
  other arithmetic  6.77 us (4%)
  matrix products  2.37 us (1%)
    ppermute x22, waiting for transfers between devices, along_z(): return lax.ppermute(x, 'z', [(s, (s + step) % n) for s in range(n)])  57.7 us
    ppermute x22, starting transfers between devices, along_z(): return lax.ppermute(x, 'z', [(s, (s + step) % n) for s in range(n)])  33.8 us
    all_to_all x1, waiting for transfers between devices, on_device(): lax.all_to_all(back.reshape(experts, capacity, width), PLANE, split_axis=...  10.2 us
    pallas_call x2, Pallas kernels, pack_gate_up(): pl.pallas_call(lambda *refs: pack_gate_up_body(units, *refs), grid_spec=p...  9.67 us
    all_to_all x1, starting transfers between devices, on_device(): lax.all_to_all(leaving.reshape(experts, capacity, width), PLANE, split_ax...  7.96 us
    ppermute x4, starting transfers between devices, from_swapped(): return lax.ppermute(x, ('core', 'xh'), [(1, 2), (2, 1)])  6.1 us
    pallas_call x2, Pallas kernels, gate_up_near(): pl.pallas_call(lambda *refs: near_body(tops, counts, units, *refs), grid=...  5.56 us
    select_n x3, other arithmetic, pick(): return jnp.where(lax.axis_index('core') == lax.axis_index('xh'), mine, came)  5.24 us
  transfers between devices with their start and end apart: 31, of which 16 were waited for; matrix products, arithmetic and copies ran while one was open for 7% of the time, Pallas kernels for 12%

profile of v5, /device:TPU:96, one launch (start us, length us, event | category | flops | bytes accessed | tf_op | source)
XLA Modules:
  0.0 169.9 jit_solution(18092170664205728878)
XLA Ops:
  0.0 2.2 %slice_bitcast_fusion = bf16[64,7168]{1,0:T(8,128)(2,1)} fusion(bf16[1,128,7168]{2,1,0:T(8,128)(2,1)} %param.11), kind=kLoop, calls=%fused_computation.9 | loop fusion | bytes 1835008 | tf_op jit(solution)/shard_map/squeeze | solution.py:246
  5.7 8.0 %all-to-all-start = ((bf16[16,40,448]{2,1,0:T(8,128)(2,1)}), bf16[16,40,448]{2,1,0:T(8,128)(2,1)S(1)}, u32[]{:S(2)}, u32[]{:S(2)}) async-start(bf16[16,40,448]{2,1,0:T(8,128)(2,1)} %bitcast.11), calls=%async_computation | async-start | bytes 1310720 | tf_op jit(solution)/shard_map/all_to_all | solution.py:229
  14.4 4.1 %shard_map.64 = bf16[2688,256]{1,0:T(8,128)(2,1)} custom-call(s32[3]{0:T(128)} %pad_add_fusion.refs_0_, bf16[7168,128]{1,0:T(8,128)(2,1)} %bitcast.32, bf16[7168,128]{1,0:T(8,128)(2,1)} %bitcast.34), custom_call_target="tpu_custom_call" | custom-call | bytes 2752512 | tf_op jit(solution)/shard_map/pallas_call | solution.py:189
  19.1 5.6 %shard_map.65 = bf16[4480,256]{1,0:T(8,128)(2,1)} custom-call(s32[5]{0:T(128)} %stack.54.refs_0_, bf16[7168,128]{1,0:T(8,128)(2,1)} %bitcast.33, bf16[7168,128]{1,0:T(8,128)(2,1)} %bitcast.35), custom_call_target="tpu_custom_call" | custom-call | bytes 4587520 | tf_op jit(solution)/shard_map/pallas_call | solution.py:189
  24.7 2.8 %all-to-all-done = bf16[16,40,448]{2,1,0:T(8,128)(2,1)S(1)} async-done(((bf16[16,40,448]{2,1,0:T(8,128)(2,1)}), bf16[16,40,448]{2,1,0:T(8,128)(2,1)S(1)}, u32[]{:S(2)}, u32[]{:S(2)}) %all-to-all-start) | async-done | bytes 573472 | tf_op jit(solution)/shard_map/all_to_all | solution.py:229
  30.3 2.1 %collective-permute-start.9 = (bf16[4480,256]{1,0:T(8,128)(2,1)}, bf16[4480,256]{1,0:T(8,128)(2,1)}, u32[]{:S(2)}, u32[]{:S(2)}) collective-permute-start(bf16[4480,256]{1,0:T(8,128)(2,1)} %shard_map.65), channel_id=1, source_target_pairs={{1,16},{16,1},{3,18},{18,3},{5,20},{20,5},{7,22},{22,7},{9,24},{24... | collective-permute-start | bytes 6881288 | tf_op jit(solution)/shard_map/ppermute | solution.py:20
  32.4 3.1 %collective-permute-start.1 = (bf16[320,896]{1,0:T(8,128)(2,1)S(1)}, bf16[320,896]{1,0:T(8,128)(2,1)S(1)}, u32[]{:S(2)}, u32[]{:S(2)}) collective-permute-start(bf16[320,896]{1,0:T(8,128)(2,1)S(1)} %reshape.27.refs_0_), channel_id=1, source_target_pairs={{0,2},{2,4},{4,6},{6,8},{8,10},{10,12},{12,14},{14,0},{1,3},{3,5},... | collective-permute-start | bytes 1720328 | tf_op jit(solution)/shard_map/ppermute | solution.py:16
  35.7 10.2 %collective-permute-done.1.refs_1_ = bf16[320,896]{1,0:T(8,128)(2,1)S(1)} collective-permute-done((bf16[320,896]{1,0:T(8,128)(2,1)S(1)}, bf16[320,896]{1,0:T(8,128)(2,1)S(1)}, u32[]{:S(2)}, u32[]{:S(2)}) %collective-permute-start.1) | collective-permute-done | bytes 573472 | tf_op jit(solution)/shard_map/ppermute | solution.py:16
  45.8 4.0 %collective-permute-done.2.refs_2_ = bf16[320,896]{1,0:T(8,128)(2,1)S(1)} collective-permute-done((bf16[320,896]{1,0:T(8,128)(2,1)S(1)}, bf16[320,896]{1,0:T(8,128)(2,1)S(1)}, u32[]{:S(2)}, u32[]{:S(2)}) %collective-permute-start.2) | collective-permute-done | bytes 573472 | tf_op jit(solution)/shard_map/ppermute | solution.py:16
  49.8 2.6 %collective-permute-start.6 = (bf16[2688,256]{1,0:T(8,128)(2,1)S(1)}, bf16[2688,256]{1,0:T(8,128)(2,1)S(1)}, u32[]{:S(2)}, u32[]{:S(2)}) collective-permute-start(bf16[2688,256]{1,0:T(8,128)(2,1)S(1)} %broadcast_select_fusion.1.refs_3_), channel_id=1, source_target_pairs={{0,16},{16,0},{1,17},{17,1},{2,18},{18,2},{3,19},{19,3},{4,20},{20... | collective-permute-start | bytes 4128776 | tf_op jit(solution)/shard_map/ppermute | solution.py:28
  56.8 10.5 %collective-permute-done.4.refs_0_ = bf16[320,896]{1,0:T(8,128)(2,1)S(1)} collective-permute-done((bf16[320,896]{1,0:T(8,128)(2,1)S(1)}, bf16[320,896]{1,0:T(8,128)(2,1)S(1)}, u32[]{:S(2)}, u32[]{:S(2)}) %collective-permute-start.4) | collective-permute-done | bytes 573472 | tf_op jit(solution)/shard_map/ppermute | solution.py:16
  67.3 2.7 %collective-permute-done.5.refs_1_ = bf16[320,896]{1,0:T(8,128)(2,1)S(1)} collective-permute-done((bf16[320,896]{1,0:T(8,128)(2,1)S(1)}, bf16[320,896]{1,0:T(8,128)(2,1)S(1)}, u32[]{:S(2)}, u32[]{:S(2)}) %collective-permute-start.5) | collective-permute-done | bytes 573472 | tf_op jit(solution)/shard_map/ppermute | solution.py:16
  72.0 3.3 %broadcast_select_fusion.refs_4_.refs_3_ = bf16[4480,256]{1,0:T(8,128)(2,1)} fusion(bf16[4480,256]{1,0:T(8,128)(2,1)} %shard_map.65, bf16[4480,256]{1,0:T(8,128)(2,1)} %collective-permute-done.9, pred[]{:T(512)S(6)} %eq.76), kind=kLoop, calls=%fused_computation | loop fusion | flops 1146880 | bytes 6881281 | tf_op jit(solution)/shard_map/jit(_where)/select_n | solution.py:236
  75.3 8.5 %collective-permute-done.7.refs_2_ = bf16[320,896]{1,0:T(8,128)(2,1)S(1)} collective-permute-done((bf16[320,896]{1,0:T(8,128)(2,1)S(1)}, bf16[320,896]{1,0:T(8,128)(2,1)S(1)}, u32[]{:S(2)}, u32[]{:S(2)}) %collective-permute-start.7) | collective-permute-done | bytes 573472 | tf_op jit(solution)/shard_map/ppermute | solution.py:16
  94.3 4.0 %shard_map.67.refs_5_ = f32[320,512]{1,0:T(8,128)S(1)} custom-call(bf16[320,896]{1,0:T(8,128)(2,1)S(1)} %copy-done.4, bf16[320,896]{1,0:T(8,128)(2,1)S(1)} %copy-done.6, bf16[320,896]{1,0:T(8,128)(2,1)S(1)} %collective-permute-done.7.refs_2_, bf16[320,896]{1,0:T(8,128)(2,1)S(1)} %copy-done.2, bf16[4480,256]{1,0:T(8,128)(2,1)} %broadcast_select_fusion.refs_4_.refs_3_, ...), custom_call_target="tpu_custom_call" | custom-call | flops 1174405120 | bytes 5963776 | tf_op jit(solution)/shard_map/pallas_call | solution.py:105
  98.3 2.2 %collective-permute-done.11.refs_2_ = bf16[160,896]{1,0:T(8,128)(2,1)} collective-permute-done((bf16[160,896]{1,0:T(8,128)(2,1)}, bf16[160,896]{1,0:T(8,128)(2,1)}, u32[]{:S(2)}, u32[]{:S(2)}) %collective-permute-start.11) | collective-permute-done | bytes 286752 | tf_op jit(solution)/shard_map/ppermute | solution.py:16
  100.5 3.2 %shard_map.68 = (bf16[320,256]{1,0:T(8,128)(2,1)S(1)}, bf16[160,896]{1,0:T(8,128)(2,1)S(1)}, bf16[160,896]{1,0:T(8,128)(2,1)S(1)}, f32[160,896]{1,0:T(8,128)S(1)...) custom-call(s32[8]{0:T(128)S(1)} %stack.51.refs_0_.at_ref, ...), custom_call_target="tpu_custom_call" | custom-call | flops 734003200 | bytes 4243456 | tf_op jit(solution)/shard_map/pallas_call | solution.py:130
  103.8 3.2 %collective-permute-start.22 = (bf16[160,896]{1,0:T(8,128)(2,1)S(1)}, bf16[160,896]{1,0:T(8,128)(2,1)S(1)}, u32[]{:S(2)}, u32[]{:S(2)}) collective-permute-start(bf16[160,896]{1,0:T(8,128)(2,1)S(1)} %get-tuple-element.68), channel_id=1, source_target_pairs={{0,2},{2,4},{4,6},{6,8},{8,10},{10,12},{12,14},{14,0},{1,3},{3,5},... | collective-permute-start | bytes 860168 | tf_op jit(solution)/shard_map/ppermute | solution.py:16
  107.0 3.2 %collective-permute-start.15 = (bf16[160,896]{1,0:T(8,128)(2,1)S(1)}, bf16[160,896]{1,0:T(8,128)(2,1)S(1)}, u32[]{:S(2)}, u32[]{:S(2)}) collective-permute-start(bf16[160,896]{1,0:T(8,128)(2,1)S(1)} %get-tuple-element.61), channel_id=1, source_target_pairs={{0,2},{2,4},{4,6},{6,8},{8,10},{10,12},{12,14},{14,0},{1,3},{3,5},... | collective-permute-start | bytes 860168 | tf_op jit(solution)/shard_map/ppermute | solution.py:16
  110.3 4.8 %shard_map.69 = (f32[160,896]{1,0:T(8,128)S(1)}, f32[160,896]{1,0:T(8,128)S(1)}, f32[160,896]{1,0:T(8,128)S(1)}, f32[160,896]{1,0:T(8,128)S(1)}, f32[160,896]{1,...) custom-call(s32[8]{0:T(128)S(1)} %stack.51.refs_0_.at_ref, ...), custom_call_target="tpu_custom_call" | custom-call | flops 734003200 | bytes 8028160 | tf_op jit(solution)/shard_map/pallas_call | solution.py:163
  115.3 3.3 %collective-permute-start.23 = (bf16[160,896]{1,0:T(8,128)(2,1)S(1)}, bf16[160,896]{1,0:T(8,128)(2,1)S(1)}, u32[]{:S(2)}, u32[]{:S(2)}) collective-permute-start(bf16[160,896]{1,0:T(8,128)(2,1)S(1)} %add_convert_fusion.5), channel_id=1, source_target_pairs={{0,2},{2,4},{4,6},{6,8},{8,10},{10,12},{12,14},{14,0},{1,3},{3,5},... | collective-permute-start | bytes 860168 | tf_op jit(solution)/shard_map/ppermute | solution.py:16
  118.6 2.3 %collective-permute-done.19 = bf16[160,896]{1,0:T(8,128)(2,1)S(1)} collective-permute-done((bf16[160,896]{1,0:T(8,128)(2,1)S(1)}, bf16[160,896]{1,0:T(8,128)(2,1)S(1)}, u32[]{:S(2)}, u32[]{:S(2)}) %collective-permute-start.19) | collective-permute-done | bytes 286752 | tf_op jit(solution)/shard_map/ppermute | solution.py:16
  121.1 3.3 %collective-permute-start.16 = (bf16[160,896]{1,0:T(8,128)(2,1)S(1)}, bf16[160,896]{1,0:T(8,128)(2,1)S(1)}, u32[]{:S(2)}, u32[]{:S(2)}) collective-permute-start(bf16[160,896]{1,0:T(8,128)(2,1)S(1)} %add_convert_fusion.11), channel_id=1, source_target_pairs={{0,2},{2,4},{4,6},{6,8},{8,10},{10,12},{12,14},{14,0},{1,3},{3,5},... | collective-permute-start | bytes 860168 | tf_op jit(solution)/shard_map/ppermute | solution.py:16
  124.4 2.6 %collective-permute-done.26 = bf16[160,896]{1,0:T(8,128)(2,1)S(1)} collective-permute-done((bf16[160,896]{1,0:T(8,128)(2,1)S(1)}, bf16[160,896]{1,0:T(8,128)(2,1)S(1)}, u32[]{:S(2)}, u32[]{:S(2)}) %collective-permute-start.26) | collective-permute-done | bytes 286752 | tf_op jit(solution)/shard_map/ppermute | solution.py:16
  127.3 3.3 %collective-permute-start.24 = (bf16[160,896]{1,0:T(8,128)(2,1)S(1)}, bf16[160,896]{1,0:T(8,128)(2,1)S(1)}, u32[]{:S(2)}, u32[]{:S(2)}) collective-permute-start(bf16[160,896]{1,0:T(8,128)(2,1)S(1)} %add_convert_fusion.4), channel_id=1, source_target_pairs={{0,2},{2,4},{4,6},{6,8},{8,10},{10,12},{12,14},{14,0},{1,3},{3,5},... | collective-permute-start | bytes 860168 | tf_op jit(solution)/shard_map/ppermute | solution.py:16
  132.5 4.0 %collective-permute-start.17 = (bf16[160,896]{1,0:T(8,128)(2,1)S(1)}, bf16[160,896]{1,0:T(8,128)(2,1)S(1)}, u32[]{:S(2)}, u32[]{:S(2)}) collective-permute-start(bf16[160,896]{1,0:T(8,128)(2,1)S(1)} %add_convert_fusion.10), channel_id=1, source_target_pairs={{0,2},{2,4},{4,6},{6,8},{8,10},{10,12},{12,14},{14,0},{1,3},{3,5},... | collective-permute-start | bytes 860168 | tf_op jit(solution)/shard_map/ppermute | solution.py:16
  137.9 5.1 %collective-permute-done.17 = bf16[160,896]{1,0:T(8,128)(2,1)S(1)} collective-permute-done((bf16[160,896]{1,0:T(8,128)(2,1)S(1)}, bf16[160,896]{1,0:T(8,128)(2,1)S(1)}, u32[]{:S(2)}, u32[]{:S(2)}) %collective-permute-start.17) | collective-permute-done | bytes 286752 | tf_op jit(solution)/shard_map/ppermute | solution.py:16
  143.0 3.8 %collective-permute-start.18 = (bf16[160,896]{1,0:T(8,128)(2,1)S(1)}, bf16[160,896]{1,0:T(8,128)(2,1)S(1)}, u32[]{:S(2)}, u32[]{:S(2)}) collective-permute-start(bf16[160,896]{1,0:T(8,128)(2,1)S(1)} %add_convert_fusion.9), channel_id=1, source_target_pairs={{0,2},{2,4},{4,6},{6,8},{8,10},{10,12},{12,14},{14,0},{1,3},{3,5},... | collective-permute-start | bytes 860168 | tf_op jit(solution)/shard_map/ppermute | solution.py:16
  146.8 1.9 %collective-permute-done.28 = bf16[160,896]{1,0:T(8,128)(2,1)S(1)} collective-permute-done((bf16[160,896]{1,0:T(8,128)(2,1)S(1)}, bf16[160,896]{1,0:T(8,128)(2,1)S(1)}, u32[]{:S(2)}, u32[]{:S(2)}) %collective-permute-start.28) | collective-permute-done | bytes 286752 | tf_op jit(solution)/shard_map/ppermute | solution.py:16
  148.8 3.3 %collective-permute-done.21 = bf16[160,896]{1,0:T(8,128)(2,1)S(1)} collective-permute-done((bf16[160,896]{1,0:T(8,128)(2,1)S(1)}, bf16[160,896]{1,0:T(8,128)(2,1)S(1)}, u32[]{:S(2)}, u32[]{:S(2)}) %collective-permute-start.21) | collective-permute-done | bytes 286752 | tf_op jit(solution)/shard_map/ppermute | solution.py:16
  153.8 4.2 %all-to-all-start.1 = ((bf16[16,40,448]{2,1,0:T(8,128)(2,1)}), bf16[16,40,448]{2,1,0:T(8,128)(2,1)S(1)}, u32[]{:S(2)}, u32[]{:S(2)}) async-start(bf16[16,40,448]{2,1,0:T(8,128)(2,1)} %bitcast.20), calls=%async_computation.1 | async-start | bytes 1310720 | tf_op jit(solution)/shard_map/all_to_all | solution.py:304
  158.0 10.2 %all-to-all-done.1 = bf16[16,40,448]{2,1,0:T(8,128)(2,1)S(1)} async-done(((bf16[16,40,448]{2,1,0:T(8,128)(2,1)}), bf16[16,40,448]{2,1,0:T(8,128)(2,1)S(1)}, u32[]{:S(2)}, u32[]{:S(2)}) %all-to-all-start.1) | async-done | bytes 573472 | tf_op jit(solution)/shard_map/all_to_all | solution.py:304
  (96 shorter events, 32.1 us)
Async XLA Ops:
  2.2 25.3 %collective-permute-start = (bf16[64,7168]{1,0:T(8,128)(2,1)}, bf16[64,7168]{1,0:T(8,128)(2,1)}, u32[]{:S(2)}, u32[]{:S(2)}) collective-permute-start(bf16[64,7168]{1,0:T(8,128)(2,1)} %slice_bitcast_fusion), channel_id=1, source_target_pairs={{1,16},{16,1},{3,18},{18,3},{5,20},{20,5},{7,22},{22,7},{9,24},{24... | collective-permute-start | bytes 2752520 | tf_op jit(solution)/shard_map/ppermute | solution.py:20
  5.7 21.8 %all-to-all-start = ((bf16[16,40,448]{2,1,0:T(8,128)(2,1)}), bf16[16,40,448]{2,1,0:T(8,128)(2,1)S(1)}, u32[]{:S(2)}, u32[]{:S(2)}) async-start(bf16[16,40,448]{2,1,0:T(8,128)(2,1)} %bitcast.11), calls=%async_computation | async-start | bytes 1310720 | tf_op jit(solution)/shard_map/all_to_all | solution.py:229
  27.5 8.0 %collective-permute-start.3 = (bf16[2688,256]{1,0:T(8,128)(2,1)S(1)}, bf16[2688,256]{1,0:T(8,128)(2,1)}, u32[]{:S(2)}, u32[]{:S(2)}) collective-permute-start(bf16[2688,256]{1,0:T(8,128)(2,1)S(1)} %copy-done.8), channel_id=1, source_target_pairs={{1,16},{16,1},{3,18},{18,3},{5,20},{20,5},{7,22},{22,7},{9,24},{24... | collective-permute-start | bytes 4128776 | tf_op jit(solution)/shard_map/ppermute | solution.py:20
  30.3 41.7 %collective-permute-start.9 = (bf16[4480,256]{1,0:T(8,128)(2,1)}, bf16[4480,256]{1,0:T(8,128)(2,1)}, u32[]{:S(2)}, u32[]{:S(2)}) collective-permute-start(bf16[4480,256]{1,0:T(8,128)(2,1)} %shard_map.65), channel_id=1, source_target_pairs={{1,16},{16,1},{3,18},{18,3},{5,20},{20,5},{7,22},{22,7},{9,24},{24... | collective-permute-start | bytes 6881288 | tf_op jit(solution)/shard_map/ppermute | solution.py:20
  32.4 22.0 %copy-start.7 = (bf16[1,128,7168]{2,1,0:T(8,128)(2,1)S(1)}, bf16[1,128,7168]{2,1,0:T(8,128)(2,1)}, u32[]{:S(2)}) copy-start(bf16[1,128,7168]{2,1,0:T(8,128)(2,1)} %param.11) | copy-start | bytes 5505028
  32.4 13.5 %collective-permute-start.1 = (bf16[320,896]{1,0:T(8,128)(2,1)S(1)}, bf16[320,896]{1,0:T(8,128)(2,1)S(1)}, u32[]{:S(2)}, u32[]{:S(2)}) collective-permute-start(bf16[320,896]{1,0:T(8,128)(2,1)S(1)} %reshape.27.refs_0_), channel_id=1, source_target_pairs={{0,2},{2,4},{4,6},{6,8},{8,10},{10,12},{12,14},{14,0},{1,3},{3,5},... | collective-permute-start | bytes 1720328 | tf_op jit(solution)/shard_map/ppermute | solution.py:16
  35.5 14.3 %collective-permute-start.2 = (bf16[320,896]{1,0:T(8,128)(2,1)S(1)}, bf16[320,896]{1,0:T(8,128)(2,1)S(1)}, u32[]{:S(2)}, u32[]{:S(2)}) collective-permute-start(bf16[320,896]{1,0:T(8,128)(2,1)S(1)} %reshape.27.refs_0_), channel_id=1, source_target_pairs={{0,14},{2,0},{4,2},{6,4},{8,6},{10,8},{12,10},{14,12},{1,15},{3,1}... | collective-permute-start | bytes 1720328 | tf_op jit(solution)/shard_map/ppermute | solution.py:16
  49.8 5.4 %collective-permute-start.6 = (bf16[2688,256]{1,0:T(8,128)(2,1)S(1)}, bf16[2688,256]{1,0:T(8,128)(2,1)S(1)}, u32[]{:S(2)}, u32[]{:S(2)}) collective-permute-start(bf16[2688,256]{1,0:T(8,128)(2,1)S(1)} %broadcast_select_fusion.1.refs_3_), channel_id=1, source_target_pairs={{0,16},{16,0},{1,17},{17,1},{2,18},{18,2},{3,19},{19,3},{4,20},{20... | collective-permute-start | bytes 4128776 | tf_op jit(solution)/shard_map/ppermute | solution.py:28
  52.4 14.9 %collective-permute-start.4 = (bf16[320,896]{1,0:T(8,128)(2,1)S(1)}, bf16[320,896]{1,0:T(8,128)(2,1)S(1)}, u32[]{:S(2)}, u32[]{:S(2)}) collective-permute-start(bf16[320,896]{1,0:T(8,128)(2,1)S(1)} %collective-permute-done.1.refs_1_), channel_id=1, source_target_pairs={{0,2},{2,4},{4,6},{6,8},{8,10},{10,12},{12,14},{14,0},{1,3},{3,5},... | collective-permute-start | bytes 1720328 | tf_op jit(solution)/shard_map/ppermute | solution.py:16
  54.0 15.9 %collective-permute-start.5 = (bf16[320,896]{1,0:T(8,128)(2,1)S(1)}, bf16[320,896]{1,0:T(8,128)(2,1)S(1)}, u32[]{:S(2)}, u32[]{:S(2)}) collective-permute-start(bf16[320,896]{1,0:T(8,128)(2,1)S(1)} %collective-permute-done.2.refs_2_), channel_id=1, source_target_pairs={{0,14},{2,0},{4,2},{6,4},{8,6},{10,8},{12,10},{14,12},{1,15},{3,1}... | collective-permute-start | bytes 1720328 | tf_op jit(solution)/shard_map/ppermute | solution.py:16
  54.5 20.8 %collective-permute-start.13 = (bf16[64,7168]{1,0:T(8,128)(2,1)S(1)}, bf16[64,7168]{1,0:T(8,128)(2,1)S(1)}, u32[]{:S(2)}, u32[]{:S(2)}) collective-permute-start(bf16[64,7168]{1,0:T(8,128)(2,1)S(1)} %slice.30), channel_id=1, source_target_pairs={{1,16},{16,1},{3,18},{18,3},{5,20},{20,5},{7,22},{22,7},{9,24},{24... | collective-permute-start | bytes 2752520 | tf_op jit(solution)/shard_map/ppermute | solution.py:20
  69.9 13.8 %collective-permute-start.7 = (bf16[320,896]{1,0:T(8,128)(2,1)S(1)}, bf16[320,896]{1,0:T(8,128)(2,1)S(1)}, u32[]{:S(2)}, u32[]{:S(2)}) collective-permute-start(bf16[320,896]{1,0:T(8,128)(2,1)S(1)} %collective-permute-done.4.refs_0_), channel_id=1, source_target_pairs={{0,2},{2,4},{4,6},{6,8},{8,10},{10,12},{12,14},{14,0},{1,3},{3,5},... | collective-permute-start | bytes 1720328 | tf_op jit(solution)/shard_map/ppermute | solution.py:16
  70.3 15.1 %collective-permute-start.8 = (bf16[320,896]{1,0:T(8,128)(2,1)S(1)}, bf16[320,896]{1,0:T(8,128)(2,1)S(1)}, u32[]{:S(2)}, u32[]{:S(2)}) collective-permute-start(bf16[320,896]{1,0:T(8,128)(2,1)S(1)} %collective-permute-done.5.refs_1_), channel_id=1, source_target_pairs={{0,14},{2,0},{4,2},{6,4},{8,6},{10,8},{12,10},{14,12},{1,15},{3,1}... | collective-permute-start | bytes 1720328 | tf_op jit(solution)/shard_map/ppermute | solution.py:16
  85.4 5.8 %collective-permute-start.12 = (bf16[4480,256]{1,0:T(8,128)(2,1)}, bf16[4480,256]{1,0:T(8,128)(2,1)}, u32[]{:S(2)}, u32[]{:S(2)}) collective-permute-start(bf16[4480,256]{1,0:T(8,128)(2,1)} %broadcast_select_fusion.refs_4_.refs_3_), channel_id=1, source_target_pairs={{0,16},{16,0},{1,17},{17,1},{2,18},{18,2},{3,19},{19,3},{4,20},{20... | collective-permute-start | bytes 6881288 | tf_op jit(solution)/shard_map/ppermute | solution.py:28
  87.2 13.3 %collective-permute-start.14 = (bf16[128,7168]{1,0:T(8,128)(2,1)S(1)}, bf16[128,7168]{1,0:T(8,128)(2,1)}, u32[]{:S(2)}, u32[]{:S(2)}) collective-permute-start(bf16[128,7168]{1,0:T(8,128)(2,1)S(1)} %maximum_select_fusion.refs_6_.refs_8_.refs_10_.own_ref), channel_id=1, source_target_pairs={{0,16},{16,0},{1,17},{17,1},{2,18},{18,2},{3,19},{19,3},{4,20},{20... | collective-permute-start | bytes 5505032 | tf_op jit(solution)/shard_map/ppermute | solution.py:28
  88.3 10.0 %collective-permute-start.10 = (bf16[160,896]{1,0:T(8,128)(2,1)}, bf16[160,896]{1,0:T(8,128)(2,1)}, u32[]{:S(2)}, u32[]{:S(2)}) collective-permute-start(bf16[160,896]{1,0:T(8,128)(2,1)} %slice.28), channel_id=1, source_target_pairs={{0,2},{2,4},{4,6},{6,8},{8,10},{10,12},{12,14},{14,0},{1,3},{3,5},... | collective-permute-start | bytes 860168 | tf_op jit(solution)/shard_map/ppermute | solution.py:16
  90.1 10.3 %collective-permute-start.11 = (bf16[160,896]{1,0:T(8,128)(2,1)}, bf16[160,896]{1,0:T(8,128)(2,1)}, u32[]{:S(2)}, u32[]{:S(2)}) collective-permute-start(bf16[160,896]{1,0:T(8,128)(2,1)} %slice.29), channel_id=1, source_target_pairs={{0,14},{2,0},{4,2},{6,4},{8,6},{10,8},{12,10},{14,12},{1,15},{3,1}... | collective-permute-start | bytes 860168 | tf_op jit(solution)/shard_map/ppermute | solution.py:16
  103.7 11.3 %collective-permute-start.25 = (bf16[160,896]{1,0:T(8,128)(2,1)S(1)}, bf16[160,896]{1,0:T(8,128)(2,1)S(1)}, u32[]{:S(2)}, u32[]{:S(2)}) collective-permute-start(bf16[160,896]{1,0:T(8,128)(2,1)S(1)} %get-tuple-element.72), channel_id=1, source_target_pairs={{0,14},{2,0},{4,2},{6,4},{8,6},{10,8},{12,10},{14,12},{1,15},{3,1}... | collective-permute-start | bytes 860168 | tf_op jit(solution)/shard_map/ppermute | solution.py:16
  103.8 11.4 %collective-permute-start.22 = (bf16[160,896]{1,0:T(8,128)(2,1)S(1)}, bf16[160,896]{1,0:T(8,128)(2,1)S(1)}, u32[]{:S(2)}, u32[]{:S(2)}) collective-permute-start(bf16[160,896]{1,0:T(8,128)(2,1)S(1)} %get-tuple-element.68), channel_id=1, source_target_pairs={{0,2},{2,4},{4,6},{6,8},{8,10},{10,12},{12,14},{14,0},{1,3},{3,5},... | collective-permute-start | bytes 860168 | tf_op jit(solution)/shard_map/ppermute | solution.py:16
  107.0 13.9 %collective-permute-start.19 = (bf16[160,896]{1,0:T(8,128)(2,1)S(1)}, bf16[160,896]{1,0:T(8,128)(2,1)S(1)}, u32[]{:S(2)}, u32[]{:S(2)}) collective-permute-start(bf16[160,896]{1,0:T(8,128)(2,1)S(1)} %get-tuple-element.64), channel_id=1, source_target_pairs={{0,14},{2,0},{4,2},{6,4},{8,6},{10,8},{12,10},{14,12},{1,15},{3,1}... | collective-permute-start | bytes 860168 | tf_op jit(solution)/shard_map/ppermute | solution.py:16
  107.0 14.0 %collective-permute-start.15 = (bf16[160,896]{1,0:T(8,128)(2,1)S(1)}, bf16[160,896]{1,0:T(8,128)(2,1)S(1)}, u32[]{:S(2)}, u32[]{:S(2)}) collective-permute-start(bf16[160,896]{1,0:T(8,128)(2,1)S(1)} %get-tuple-element.61), channel_id=1, source_target_pairs={{0,2},{2,4},{4,6},{6,8},{8,10},{10,12},{12,14},{14,0},{1,3},{3,5},... | collective-permute-start | bytes 860168 | tf_op jit(solution)/shard_map/ppermute | solution.py:16
  115.1 11.9 %collective-permute-start.26 = (bf16[160,896]{1,0:T(8,128)(2,1)S(1)}, bf16[160,896]{1,0:T(8,128)(2,1)S(1)}, u32[]{:S(2)}, u32[]{:S(2)}) collective-permute-start(bf16[160,896]{1,0:T(8,128)(2,1)S(1)} %add_convert_fusion.3), channel_id=1, source_target_pairs={{0,14},{2,0},{4,2},{6,4},{8,6},{10,8},{12,10},{14,12},{1,15},{3,1}... | collective-permute-start | bytes 860168 | tf_op jit(solution)/shard_map/ppermute | solution.py:16
  115.3 11.9 %collective-permute-start.23 = (bf16[160,896]{1,0:T(8,128)(2,1)S(1)}, bf16[160,896]{1,0:T(8,128)(2,1)S(1)}, u32[]{:S(2)}, u32[]{:S(2)}) collective-permute-start(bf16[160,896]{1,0:T(8,128)(2,1)S(1)} %add_convert_fusion.5), channel_id=1, source_target_pairs={{0,2},{2,4},{4,6},{6,8},{8,10},{10,12},{12,14},{14,0},{1,3},{3,5},... | collective-permute-start | bytes 860168 | tf_op jit(solution)/shard_map/ppermute | solution.py:16
  121.0 16.8 %collective-permute-start.20 = (bf16[160,896]{1,0:T(8,128)(2,1)S(1)}, bf16[160,896]{1,0:T(8,128)(2,1)S(1)}, u32[]{:S(2)}, u32[]{:S(2)}) collective-permute-start(bf16[160,896]{1,0:T(8,128)(2,1)S(1)} %add_convert_fusion.8), channel_id=1, source_target_pairs={{0,14},{2,0},{4,2},{6,4},{8,6},{10,8},{12,10},{14,12},{1,15},{3,1}... | collective-permute-start | bytes 860168 | tf_op jit(solution)/shard_map/ppermute | solution.py:16
  121.1 11.3 %collective-permute-start.16 = (bf16[160,896]{1,0:T(8,128)(2,1)S(1)}, bf16[160,896]{1,0:T(8,128)(2,1)S(1)}, u32[]{:S(2)}, u32[]{:S(2)}) collective-permute-start(bf16[160,896]{1,0:T(8,128)(2,1)S(1)} %add_convert_fusion.11), channel_id=1, source_target_pairs={{0,2},{2,4},{4,6},{6,8},{8,10},{10,12},{12,14},{14,0},{1,3},{3,5},... | collective-permute-start | bytes 860168 | tf_op jit(solution)/shard_map/ppermute | solution.py:16
  127.1 10.4 %collective-permute-start.27 = (bf16[160,896]{1,0:T(8,128)(2,1)S(1)}, bf16[160,896]{1,0:T(8,128)(2,1)S(1)}, u32[]{:S(2)}, u32[]{:S(2)}) collective-permute-start(bf16[160,896]{1,0:T(8,128)(2,1)S(1)} %add_convert_fusion.2), channel_id=1, source_target_pairs={{0,14},{2,0},{4,2},{6,4},{8,6},{10,8},{12,10},{14,12},{1,15},{3,1}... | collective-permute-start | bytes 860168 | tf_op jit(solution)/shard_map/ppermute | solution.py:16
  127.3 19.5 %collective-permute-start.24 = (bf16[160,896]{1,0:T(8,128)(2,1)S(1)}, bf16[160,896]{1,0:T(8,128)(2,1)S(1)}, u32[]{:S(2)}, u32[]{:S(2)}) collective-permute-start(bf16[160,896]{1,0:T(8,128)(2,1)S(1)} %add_convert_fusion.4), channel_id=1, source_target_pairs={{0,2},{2,4},{4,6},{6,8},{8,10},{10,12},{12,14},{14,0},{1,3},{3,5},... | collective-permute-start | bytes 860168 | tf_op jit(solution)/shard_map/ppermute | solution.py:16
  132.5 10.5 %collective-permute-start.17 = (bf16[160,896]{1,0:T(8,128)(2,1)S(1)}, bf16[160,896]{1,0:T(8,128)(2,1)S(1)}, u32[]{:S(2)}, u32[]{:S(2)}) collective-permute-start(bf16[160,896]{1,0:T(8,128)(2,1)S(1)} %add_convert_fusion.10), channel_id=1, source_target_pairs={{0,2},{2,4},{4,6},{6,8},{8,10},{10,12},{12,14},{14,0},{1,3},{3,5},... | collective-permute-start | bytes 860168 | tf_op jit(solution)/shard_map/ppermute | solution.py:16
  137.6 11.1 %collective-permute-start.28 = (bf16[160,896]{1,0:T(8,128)(2,1)S(1)}, bf16[160,896]{1,0:T(8,128)(2,1)S(1)}, u32[]{:S(2)}, u32[]{:S(2)}) collective-permute-start(bf16[160,896]{1,0:T(8,128)(2,1)S(1)} %add_convert_fusion.1), channel_id=1, source_target_pairs={{0,14},{2,0},{4,2},{6,4},{8,6},{10,8},{12,10},{14,12},{1,15},{3,1}... | collective-permute-start | bytes 860168 | tf_op jit(solution)/shard_map/ppermute | solution.py:16
  137.8 14.3 %collective-permute-start.21 = (bf16[160,896]{1,0:T(8,128)(2,1)S(1)}, bf16[160,896]{1,0:T(8,128)(2,1)S(1)}, u32[]{:S(2)}, u32[]{:S(2)}) collective-permute-start(bf16[160,896]{1,0:T(8,128)(2,1)S(1)} %add_convert_fusion.7), channel_id=1, source_target_pairs={{0,14},{2,0},{4,2},{6,4},{8,6},{10,8},{12,10},{14,12},{1,15},{3,1}... | collective-permute-start | bytes 860168 | tf_op jit(solution)/shard_map/ppermute | solution.py:16
  143.0 9.1 %collective-permute-start.18 = (bf16[160,896]{1,0:T(8,128)(2,1)S(1)}, bf16[160,896]{1,0:T(8,128)(2,1)S(1)}, u32[]{:S(2)}, u32[]{:S(2)}) collective-permute-start(bf16[160,896]{1,0:T(8,128)(2,1)S(1)} %add_convert_fusion.9), channel_id=1, source_target_pairs={{0,2},{2,4},{4,6},{6,8},{8,10},{10,12},{12,14},{14,0},{1,3},{3,5},... | collective-permute-start | bytes 860168 | tf_op jit(solution)/shard_map/ppermute | solution.py:16
  153.8 14.4 %all-to-all-start.1 = ((bf16[16,40,448]{2,1,0:T(8,128)(2,1)}), bf16[16,40,448]{2,1,0:T(8,128)(2,1)S(1)}, u32[]{:S(2)}, u32[]{:S(2)}) async-start(bf16[16,40,448]{2,1,0:T(8,128)(2,1)} %bitcast.20), calls=%async_computation.1 | async-start | bytes 1310720 | tf_op jit(solution)/shard_map/all_to_all | solution.py:304
  (10 other events, 42.5 us)
